TPU v7x, 32 devices: a whole 2x2x4 slice. The times are simulated.
32 devices in a mesh: groups: 2 (over x), row: 16 (over z, y, core).
Axes of the slice: x: 2, y: 2, z: 4, core: 2. Of those that a mesh axis runs over, the one named last changes fastest.
Arguments:
- inputs: bfloat16 [1024, 8192], P(('groups', 'row')), parts along dimension 0, may hold values from -6 to 6
- input_factor: bfloat16 [16384, 8192], P(('groups', 'row')), parts along dimension 0, as said below
- out_grads: bfloat16 [1024, 16384], P(('groups', 'row')), parts along dimension 0, may hold values from -6 to 6
- output_factor: float32 [32768, 4096], P(('groups', 'row')), parts along dimension 0, may hold values from -6 to 6
Outputs:
- updated_factor: float32 [32768, 4096], P(('groups', 'row')), parts along dimension 0
There are 2 independent parts, one for each index of `groups`. A program takes and returns all parts, laid end to end along the dimension named above; each array names one. Nothing has to cross between parts.
Inputs may be any that keep to these rules, and one draw needn't show every extreme that they name: input_factor is symmetric.
All inputs are finite; a program needn't handle non-finite values.
Results may differ from a plain program's by a relative error of at most 0.0041.
Values may be sent and summed in bfloat16 or wider, within the bound.
No kernel may reach another device: no remote copies, remote signals or barrier semaphores. Data moves between devices by JAX's collectives and lax.ppermute only.
A program may use at most 192 MiB of HBM per device.

v0:
```python
import jax
import jax.numpy as jnp
from jax import lax
from jax.sharding import PartitionSpec as P


def per_device(inputs, input_factor, out_grads, output_factor):
    grad_cols = lax.all_to_all(out_grads, "row", split_axis=1, concat_axis=0, tiled=True)
    whole = lax.all_gather(inputs, "row", axis=0, tiled=True)
    proj_half = lax.dot_general(
        input_factor, whole, (((1,), (1,)), ((), ())), preferred_element_type=jnp.float32
    ).astype(jnp.bfloat16)
    feature_width = input_factor.shape[0]
    own_cols = lax.dynamic_slice_in_dim(
        whole, lax.axis_index("row") * feature_width, feature_width, 1
    )
    partial_value = lax.dot_general(
        proj_half, own_cols, (((0,), (1,)), ((), ())), preferred_element_type=jnp.float32
    )
    factor = float(input_factor.shape[1]) ** (-0.5)
    gram = (lax.psum(partial_value, "row") * factor).astype(jnp.bfloat16)
    left = lax.dot_general(
        grad_cols, gram, (((0,), (0,)), ((), ())), preferred_element_type=jnp.float32
    ).astype(jnp.bfloat16)
    slab_width = output_factor.shape[1]
    slab_all = lax.all_gather(out_grads[:, :slab_width], "row", axis=0, tiled=True)
    update = jnp.dot(left, slab_all, preferred_element_type=jnp.float32)
    return output_factor + update * (1.0 / gram.shape[0])


def solution(mesh):
    in_specs = (
        P(("groups", "row"), None),
        P(("groups", "row"), None),
        P(("groups", "row"), None),
        P(("groups", "row"), None),
    )
    out_specs = P(("groups", "row"), None)
    return jax.shard_map(
        per_device, mesh=mesh, in_specs=in_specs, out_specs=out_specs, check_vma=False
    )
```

profile of v0, /device:TPU:0, one launch (start us, length us, event | category | flops | bytes accessed | tf_op | source)
XLA Modules:
  0.0 273.1 jit_solution(11603541428070253687)
XLA Ops:
  6.5 0.0 all-gather.3.cloned.1.call-start
  6.5 0.7 all-gather.3.cloned.1.call-update
  7.3 0.0 all-gather.5.cloned.1.call-start
  7.3 1.7 slice.3
  9.0 0.0 all-gather.5.cloned.1.call-update
  9.0 2.3 copy.9
  11.3 7.4 %all-to-all-start = ((bf16[32,16,1024]{2,0,1:T(8,128)(2,1)}), bf16[32,16,1024]{2,0,1:T(8,128)(2,1)S(1)}, u32[]{:S(2)}, u32[]{:S(2)}) async-start(bf16[32,16,1024]{2,0,1:T(8,128)(2,1)} %bitcast.10), calls=%async_computation | async-start | bytes 2097152 | tf_op jit(solution)/shard_map/all_to_all | solution.py:8
  18.7 0.0 all-reduce.2.cloned.1.call-start
  18.7 87.8 %all-gather.3.cloned.1.call-done = bf16[512,8192]{1,0:T(8,128)(2,1)} async-done(((bf16[32,8192]{1,0:T(8,128)(2,1)}), bf16[512,8192]{1,0:T(8,128)(2,1)}) %all-gather.3.cloned.1.call-update) | async-done | bytes 8388624 | tf_op jit(solution)/shard_map/all_gather | solution.py:9
  106.6 11.8 %fusion = f32[512,512]{1,0:T(8,128)} fusion(bf16[512,8192]{1,0:T(8,128)(2,1)} %param.5, bf16[512,8192]{1,0:T(8,128)(2,1)} %all-gather.3.cloned.1.call-done, s32[]{:T(128)S(6)} %select_n.3), kind=kOutput, calls=%fused_computation.3 | convolution fusion | flops 4563664896 | bytes 18350084 | tf_op jit(solution)/shard_map/dot_general | solution.py:17
  118.3 0.0 all-reduce.2.cloned.1.call-update
  118.4 0.0 all-to-all-done
  118.4 39.2 %all-gather.5.cloned.1.call-done = bf16[512,4096]{1,0:T(8,128)(2,1)} async-done(((bf16[32,4096]{1,0:T(8,128)(2,1)}), bf16[512,4096]{1,0:T(8,128)(2,1)}) %all-gather.5.cloned.1.call-update) | async-done | bytes 4194320 | tf_op jit(solution)/shard_map/all_gather | solution.py:26
  157.6 95.3 %all-reduce.2.cloned.1.call-done = f32[512,512]{1,0:T(8,128)} async-done(((f32[512,512]{1,0:T(8,128)}), f32[512,512]{1,0:T(8,128)}) %all-reduce.2.cloned.1.call-update) | async-done | bytes 1048592 | tf_op jit(solution)/shard_map/psum | solution.py:21
  252.9 13.6 %multiply_add_fusion = f32[1024,4096]{1,0:T(8,128)} fusion(f32[1024,4096]{1,0:T(8,128)} %param.7, bf16[512,4096]{1,0:T(8,128)(2,1)} %all-gather.5.cloned.1.call-done, bf16[512,1024]{1,0:T(8,128)(2,1)S(1)} %bitcast.11, f32[512,512]{1,0:T(8,128)} %all-reduce.2.cloned.1.call-done), kind=kOutput, calls=%fused_computation | convolution fusion | flops 4841275392 | bytes 39845888 | tf_op jit(solution)/shard_map/dot_general | solution.py:27
Async XLA Ops:
  6.5 100.0 %all-gather.3.cloned.1.call-start = ((), (), s32[]{:S(2)}) async-start(), calls=%async_computation.1 | async-start | bytes 8912896 | tf_op jit(solution)/shard_map/all_gather | solution.py:9
  7.3 150.3 %all-gather.5.cloned.1.call-start = ((), (), s32[]{:S(2)}) async-start(), calls=%async_computation.3 | async-start | bytes 4456448 | tf_op jit(solution)/shard_map/all_gather | solution.py:26
  11.3 107.1 %all-to-all-start = ((bf16[32,16,1024]{2,0,1:T(8,128)(2,1)}), bf16[32,16,1024]{2,0,1:T(8,128)(2,1)S(1)}, u32[]{:S(2)}, u32[]{:S(2)}) async-start(bf16[32,16,1024]{2,0,1:T(8,128)(2,1)} %bitcast.10), calls=%async_computation | async-start | bytes 2097152 | tf_op jit(solution)/shard_map/all_to_all | solution.py:8
  18.7 234.2 %all-reduce.2.cloned.1.call-start = ((), (), s32[]{:S(2)}) async-start(), calls=%async_computation.2 | async-start | bytes 2097152 | tf_op jit(solution)/shard_map/psum | solution.py:21
Sparse Core Ops, SparseCore 0:
  9.5 97.0 all-gather.2
  108.7 48.7 all-gather.4
  161.1 91.8 all-reduce.1
where the time goes:
time: 273 us
  waiting for transfers between devices  223 us (82%)
  matrix products  25.4 us (9%)
  between operations  13.1 us (5%)
  starting transfers between devices  7.47 us (3%)
  local copies, waits for them, and re-layouts  3.96 us (1%)
    psum x1, waiting for transfers between devices, per_device(): gram = (lax.psum(partial_value, 'row') * factor).astype(jnp.bfloat16)  95.3 us
    all_gather x1, waiting for transfers between devices, per_device(): whole = lax.all_gather(inputs, 'row', axis=0, tiled=True)  87.8 us
    all_gather x1, waiting for transfers between devices, per_device(): lax.all_gather(out_grads[:, :slab_width], 'row', axis=0, tiled=True)  39.2 us
    dot_general x1, matrix products, per_device(): update = jnp.dot(left, slab_all, preferred_element_type=jnp.float32)  13.6 us
    dot_general x1, matrix products, per_device(): lax.dot_general(proj_half, own_cols, (((0,), (1,)), ((), ())), preferred_...  11.8 us
    all_to_all x1, starting transfers between devices, per_device(): lax.all_to_all(out_grads, 'row', split_axis=1, concat_axis=0, tiled=True)  7.39 us
  transfers between devices with their start and end apart: 4, of which 3 were waited for; matrix products, arithmetic and copies ran while one was open for 6% of the time, Pallas kernels for 0%

commit v1 on v0

v1 whole, which is shorter than its diff:
```python
import functools

import jax
import jax.numpy as jnp
from jax import lax
from jax.experimental import pallas as pl
from jax.experimental.pallas import tpu as pltpu
from jax.sharding import PartitionSpec as P

BF16 = jnp.bfloat16
F32 = jnp.float32
VMEM_LIMIT = 56 * 1024 * 1024


def permute(value, perm):
    return lax.ppermute(value, "row", perm)


def core_perm(n):
    return [(i, i ^ 1) for i in range(n)]


def y_perm(n):
    return [(i, i ^ 2) for i in range(n)]


def plane_perm(n, step):
    return [(i, (i + 4 * step) % n) for i in range(n)]


def takes_extra(plane, planes):
    return (plane % 2 == 0) == (plane < planes // 2)


def spread(value):
    n = lax.axis_size("row")
    two = jnp.concatenate([value, permute(value, y_perm(n))], 0)
    return two, permute(two, core_perm(n))


def block_row(i, place, planes):
    step, inner = i // 4, i % 4
    plane = lax.rem(place // 4 + planes - step, planes)
    y = lax.rem(place // 2, 2)
    core = lax.rem(place, 2)
    y = 1 - y if inner % 2 else y
    core = 1 - core if inner >= 2 else core
    return plane * 4 + y * 2 + core


def gram_kernel(place_ref, *refs, planes, chunk, width, scale):
    pieces, a_ref, out_ref, acc, whole = refs[: 2 * planes], refs[-4], refs[-3], refs[-2], refs[-1]
    j = pl.program_id(0)
    place = place_ref[0]
    shard = pieces[0].shape[0] // 2

    @pl.when(j == 0)
    def _():
        acc[...] = jnp.zeros_like(acc)

    tokens = jnp.concatenate([p[:, pl.ds(pl.multiple_of(j * chunk, chunk), chunk)] for p in pieces], 0)
    part = lax.dot_general(tokens, a_ref[...], (((1,), (1,)), ((), ())), preferred_element_type=F32)
    acc[...] += part * jnp.where(j < width // chunk, 0.5, 1.0)

    @pl.when(j == pl.num_programs(0) - 1)
    def _():
        own = a_ref.shape[0]
        left = pl.multiple_of(lax.rem(place, 4) * own, own)
        total = acc.shape[0]
        for i in range(4 * planes):
            row = pl.multiple_of(block_row(i, place, planes) * shard, shard)
            whole[0, pl.ds(row, shard), :] = acc[i * shard:(i + 1) * shard, :].astype(BF16)
            piece = pieces[i // 2]
            whole[1, pl.ds(row, shard), :] = piece[(i % 2) * shard:(i % 2 + 1) * shard, pl.ds(left, own)]
        half = lax.dot_general(whole[1], whole[0], (((1,), (1,)), ((), ())), preferred_element_type=F32)
        out_ref[...] = (half + half.T) * scale


def gram_part(pieces, input_factor, place, planes):
    own, features = input_factor.shape
    width = features // planes
    chunk = min(1024, width)
    steps = (planes // 2 + 1) * width // chunk
    tokens = sum(p.shape[0] for p in pieces)
    per_plane = width // chunk
    columns = features // chunk

    def a_map(j, place_ref):
        return 0, lax.rem(place_ref[0] // 4 * per_plane + j, columns)

    return pl.pallas_call(
        functools.partial(gram_kernel, planes=planes, chunk=chunk, width=width, scale=float(features) ** -0.5),
        grid_spec=pltpu.PrefetchScalarGridSpec(
            num_scalar_prefetch=1,
            grid=(steps,),
            in_specs=[pl.BlockSpec(memory_space=pltpu.VMEM)] * len(pieces) + [pl.BlockSpec((own, chunk), a_map)],
            out_specs=pl.BlockSpec((tokens, tokens), lambda j, _: (0, 0)),
            scratch_shapes=[pltpu.VMEM((tokens, own), F32), pltpu.VMEM((2, tokens, own), BF16)],
        ),
        out_shape=jax.ShapeDtypeStruct((tokens, tokens), F32),
        compiler_params=pltpu.CompilerParams(vmem_limit_bytes=VMEM_LIMIT),
        cost_estimate=pl.CostEstimate(
            flops=2 * tokens * own * (steps * chunk + tokens), bytes_accessed=2 * own * steps * chunk, transcendentals=0
        ),
    )(place, *pieces, input_factor)


def update_kernel(place_ref, *refs, planes, scale):
    pieces = refs[: 2 * planes]
    gram_ref, grads_ref, factor_ref, out_ref, left_abs, left = refs[2 * planes:]
    place = place_ref[0]
    shard = pieces[0].shape[0] // 2

    @pl.when(pl.program_id(0) == 0)
    def _():
        left_abs[...] = jnp.dot(gram_ref[...], grads_ref[...], preferred_element_type=F32).astype(BF16)
        rows = []
        for i in range(4 * planes):
            row = pl.multiple_of(block_row(i, place, planes) * shard, shard)
            rows.append(left_abs[pl.ds(row, shard), :])
        left[...] = jnp.concatenate(rows, 0).T

    slab = jnp.concatenate([p[...] for p in pieces], 0)
    out_ref[...] = factor_ref[...] + jnp.dot(left[...], slab, preferred_element_type=F32) * scale


def update(pieces, gram, grads, output_factor, place, planes):
    rows, columns = output_factor.shape
    tokens = gram.shape[0]
    chunk = min(512, columns)
    shard2 = pieces[0].shape[0]
    return pl.pallas_call(
        functools.partial(update_kernel, planes=planes, scale=1.0 / tokens),
        grid_spec=pltpu.PrefetchScalarGridSpec(
            num_scalar_prefetch=1,
            grid=(columns // chunk,),
            in_specs=[pl.BlockSpec((shard2, chunk), lambda j, _: (0, j))] * len(pieces)
            + [
                pl.BlockSpec((tokens, tokens), lambda j, _: (0, 0)),
                pl.BlockSpec((tokens, rows), lambda j, _: (0, 0)),
                pl.BlockSpec((rows, chunk), lambda j, _: (0, j)),
            ],
            out_specs=pl.BlockSpec((rows, chunk), lambda j, _: (0, j)),
            scratch_shapes=[pltpu.VMEM((tokens, rows), BF16), pltpu.VMEM((rows, tokens), BF16)],
        ),
        out_shape=jax.ShapeDtypeStruct((rows, columns), F32),
        compiler_params=pltpu.CompilerParams(vmem_limit_bytes=VMEM_LIMIT),
        cost_estimate=pl.CostEstimate(
            flops=2 * rows * tokens * (columns + tokens), bytes_accessed=8 * rows * columns, transcendentals=0
        ),
    )(place, *pieces, gram, grads, output_factor)


def sum_over_row(part, place):
    n = lax.axis_size("row")
    core, y = place % 2, place // 2 % 2

    def split(value, which):
        halves = value.reshape(2, value.shape[0] // 2, value.shape[1])
        pick = functools.partial(lax.dynamic_index_in_dim, halves, axis=0, keepdims=False)
        return pick(which), pick(1 - which)

    def join(mine, other, which):
        return jnp.where(which == 0, jnp.concatenate([mine, other], 0), jnp.concatenate([other, mine], 0))

    mine, other = split(part, core)
    mine = mine + permute(other, core_perm(n))
    mine, other = split(mine, y)
    mine = mine + permute(other.astype(BF16), y_perm(n)).astype(F32)
    step = 4
    while step < n:
        mine = mine + permute(mine.astype(BF16), [(i, i ^ step) for i in range(n)]).astype(F32)
        step *= 2
    mine = mine.astype(BF16)
    mine = join(mine, permute(mine, y_perm(n)), y)
    return join(mine, permute(mine, core_perm(n)), core)


def per_device(inputs, input_factor, out_grads, output_factor):
    n = lax.axis_size("row")
    planes = n // 4
    place = lax.axis_index("row")
    plane = place // 4
    half = planes // 2
    width = inputs.shape[1] // planes

    turned = lax.dynamic_slice_in_dim(jnp.concatenate([inputs, inputs], 1), plane * width, inputs.shape[1], 1)
    turned = jnp.concatenate([turned, turned[:, : (half + 1) * width]], 1)

    def main(step):
        return turned[:, step * width:(step + half) * width]

    def extra(step):
        return turned[:, (step + half) * width:(step + half + 1) * width]

    wanted = [takes_extra(q, planes) for q in range(planes)]
    steps = sorted(range(1, planes), key=lambda k: -min(k, planes - k))
    arrived = {}
    for k in steps:
        some = [(i, j) for i, j in plane_perm(n, k) if wanted[j // 4]]
        arrived[k] = (permute(main(k), plane_perm(n, k)), permute(extra(k), some))
    mine = jnp.asarray(wanted)[plane]
    arrived[0] = (main(0), jnp.where(mine, extra(0), jnp.zeros_like(extra(0))))
    pieces = []
    for k in range(planes):
        pieces += spread(jnp.concatenate(arrived[k], 1))

    slab_width = output_factor.shape[1]
    hold, _ = lax.optimization_barrier((out_grads, arrived[half][0]))
    grad_cols = lax.all_to_all(hold, "row", split_axis=1, concat_axis=0, tiled=True)
    slab = hold[:, :slab_width]
    slab_pieces = []
    for k in range(planes):
        slab_pieces += spread(permute(slab, plane_perm(n, k)) if k else slab)

    scalar = place.reshape(1)
    gram = sum_over_row(gram_part(pieces, input_factor, scalar, planes), place)
    return update(slab_pieces, gram, grad_cols, output_factor, scalar, planes)


def solution(mesh):
    spec = P(("groups", "row"), None)
    return jax.shard_map(per_device, mesh=mesh, in_specs=(spec,) * 4, out_specs=spec, check_vma=False)
```

time: 273 us -> 196 us (0.72)
  waiting for transfers between devices: 223 us -> 106 us
  starting transfers between devices: 7.47 us -> 45.7 us
  Pallas kernels: 0 us -> 29 us
  matrix products: 25.4 us -> 0 us
  between operations: 13.1 us -> 0.43 us
  other arithmetic: 0 us -> 8.37 us
    all_gather x2 -> x0, waiting for transfers between devices: 127 us -> none  [the longest x1 87.8 us: per_device(): whole = lax.all_gather(inputs, 'row', axis=0, tiled=True)]
    ppermute x0 -> x31, waiting for transfers between devices: none -> 106 us  [permute(): return lax.ppermute(value, 'row', perm)]
    psum x1 -> x0, waiting for transfers between devices: 95.3 us -> none  [per_device(): gram = (lax.psum(partial_value, 'row') * factor).astype(jnp.bfloat16)]
    ppermute x0 -> x31, starting transfers between devices: none -> 40.8 us  [permute(): return lax.ppermute(value, 'row', perm)]
    pallas_call x0 -> x2, Pallas kernels: none -> 29 us  [the longest x1 18.4 us: update(): pl.pallas_call(functools.partial(update_kernel, planes=planes, scale=1.0...]
    dot_general x2 -> x0, matrix products: 25.4 us -> none  [the longest x1 13.6 us: per_device(): update = jnp.dot(left, slab_all, preferred_element_type=jnp.float32)]
    concatenate x0 -> x8, other arithmetic: none -> 4.43 us  [the longest x5 3.04 us: spread(): two = jnp.concatenate([value, permute(value, y_perm(n))], 0)]
    select_n x0 -> x2, other arithmetic: none -> 3.02 us  [join(): jnp.where(which == 0, jnp.concatenate([mine, other], 0), jnp.concatenate(...]
  transfers between devices with their start and end apart: 4 -> 32, of which waited for: 3 -> 11; matrix products, arithmetic and copies ran while one was open for 6% -> 5% of each run, Pallas kernels for 0% -> 5%
where the time goes in v1:
time: 196 us; the launch traced here: 195 us
  waiting for transfers between devices  106 us (54%)
  starting transfers between devices  45.7 us (23%)
  Pallas kernels  29 us (15%)
  other arithmetic  8.37 us (4%)
  local copies, waits for them, and re-layouts  5.69 us (3%)
    ppermute x31, waiting for transfers between devices, permute(): return lax.ppermute(value, 'row', perm)  106 us
    ppermute x31, starting transfers between devices, permute(): return lax.ppermute(value, 'row', perm)  40.8 us
    pallas_call x1, Pallas kernels, update(): pl.pallas_call(functools.partial(update_kernel, planes=planes, scale=1.0...  18.4 us
    pallas_call x1, Pallas kernels, gram_part(): pl.pallas_call(functools.partial(gram_kernel, planes=planes, chunk=chunk,...  10.6 us
    all_to_all x1, starting transfers between devices, per_device(): lax.all_to_all(hold, 'row', split_axis=1, concat_axis=0, tiled=True)  4.92 us
  transfers between devices with their start and end apart: 32, of which 11 were waited for; matrix products, arithmetic and copies ran while one was open for 5% of the time, Pallas kernels for 5%

profile of v1, /device:TPU:0, one launch (start us, length us, event | category | flops | bytes accessed | tf_op | source)
XLA Modules:
  0.0 195.2 jit_solution(13800649010028136063)
XLA Ops:
  0.0 1.2 dynamic_slice.21
  1.2 1.3 fusion
  2.5 0.7 fusion.4
  3.2 7.0 %collective-permute-start.22 = (bf16[32,2048]{1,0:T(8,128)(2,1)S(1)}, bf16[32,2048]{1,0:T(8,128)(2,1)S(1)}, u32[]{:S(2)}, u32[]{:S(2)}) collective-permute-start(bf16[32,2048]{1,0:T(8,128)(2,1)S(1)} %get-tuple-element.7), channel_id=1, source_target_pairs={{0,12},{1,13},{2,14},{3,15},{4,0},{5,1},{6,2},{7,3},{16,28},{17,29... | collective-permute-start | bytes 393224 | tf_op jit(solution)/shard_map/ppermute | solution.py:16
  10.2 1.3 collective-permute-start.18
  11.5 1.3 collective-permute-start.15
  12.8 0.1 pad_maximum_fusion.6
  12.9 4.5 %collective-permute-start.21 = (bf16[32,4096]{1,0:T(8,128)(2,1)S(1)}, bf16[32,4096]{1,0:T(8,128)(2,1)S(1)}, u32[]{:S(2)}, u32[]{:S(2)}) collective-permute-start(bf16[32,4096]{1,0:T(8,128)(2,1)S(1)} %get-tuple-element.11), channel_id=1, source_target_pairs={{0,12},{1,13},{2,14},{3,15},{4,0},{5,1},{6,2},{7,3},{8,4},{9,5},{1... | collective-permute-start | bytes 786440 | tf_op jit(solution)/shard_map/ppermute | solution.py:16
  17.5 20.2 %collective-permute-done = bf16[32,4096]{1,0:T(8,128)(2,1)S(1)} collective-permute-done((bf16[32,4096]{1,0:T(8,128)(2,1)S(1)}, bf16[32,4096]{1,0:T(8,128)(2,1)S(1)}, u32[]{:S(2)}, u32[]{:S(2)}) %collective-permute-start) | collective-permute-done | bytes 262176 | tf_op jit(solution)/shard_map/ppermute | solution.py:16
  37.6 1.6 collective-permute-start.12
  39.2 7.2 %collective-permute-done.14 = bf16[32,4096]{1,0:T(8,128)(2,1)S(1)} collective-permute-done((bf16[32,4096]{1,0:T(8,128)(2,1)S(1)}, bf16[32,4096]{1,0:T(8,128)(2,1)S(1)}, u32[]{:S(2)}, u32[]{:S(2)}) %collective-permute-start.14) | collective-permute-done | bytes 262176 | tf_op jit(solution)/shard_map/ppermute | solution.py:16
  46.4 1.5 collective-permute-start.19
  48.0 0.0 collective-permute-done.15
  48.0 0.6 collective-permute-start.16
  48.6 0.0 collective-permute-done.21
  48.6 0.0 collective-permute-done.22
  48.6 1.6 collective-permute-start.23
  50.2 0.1 pad_maximum_fusion.refs_0_
  50.3 0.1 collective-permute-start.13
  50.4 22.5 %collective-permute-done.23 = bf16[32,6144]{1,0:T(8,128)(2,1)S(1)} collective-permute-done((bf16[32,6144]{1,0:T(8,128)(2,1)S(1)}, bf16[32,6144]{1,0:T(8,128)(2,1)S(1)}, u32[]{:S(2)}, u32[]{:S(2)}) %collective-permute-start.23) | collective-permute-done | bytes 393248 | tf_op jit(solution)/shard_map/ppermute | solution.py:16
  72.8 0.1 pad_maximum_fusion.3.refs_6_
  72.9 0.0 copy-start.5
  72.9 0.1 collective-permute-start.24
  73.0 0.1 pad_maximum_fusion.1.refs_2_
  73.1 0.5 collective-permute-start.17
  73.6 1.0 pad_maximum_fusion.2.refs_4_
  74.6 0.2 collective-permute-start.20
  74.8 0.1 copy-done.5
  74.9 0.7 slice.33
  75.6 1.5 collective-permute-start.1
  77.1 1.1 copy.9
  78.2 4.9 %all-to-all-start = ((bf16[32,16,1024]{2,0,1:T(8,128)(2,1)}), bf16[32,16,1024]{2,0,1:T(8,128)(2,1)S(1)}, u32[]{:S(2)}, u32[]{:S(2)}) async-start(bf16[32,16,1024]{2,0,1:T(8,128)(2,1)} %bitcast.24), calls=%async_computation | async-start | bytes 2097152 | tf_op jit(solution)/shard_map/all_to_all | solution.py:210
  83.1 1.2 collective-permute-done.1
  84.4 0.7 collective-permute-start.3
  85.1 1.9 pad_maximum_fusion.4.refs_0_
  87.0 23.7 %collective-permute-done.3 = bf16[32,4096]{1,0:T(8,128)(2,1)S(1)} collective-permute-done((bf16[32,4096]{1,0:T(8,128)(2,1)}, bf16[32,4096]{1,0:T(8,128)(2,1)S(1)}, u32[]{:S(2)}, u32[]{:S(2)}) %collective-permute-start.3) | collective-permute-done | bytes 262176 | tf_op jit(solution)/shard_map/ppermute | solution.py:16
  110.8 10.7 %collective-permute-start.6 = (bf16[32,4096]{1,0:T(8,128)(2,1)}, bf16[32,4096]{1,0:T(8,128)(2,1)S(1)}, u32[]{:S(2)}, u32[]{:S(2)}) collective-permute-start(bf16[32,4096]{1,0:T(8,128)(2,1)} %slice.33), channel_id=1, source_target_pairs={{0,8},{1,9},{2,10},{3,11},{4,12},{5,13},{6,14},{7,15},{8,0},{9,1},... | collective-permute-start | bytes 786440 | tf_op jit(solution)/shard_map/ppermute | solution.py:16
  121.5 1.6 collective-permute-start.4
  123.1 10.6 %shard_map.55 = f32[512,512]{1,0:T(8,128)} custom-call(s32[1]{0:T(128)} %bitcast.place_ref, bf16[64,6144]{1,0:T(8,128)(2,1)} %copy-done.2, bf16[64,6144]{1,0:T(8,128)(2,1)} %collective-permute-done.13.refs_1_, bf16[64,6144]{1,0:T(8,128)(2,1)} %copy-done.4, bf16[64,6144]{1,0:T(8,128)(2,1)} %collective-permute-done.17.refs_3_, ...), custom_call_target="tpu_custom_call" | custom-call | flops 3489660928 | bytes 6291456 | tf_op jit(solution)/shard_map/pallas_call | solution.py:91
  133.7 1.2 dynamic-slice_bitcast_fusion
  134.9 0.2 collective-permute-start.25
  135.1 0.6 collective-permute-start.10
  135.7 3.3 %collective-permute-done.6 = bf16[32,4096]{1,0:T(8,128)(2,1)S(1)} collective-permute-done((bf16[32,4096]{1,0:T(8,128)(2,1)}, bf16[32,4096]{1,0:T(8,128)(2,1)S(1)}, u32[]{:S(2)}, u32[]{:S(2)}) %collective-permute-start.6) | collective-permute-done | bytes 262176 | tf_op jit(solution)/shard_map/ppermute | solution.py:16
  139.1 1.5 collective-permute-start.7
  140.6 0.1 bitcast_add_fusion
  140.8 0.6 collective-permute-start.26
  141.4 10.8 %collective-permute-done.26 = bf16[128,512]{1,0:T(8,128)(2,1)S(1)} collective-permute-done((bf16[128,512]{1,0:T(8,128)(2,1)S(1)}, bf16[128,512]{1,0:T(8,128)(2,1)S(1)}, u32[]{:S(2)}, u32[]{:S(2)}) %collective-permute-start.26) | collective-permute-done | bytes 131104 | tf_op jit(solution)/shard_map/ppermute | solution.py:16
  152.2 2.1 %collective-permute-start.27 = (bf16[128,512]{1,0:T(8,128)(2,1)S(1)}, bf16[128,512]{1,0:T(8,128)(2,1)S(1)}, u32[]{:S(2)}, u32[]{:S(2)}) collective-permute-start(bf16[128,512]{1,0:T(8,128)(2,1)S(1)} %fusion.3), channel_id=1, source_target_pairs={{0,4},{1,5},{2,6},{3,7},{4,0},{5,1},{6,2},{7,3},{8,12},{9,13},{10,... | collective-permute-start | bytes 393224 | tf_op jit(solution)/shard_map/ppermute | solution.py:16
  154.4 0.1 collective-permute-start.11
  154.4 3.1 %collective-permute-done.27 = bf16[128,512]{1,0:T(8,128)(2,1)S(1)} collective-permute-done((bf16[128,512]{1,0:T(8,128)(2,1)S(1)}, bf16[128,512]{1,0:T(8,128)(2,1)S(1)}, u32[]{:S(2)}, u32[]{:S(2)}) %collective-permute-start.27) | collective-permute-done | bytes 131104 | tf_op jit(solution)/shard_map/ppermute | solution.py:16
  157.6 0.1 collective-permute-start.28
  157.8 0.1 collective-permute-start.8
  157.8 7.9 %collective-permute-done.28 = bf16[128,512]{1,0:T(8,128)(2,1)S(1)} collective-permute-done((bf16[128,512]{1,0:T(8,128)(2,1)S(1)}, bf16[128,512]{1,0:T(8,128)(2,1)S(1)}, u32[]{:S(2)}, u32[]{:S(2)}) %collective-permute-start.28) | collective-permute-done | bytes 131104 | tf_op jit(solution)/shard_map/ppermute | solution.py:16
  165.7 0.1 add_convert_fusion
  165.8 0.6 collective-permute-start.29
  166.4 0.1 collective-permute-start.5
  166.5 4.5 %collective-permute-done.29 = bf16[128,512]{1,0:T(8,128)(2,1)} collective-permute-done((bf16[128,512]{1,0:T(8,128)(2,1)S(1)}, bf16[128,512]{1,0:T(8,128)(2,1)}, u32[]{:S(2)}, u32[]{:S(2)}) %collective-permute-start.29) | collective-permute-done | bytes 131104 | tf_op jit(solution)/shard_map/ppermute | solution.py:16
  170.9 1.1 maximum_select_fusion.1
  172.0 0.1 collective-permute-start.30
  172.1 1.6 collective-permute-done.30
  173.7 2.0 %maximum_select_fusion.refs_8_ = bf16[512,512]{1,0:T(8,128)(2,1)} fusion(bf16[256,512]{1,0:T(8,128)(2,1)} %collective-permute-done.30, bf16[256,512]{1,0:T(8,128)(2,1)S(1)} %maximum_select_fusion.1, pred[]{:T(512)S(6)} %eq.9), kind=kLoop, calls=%fused_computation.9 | loop fusion | flops 2359296 | bytes 1048577 | tf_op jit(solution)/shard_map/jit(_where)/select_n | solution.py:164
  175.8 0.7 copy-done.9
  176.5 0.4 copy-done.1
  176.8 18.4 %shard_map.56 = f32[1024,4096]{1,0:T(8,128)} custom-call(s32[1]{0:T(128)} %bitcast.place_ref, bf16[64,4096]{1,0:T(8,128)(2,1)} %pad_maximum_fusion.4.refs_0_, bf16[64,4096]{1,0:T(8,128)(2,1)} %collective-permute-done.2.refs_1_, bf16[64,4096]{1,0:T(8,128)(2,1)} %copy-done.6, bf16[64,4096]{1,0:T(8,128)(2,1)} %collective-permute-done.5.refs_3_, ...), custom_call_target="tpu_custom_call" | custom-call | flops 4831838208 | bytes 33554432 | tf_op jit(solution)/shard_map/pallas_call | solution.py:132
  (55 shorter events, 0.4 us)
Async XLA Ops:
  3.2 45.4 %collective-permute-start.22 = (bf16[32,2048]{1,0:T(8,128)(2,1)S(1)}, bf16[32,2048]{1,0:T(8,128)(2,1)S(1)}, u32[]{:S(2)}, u32[]{:S(2)}) collective-permute-start(bf16[32,2048]{1,0:T(8,128)(2,1)S(1)} %get-tuple-element.7), channel_id=1, source_target_pairs={{0,12},{1,13},{2,14},{3,15},{4,0},{5,1},{6,2},{7,3},{16,28},{17,29... | collective-permute-start | bytes 393224 | tf_op jit(solution)/shard_map/ppermute | solution.py:16
  10.2 27.5 %collective-permute-start.18 = (bf16[32,2048]{1,0:T(8,128)(2,1)S(1)}, bf16[32,2048]{1,0:T(8,128)(2,1)S(1)}, u32[]{:S(2)}, u32[]{:S(2)}) collective-permute-start(bf16[32,2048]{1,0:T(8,128)(2,1)S(1)} %get-tuple-element.8), channel_id=1, source_target_pairs={{4,12},{5,13},{6,14},{7,15},{8,0},{9,1},{10,2},{11,3},{20,28},{21,... | collective-permute-start | bytes 393224 | tf_op jit(solution)/shard_map/ppermute | solution.py:16
  11.5 36.5 %collective-permute-start.15 = (bf16[32,2048]{1,0:T(8,128)(2,1)S(1)}, bf16[32,2048]{1,0:T(8,128)(2,1)S(1)}, u32[]{:S(2)}, u32[]{:S(2)}) collective-permute-start(bf16[32,2048]{1,0:T(8,128)(2,1)S(1)} %get-tuple-element.9), channel_id=1, source_target_pairs={{8,12},{9,13},{10,14},{11,15},{12,0},{13,1},{14,2},{15,3},{24,28},... | collective-permute-start | bytes 393224 | tf_op jit(solution)/shard_map/ppermute | solution.py:16
  12.9 35.7 %collective-permute-start.21 = (bf16[32,4096]{1,0:T(8,128)(2,1)S(1)}, bf16[32,4096]{1,0:T(8,128)(2,1)S(1)}, u32[]{:S(2)}, u32[]{:S(2)}) collective-permute-start(bf16[32,4096]{1,0:T(8,128)(2,1)S(1)} %get-tuple-element.11), channel_id=1, source_target_pairs={{0,12},{1,13},{2,14},{3,15},{4,0},{5,1},{6,2},{7,3},{8,4},{9,5},{1... | collective-permute-start | bytes 786440 | tf_op jit(solution)/shard_map/ppermute | solution.py:16
  17.4 20.2 %collective-permute-start = (bf16[32,4096]{1,0:T(8,128)(2,1)S(1)}, bf16[32,4096]{1,0:T(8,128)(2,1)S(1)}, u32[]{:S(2)}, u32[]{:S(2)}) collective-permute-start(bf16[32,4096]{1,0:T(8,128)(2,1)S(1)} %get-tuple-element.14), channel_id=1, source_target_pairs={{0,8},{1,9},{2,10},{3,11},{4,12},{5,13},{6,14},{7,15},{8,0},{9,1},... | collective-permute-start | bytes 786440 | tf_op jit(solution)/shard_map/ppermute | solution.py:16
  37.6 8.8 %collective-permute-start.14 = (bf16[32,4096]{1,0:T(8,128)(2,1)S(1)}, bf16[32,4096]{1,0:T(8,128)(2,1)S(1)}, u32[]{:S(2)}, u32[]{:S(2)}) collective-permute-start(bf16[32,4096]{1,0:T(8,128)(2,1)S(1)} %get-tuple-element.12), channel_id=1, source_target_pairs={{0,4},{1,5},{2,6},{3,7},{4,8},{5,9},{6,10},{7,11},{8,12},{9,13},{1... | collective-permute-start | bytes 786440 | tf_op jit(solution)/shard_map/ppermute | solution.py:16
  37.6 12.6 %collective-permute-start.12 = (bf16[32,6144]{1,0:T(8,128)(2,1)S(1)}, bf16[32,6144]{1,0:T(8,128)(2,1)S(1)}, u32[]{:S(2)}, u32[]{:S(2)}) collective-permute-start(bf16[32,6144]{1,0:T(8,128)(2,1)S(1)} %pad_maximum_fusion.5), channel_id=1, source_target_pairs={{0,2},{1,3},{2,0},{3,1},{4,6},{5,7},{6,4},{7,5},{8,10},{9,11},{10,... | collective-permute-start | bytes 1179656 | tf_op jit(solution)/shard_map/ppermute | solution.py:16
  46.4 27.2 %collective-permute-start.19 = (bf16[32,6144]{1,0:T(8,128)(2,1)S(1)}, bf16[32,6144]{1,0:T(8,128)(2,1)S(1)}, u32[]{:S(2)}, u32[]{:S(2)}) collective-permute-start(bf16[32,6144]{1,0:T(8,128)(2,1)S(1)} %constant_dynamic-update-slice_fusion.8), channel_id=1, source_target_pairs={{0,2},{1,3},{2,0},{3,1},{4,6},{5,7},{6,4},{7,5},{8,10},{9,11},{10,... | collective-permute-start | bytes 1179656 | tf_op jit(solution)/shard_map/ppermute | solution.py:16
  48.0 25.0 %collective-permute-start.16 = (bf16[32,6144]{1,0:T(8,128)(2,1)S(1)}, bf16[32,6144]{1,0:T(8,128)(2,1)S(1)}, u32[]{:S(2)}, u32[]{:S(2)}) collective-permute-start(bf16[32,6144]{1,0:T(8,128)(2,1)S(1)} %constant_dynamic-update-slice_fusion.6), channel_id=1, source_target_pairs={{0,2},{1,3},{2,0},{3,1},{4,6},{5,7},{6,4},{7,5},{8,10},{9,11},{10,... | collective-permute-start | bytes 1179656 | tf_op jit(solution)/shard_map/ppermute | solution.py:16
  48.6 24.2 %collective-permute-start.23 = (bf16[32,6144]{1,0:T(8,128)(2,1)S(1)}, bf16[32,6144]{1,0:T(8,128)(2,1)S(1)}, u32[]{:S(2)}, u32[]{:S(2)}) collective-permute-start(bf16[32,6144]{1,0:T(8,128)(2,1)S(1)} %constant_dynamic-update-slice_fusion.10), channel_id=1, source_target_pairs={{0,2},{1,3},{2,0},{3,1},{4,6},{5,7},{6,4},{7,5},{8,10},{9,11},{10,... | collective-permute-start | bytes 1179656 | tf_op jit(solution)/shard_map/ppermute | solution.py:16
  50.3 22.8 %copy-start.2 = (bf16[64,6144]{1,0:T(8,128)(2,1)}, bf16[64,6144]{1,0:T(8,128)(2,1)S(1)}, u32[]{:S(2)}) copy-start(bf16[64,6144]{1,0:T(8,128)(2,1)S(1)} %pad_maximum_fusion.refs_0_) | copy-start | bytes 2359300
  50.3 60.5 %collective-permute-start.13 = (bf16[64,6144]{1,0:T(8,128)(2,1)S(1)}, bf16[64,6144]{1,0:T(8,128)(2,1)}, u32[]{:S(2)}, u32[]{:S(2)}) collective-permute-start(bf16[64,6144]{1,0:T(8,128)(2,1)S(1)} %pad_maximum_fusion.refs_0_), channel_id=1, source_target_pairs={{0,1},{1,0},{2,3},{3,2},{4,5},{5,4},{6,7},{7,6},{8,9},{9,8},{10,11... | collective-permute-start | bytes 2359304 | tf_op jit(solution)/shard_map/ppermute | solution.py:16
  72.9 1.7 copy-start.3
  72.9 2.0 %copy-start.5 = (bf16[32,16384]{1,0:T(8,128)(2,1)S(1)}, bf16[32,16384]{1,0:T(8,128)(2,1)}, u32[]{:S(2)}) copy-start(bf16[32,16384]{1,0:T(8,128)(2,1)} %param.7) | copy-start | bytes 3145732
  72.9 48.6 %collective-permute-start.24 = (bf16[64,6144]{1,0:T(8,128)(2,1)S(1)}, bf16[64,6144]{1,0:T(8,128)(2,1)}, u32[]{:S(2)}, u32[]{:S(2)}) collective-permute-start(bf16[64,6144]{1,0:T(8,128)(2,1)S(1)} %pad_maximum_fusion.3.refs_6_), channel_id=1, source_target_pairs={{0,1},{1,0},{2,3},{3,2},{4,5},{5,4},{6,7},{7,6},{8,9},{9,8},{10,11... | collective-permute-start | bytes 2359304 | tf_op jit(solution)/shard_map/ppermute | solution.py:16
  73.1 5.1 %copy-start.4 = (bf16[64,6144]{1,0:T(8,128)(2,1)}, bf16[64,6144]{1,0:T(8,128)(2,1)S(1)}, u32[]{:S(2)}) copy-start(bf16[64,6144]{1,0:T(8,128)(2,1)S(1)} %pad_maximum_fusion.1.refs_2_) | copy-start | bytes 2359300
  73.1 48.5 %collective-permute-start.17 = (bf16[64,6144]{1,0:T(8,128)(2,1)S(1)}, bf16[64,6144]{1,0:T(8,128)(2,1)}, u32[]{:S(2)}, u32[]{:S(2)}) collective-permute-start(bf16[64,6144]{1,0:T(8,128)(2,1)S(1)} %pad_maximum_fusion.1.refs_2_), channel_id=1, source_target_pairs={{0,1},{1,0},{2,3},{3,2},{4,5},{5,4},{6,7},{7,6},{8,9},{9,8},{10,11... | collective-permute-start | bytes 2359304 | tf_op jit(solution)/shard_map/ppermute | solution.py:16
  74.6 48.5 %collective-permute-start.20 = (bf16[64,6144]{1,0:T(8,128)(2,1)}, bf16[64,6144]{1,0:T(8,128)(2,1)}, u32[]{:S(2)}, u32[]{:S(2)}) collective-permute-start(bf16[64,6144]{1,0:T(8,128)(2,1)} %pad_maximum_fusion.2.refs_4_), channel_id=1, source_target_pairs={{0,1},{1,0},{2,3},{3,2},{4,5},{5,4},{6,7},{7,6},{8,9},{9,8},{10,11... | collective-permute-start | bytes 2359304 | tf_op jit(solution)/shard_map/ppermute | solution.py:16
  75.6 8.8 %collective-permute-start.1 = (bf16[32,4096]{1,0:T(8,128)(2,1)}, bf16[32,4096]{1,0:T(8,128)(2,1)}, u32[]{:S(2)}, u32[]{:S(2)}) collective-permute-start(bf16[32,4096]{1,0:T(8,128)(2,1)} %slice.33), channel_id=1, source_target_pairs={{0,2},{1,3},{2,0},{3,1},{4,6},{5,7},{6,4},{7,5},{8,10},{9,11},{10,... | collective-permute-start | bytes 786440 | tf_op jit(solution)/shard_map/ppermute | solution.py:16
  78.2 97.5 %all-to-all-start = ((bf16[32,16,1024]{2,0,1:T(8,128)(2,1)}), bf16[32,16,1024]{2,0,1:T(8,128)(2,1)S(1)}, u32[]{:S(2)}, u32[]{:S(2)}) async-start(bf16[32,16,1024]{2,0,1:T(8,128)(2,1)} %bitcast.24), calls=%async_computation | async-start | bytes 2097152 | tf_op jit(solution)/shard_map/all_to_all | solution.py:210
  84.4 26.4 %collective-permute-start.3 = (bf16[32,4096]{1,0:T(8,128)(2,1)}, bf16[32,4096]{1,0:T(8,128)(2,1)S(1)}, u32[]{:S(2)}, u32[]{:S(2)}) collective-permute-start(bf16[32,4096]{1,0:T(8,128)(2,1)} %slice.33), channel_id=1, source_target_pairs={{0,4},{1,5},{2,6},{3,7},{4,8},{5,9},{6,10},{7,11},{8,12},{9,13},{1... | collective-permute-start | bytes 786440 | tf_op jit(solution)/shard_map/ppermute | solution.py:16
  110.8 24.4 %collective-permute-start.9 = (bf16[32,4096]{1,0:T(8,128)(2,1)}, bf16[32,4096]{1,0:T(8,128)(2,1)S(1)}, u32[]{:S(2)}, u32[]{:S(2)}) collective-permute-start(bf16[32,4096]{1,0:T(8,128)(2,1)} %slice.33), channel_id=1, source_target_pairs={{0,12},{1,13},{2,14},{3,15},{4,0},{5,1},{6,2},{7,3},{8,4},{9,5},{1... | collective-permute-start | bytes 786440 | tf_op jit(solution)/shard_map/ppermute | solution.py:16
  110.8 28.3 %collective-permute-start.6 = (bf16[32,4096]{1,0:T(8,128)(2,1)}, bf16[32,4096]{1,0:T(8,128)(2,1)S(1)}, u32[]{:S(2)}, u32[]{:S(2)}) collective-permute-start(bf16[32,4096]{1,0:T(8,128)(2,1)} %slice.33), channel_id=1, source_target_pairs={{0,8},{1,9},{2,10},{3,11},{4,12},{5,13},{6,14},{7,15},{8,0},{9,1},... | collective-permute-start | bytes 786440 | tf_op jit(solution)/shard_map/ppermute | solution.py:16
  121.5 54.1 %collective-permute-start.2 = (bf16[64,4096]{1,0:T(8,128)(2,1)}, bf16[64,4096]{1,0:T(8,128)(2,1)}, u32[]{:S(2)}, u32[]{:S(2)}) collective-permute-start(bf16[64,4096]{1,0:T(8,128)(2,1)} %pad_maximum_fusion.4.refs_0_), channel_id=1, source_target_pairs={{0,1},{1,0},{2,3},{3,2},{4,5},{5,4},{6,7},{7,6},{8,9},{9,8},{10,11... | collective-permute-start | bytes 1572872 | tf_op jit(solution)/shard_map/ppermute | solution.py:16
  121.5 44.8 %collective-permute-start.4 = (bf16[32,4096]{1,0:T(8,128)(2,1)S(1)}, bf16[32,4096]{1,0:T(8,128)(2,1)S(1)}, u32[]{:S(2)}, u32[]{:S(2)}) collective-permute-start(bf16[32,4096]{1,0:T(8,128)(2,1)S(1)} %collective-permute-done.3), channel_id=1, source_target_pairs={{0,2},{1,3},{2,0},{3,1},{4,6},{5,7},{6,4},{7,5},{8,10},{9,11},{10,... | collective-permute-start | bytes 786440 | tf_op jit(solution)/shard_map/ppermute | solution.py:16
  133.7 6.9 %copy-start = (f32[512,512]{1,0:T(8,128)S(1)}, f32[512,512]{1,0:T(8,128)}, u32[]{:S(2)}) copy-start(f32[512,512]{1,0:T(8,128)} %shard_map.55) | copy-start | bytes 3145732
  134.9 5.7 %collective-permute-start.25 = (f32[256,512]{1,0:T(8,128)S(1)}, f32[256,512]{1,0:T(8,128)S(1)}, u32[]{:S(2)}, u32[]{:S(2)}) collective-permute-start(f32[256,512]{1,0:T(8,128)S(1)} %dynamic-slice_bitcast_fusion), channel_id=1, source_target_pairs={{0,1},{1,0},{2,3},{3,2},{4,5},{5,4},{6,7},{7,6},{8,9},{9,8},{10,11... | collective-permute-start | bytes 1572872 | tf_op jit(solution)/shard_map/ppermute | solution.py:16
  135.1 19.2 %collective-permute-start.10 = (bf16[32,4096]{1,0:T(8,128)(2,1)S(1)}, bf16[32,4096]{1,0:T(8,128)(2,1)S(1)}, u32[]{:S(2)}, u32[]{:S(2)}) collective-permute-start(bf16[32,4096]{1,0:T(8,128)(2,1)S(1)} %collective-permute-done.9), channel_id=1, source_target_pairs={{0,2},{1,3},{2,0},{3,1},{4,6},{5,7},{6,4},{7,5},{8,10},{9,11},{10,... | collective-permute-start | bytes 786440 | tf_op jit(solution)/shard_map/ppermute | solution.py:16
  139.1 18.6 %collective-permute-start.7 = (bf16[32,4096]{1,0:T(8,128)(2,1)S(1)}, bf16[32,4096]{1,0:T(8,128)(2,1)S(1)}, u32[]{:S(2)}, u32[]{:S(2)}) collective-permute-start(bf16[32,4096]{1,0:T(8,128)(2,1)S(1)} %collective-permute-done.6), channel_id=1, source_target_pairs={{0,2},{1,3},{2,0},{3,1},{4,6},{5,7},{6,4},{7,5},{8,10},{9,11},{10,... | collective-permute-start | bytes 786440 | tf_op jit(solution)/shard_map/ppermute | solution.py:16
  140.8 11.4 %collective-permute-start.26 = (bf16[128,512]{1,0:T(8,128)(2,1)S(1)}, bf16[128,512]{1,0:T(8,128)(2,1)S(1)}, u32[]{:S(2)}, u32[]{:S(2)}) collective-permute-start(bf16[128,512]{1,0:T(8,128)(2,1)S(1)} %fusion.2), channel_id=1, source_target_pairs={{0,2},{1,3},{2,0},{3,1},{4,6},{5,7},{6,4},{7,5},{8,10},{9,11},{10,... | collective-permute-start | bytes 393224 | tf_op jit(solution)/shard_map/ppermute | solution.py:16
  152.2 5.3 %collective-permute-start.27 = (bf16[128,512]{1,0:T(8,128)(2,1)S(1)}, bf16[128,512]{1,0:T(8,128)(2,1)S(1)}, u32[]{:S(2)}, u32[]{:S(2)}) collective-permute-start(bf16[128,512]{1,0:T(8,128)(2,1)S(1)} %fusion.3), channel_id=1, source_target_pairs={{0,4},{1,5},{2,6},{3,7},{4,0},{5,1},{6,2},{7,3},{8,12},{9,13},{10,... | collective-permute-start | bytes 393224 | tf_op jit(solution)/shard_map/ppermute | solution.py:16
  154.4 21.3 %copy-start.8 = (bf16[64,4096]{1,0:T(8,128)(2,1)}, bf16[64,4096]{1,0:T(8,128)(2,1)S(1)}, u32[]{:S(2)}) copy-start(bf16[64,4096]{1,0:T(8,128)(2,1)S(1)} %constant_dynamic-update-slice_fusion.4.refs_6_) | copy-start | bytes 1572868
  154.4 21.3 %collective-permute-start.11 = (bf16[64,4096]{1,0:T(8,128)(2,1)S(1)}, bf16[64,4096]{1,0:T(8,128)(2,1)S(1)}, u32[]{:S(2)}, u32[]{:S(2)}) collective-permute-start(bf16[64,4096]{1,0:T(8,128)(2,1)S(1)} %constant_dynamic-update-slice_fusion.4.refs_6_), channel_id=1, source_target_pairs={{0,1},{1,0},{2,3},{3,2},{4,5},{5,4},{6,7},{7,6},{8,9},{9,8},{10,11... | collective-permute-start | bytes 1572872 | tf_op jit(solution)/shard_map/ppermute | solution.py:16
  157.6 8.1 %collective-permute-start.28 = (bf16[128,512]{1,0:T(8,128)(2,1)S(1)}, bf16[128,512]{1,0:T(8,128)(2,1)S(1)}, u32[]{:S(2)}, u32[]{:S(2)}) collective-permute-start(bf16[128,512]{1,0:T(8,128)(2,1)S(1)} %fusion.1), channel_id=1, source_target_pairs={{0,8},{1,9},{2,10},{3,11},{4,12},{5,13},{6,14},{7,15},{8,0},{9,1},... | collective-permute-start | bytes 393224 | tf_op jit(solution)/shard_map/ppermute | solution.py:16
  157.7 18.0 %copy-start.7 = (bf16[64,4096]{1,0:T(8,128)(2,1)}, bf16[64,4096]{1,0:T(8,128)(2,1)S(1)}, u32[]{:S(2)}) copy-start(bf16[64,4096]{1,0:T(8,128)(2,1)S(1)} %constant_dynamic-update-slice_fusion.2.refs_4_) | copy-start | bytes 1572868
  157.8 17.9 %collective-permute-start.8 = (bf16[64,4096]{1,0:T(8,128)(2,1)S(1)}, bf16[64,4096]{1,0:T(8,128)(2,1)}, u32[]{:S(2)}, u32[]{:S(2)}) collective-permute-start(bf16[64,4096]{1,0:T(8,128)(2,1)S(1)} %constant_dynamic-update-slice_fusion.2.refs_4_), channel_id=1, source_target_pairs={{0,1},{1,0},{2,3},{3,2},{4,5},{5,4},{6,7},{7,6},{8,9},{9,8},{10,11... | collective-permute-start | bytes 1572872 | tf_op jit(solution)/shard_map/ppermute | solution.py:16
  165.8 5.1 %collective-permute-start.29 = (bf16[128,512]{1,0:T(8,128)(2,1)S(1)}, bf16[128,512]{1,0:T(8,128)(2,1)}, u32[]{:S(2)}, u32[]{:S(2)}) collective-permute-start(bf16[128,512]{1,0:T(8,128)(2,1)S(1)} %add_convert_fusion), channel_id=1, source_target_pairs={{0,2},{1,3},{2,0},{3,1},{4,6},{5,7},{6,4},{7,5},{8,10},{9,11},{10,... | collective-permute-start | bytes 393224 | tf_op jit(solution)/shard_map/ppermute | solution.py:16
  166.4 9.4 %copy-start.6 = (bf16[64,4096]{1,0:T(8,128)(2,1)}, bf16[64,4096]{1,0:T(8,128)(2,1)S(1)}, u32[]{:S(2)}) copy-start(bf16[64,4096]{1,0:T(8,128)(2,1)S(1)} %constant_dynamic-update-slice_fusion.refs_2_) | copy-start | bytes 1572868
  166.4 9.3 %collective-permute-start.5 = (bf16[64,4096]{1,0:T(8,128)(2,1)S(1)}, bf16[64,4096]{1,0:T(8,128)(2,1)}, u32[]{:S(2)}, u32[]{:S(2)}) collective-permute-start(bf16[64,4096]{1,0:T(8,128)(2,1)S(1)} %constant_dynamic-update-slice_fusion.refs_2_), channel_id=1, source_target_pairs={{0,1},{1,0},{2,3},{3,2},{4,5},{5,4},{6,7},{7,6},{8,9},{9,8},{10,11... | collective-permute-start | bytes 1572872 | tf_op jit(solution)/shard_map/ppermute | solution.py:16
  172.0 1.7 collective-permute-start.30
  175.7 0.8 copy-start.9
  175.7 1.1 copy-start.1

commit v2 on v0

v2 whole, which is shorter than its diff:
```python
import functools

import jax
import jax.numpy as jnp
from jax import lax
from jax.experimental import pallas as pl
from jax.experimental.pallas import tpu as pltpu
from jax.sharding import PartitionSpec as P

BF16 = jnp.bfloat16
F32 = jnp.float32
MIB = 1024 * 1024


def permute(value, perm):
    return lax.ppermute(value, "row", perm)


def core_perm(n):
    return [(i, i ^ 1) for i in range(n)]


def y_perm(n):
    return [(i, i ^ 2) for i in range(n)]


def plane_perm(n, step):
    return [(i, (i + 4 * step) % n) for i in range(n)]


def call(body, place, inputs, outputs, scratch=(), limit=8 * MIB, flops=0, bytes_accessed=0, far=()):
    vmem = pl.BlockSpec(memory_space=pltpu.VMEM)
    anywhere = pl.BlockSpec(memory_space=pltpu.HBM)
    return pl.pallas_call(
        body,
        in_specs=[pl.BlockSpec(memory_space=pltpu.SMEM)]
        + [anywhere if i in far else vmem for i in range(len(inputs))],
        out_specs=[vmem] * len(outputs),
        out_shape=[jax.ShapeDtypeStruct(shape, dtype) for shape, dtype in outputs],
        scratch_shapes=list(scratch),
        compiler_params=pltpu.CompilerParams(vmem_limit_bytes=limit),
        cost_estimate=pl.CostEstimate(flops=flops, bytes_accessed=bytes_accessed, transcendentals=0),
    )(place, *inputs)


def pack(place, inputs, wanted):
    outputs = [
        ((sum(inputs[i].shape[0] for i in each), inputs[each[0]].shape[1]), inputs[each[0]].dtype) for each in wanted
    ]

    def body(place_ref, *refs):
        del place_ref
        ins, outs = refs[: len(inputs)], refs[len(inputs):]
        for each, out in zip(wanted, outs):
            row = 0
            for i in each:
                out[row:row + ins[i].shape[0], :] = ins[i][...]
                row += ins[i].shape[0]

    return call(body, place, inputs, outputs)


def token_blocks(groups):
    return [(k, y, core) for group in groups for core in (0, 1) for y in (0, 1) for k in group]


def shard_of(place, block, planes):
    back, other_y, other_core = block
    plane = lax.rem(place // 4 + planes - back, planes)
    y, core = lax.rem(place // 2, 2), lax.rem(place, 2)
    return plane * 4 + (1 - y if other_y else y) * 2 + (1 - core if other_core else core)


def messages(inputs, place, planes):
    rows, features = inputs.shape
    width = features // planes
    used = planes // 2 + 1

    def body(place_ref, x_ref, *outs):
        plane = place_ref[0] // 4
        for k, out in enumerate(outs):
            for j in range(used):
                left = pl.multiple_of(lax.rem(plane + k + j, planes) * width, width)
                out[:, j * width:(j + 1) * width] = x_ref[:, pl.ds(left, width)]

    return call(body, place, [inputs], [((rows, used * width), inputs.dtype)] * planes)


def gram_part(pieces, groups, input_factor, place, planes):
    own, features = input_factor.shape
    width = features // planes
    used = planes // 2 + 1
    blocks = token_blocks(groups)
    tokens = sum(p.shape[0] for p in pieces)
    shard = tokens // len(blocks)
    count = len(pieces)
    scale = float(features) ** -0.5

    def body(place_ref, *refs):
        ins, a_ref, mine_ref, other_ref, near, whole, total, sems = (
            refs[:count], refs[count], *refs[count + 1:]
        )
        here = place_ref[0]
        copies = []
        for j in range(used):
            left = pl.multiple_of(lax.rem(here // 4 + j, planes) * width, width)
            copies.append(pltpu.make_async_copy(a_ref.at[:, pl.ds(left, width)], near.at[j], sems.at[j]))
            copies[-1].start()
        acc = None
        for j in range(used):
            copies[j].wait()
            rows = jnp.concatenate([p[:, j * width:(j + 1) * width] for p in ins], 0)
            part = lax.dot_general(rows, near[j], (((1,), (1,)), ((), ())), preferred_element_type=F32)
            part = part * 0.5 if j in (0, planes // 2) else part
            acc = part if acc is None else acc + part
        left = pl.multiple_of(lax.rem(here, 4) * own, own)
        at = 0
        for piece in ins:
            for low in range(0, piece.shape[0], shard):
                row = pl.multiple_of(shard_of(here, blocks[at // shard], planes) * shard, shard)
                mine = acc[at:at + shard, :]
                high = mine.astype(BF16)
                whole[0, pl.ds(row, shard), :] = high
                whole[1, pl.ds(row, shard), :] = (mine - high.astype(F32)).astype(BF16)
                whole[2, pl.ds(row, shard), :] = piece[low:low + shard, pl.ds(left, own)]
                at += shard
        half = lax.dot_general(whole[2], whole[0], (((1,), (1,)), ((), ())), preferred_element_type=F32)
        half += lax.dot_general(whole[2], whole[1], (((1,), (1,)), ((), ())), preferred_element_type=F32)
        total[...] = (half + half.T) * scale
        core = lax.rem(here, 2)
        mine_ref[...] = total[pl.ds(pl.multiple_of(core * (tokens // 2), tokens // 2), tokens // 2), :]
        other_ref[...] = total[pl.ds(pl.multiple_of((1 - core) * (tokens // 2), tokens // 2), tokens // 2), :]

    return call(
        body, place, [*pieces, input_factor], [((tokens // 2, tokens), F32)] * 2,
        scratch=[
            pltpu.VMEM((used, own, width), BF16), pltpu.VMEM((3, tokens, own), BF16), pltpu.VMEM((tokens, tokens), F32),
            pltpu.SemaphoreType.DMA((used,)),
        ],
        limit=46 * MIB, far=(count,), flops=2 * tokens * own * (used * width + tokens),
        bytes_accessed=2 * own * used * width,
    )


def add_split(mine, other, place, bit, earlier):
    rows, columns = mine.shape
    half = rows // 2

    def body(place_ref, mine_ref, other_ref, *refs):
        keep_ref, give_ref, total = refs[-3:]
        which = lax.rem(place_ref[0] // bit, 2)
        total[...] = mine_ref[...] + other_ref[...].astype(F32)
        keep_ref[...] = total[pl.ds(pl.multiple_of(which * half, half), half), :]
        give_ref[...] = total[pl.ds(pl.multiple_of((1 - which) * half, half), half), :].astype(BF16)

    return call(
        body, place, [mine, other, *earlier], [((half, columns), F32), ((half, columns), BF16)],
        scratch=[pltpu.VMEM((rows, columns), F32)], far=tuple(range(2, 2 + len(earlier))),
    )


def add(mine, other, place, earlier=()):
    def body(place_ref, mine_ref, other_ref, *refs):
        del place_ref
        sum_ref, low_ref = refs[-2:]
        total = mine_ref[...] + other_ref[...].astype(F32)
        sum_ref[...] = total
        low_ref[...] = total.astype(BF16)

    return call(
        body, place, [mine, other, *earlier], [(mine.shape, F32), (mine.shape, BF16)],
        far=tuple(range(2, 2 + len(earlier))),
    )


def join(mine, other, place, bit):
    rows, columns = mine.shape

    def body(place_ref, mine_ref, other_ref, out_ref):
        which = lax.rem(place_ref[0] // bit, 2)
        out_ref[pl.ds(pl.multiple_of(which * rows, rows), rows), :] = mine_ref[...]
        out_ref[pl.ds(pl.multiple_of((1 - which) * rows, rows), rows), :] = other_ref[...]

    return call(body, place, [mine, other], [((2 * rows, columns), mine.dtype)])[0]


def update(slab, blocks, halves, grads, output_factor, place, planes):
    rows, columns = output_factor.shape
    tokens = grads.shape[0]
    shard = tokens // len(blocks)
    chunk = min(1024, columns)
    scale = 1.0 / tokens
    half = tokens // 2

    def body(place_ref, *refs):
        slabs = refs[: len(slab)]
        mine_ref, other_ref, grads_ref, factor_ref, out_ref, gram, left_abs, left = refs[len(slab):]
        here = place_ref[0]

        @pl.when(pl.program_id(0) == 0)
        def _():
            core = lax.rem(here, 2)
            gram[pl.ds(pl.multiple_of(core * half, half), half), :] = mine_ref[...]
            gram[pl.ds(pl.multiple_of((1 - core) * half, half), half), :] = other_ref[...]
            left_abs[...] = jnp.dot(gram[...], grads_ref[...], preferred_element_type=F32).astype(BF16)
            order = []
            for block in blocks:
                row = pl.multiple_of(shard_of(here, block, planes) * shard, shard)
                order.append(left_abs[pl.ds(row, shard), :])
            left[...] = jnp.concatenate(order, 0).T

        part = jnp.concatenate([s[...] for s in slabs], 0)
        out_ref[...] = factor_ref[...] + jnp.dot(left[...], part, preferred_element_type=F32) * scale

    vmem = pl.BlockSpec(memory_space=pltpu.VMEM)
    return pl.pallas_call(
        body,
        grid=(columns // chunk,),
        in_specs=[pl.BlockSpec(memory_space=pltpu.SMEM)]
        + [pl.BlockSpec((s.shape[0], chunk), lambda j: (0, j)) for s in slab]
        + [vmem, vmem, vmem, pl.BlockSpec((rows, chunk), lambda j: (0, j))],
        out_specs=pl.BlockSpec((rows, chunk), lambda j: (0, j)),
        scratch_shapes=[
            pltpu.VMEM((tokens, tokens), BF16), pltpu.VMEM((tokens, rows), BF16), pltpu.VMEM((rows, tokens), BF16)
        ],
        out_shape=jax.ShapeDtypeStruct((rows, columns), F32),
        compiler_params=pltpu.CompilerParams(vmem_limit_bytes=48 * MIB),
        cost_estimate=pl.CostEstimate(
            flops=2 * rows * tokens * (columns + tokens), bytes_accessed=8 * rows * columns, transcendentals=0
        ),
    )(place, *slab, *halves, grads, output_factor)


def by_owner(grads, place, earlier, n):
    rows, columns = grads.shape
    width = columns // n

    def body(place_ref, grads_ref, *refs):
        del place_ref
        out = refs[-1]
        for i in range(n):
            out[i * rows:(i + 1) * rows, :] = grads_ref[:, i * width:(i + 1) * width]

    return call(
        body, place, [grads, *earlier], [((n * rows, width), grads.dtype)], far=tuple(range(1, 1 + len(earlier)))
    )[0]


def per_device(inputs, input_factor, out_grads, output_factor):
    n = lax.axis_size("row")
    planes = n // 4
    half = planes // 2
    place = lax.axis_index("row").reshape(1)
    near = sorted((k for k in range(1, planes) if k != half), key=lambda k: min(k, planes - k))
    groups = [[0], near, [half]]
    slab = out_grads[:, : output_factor.shape[1]]

    def across(value):
        return permute(value, y_perm(n))

    def other_core(value):
        return permute(value, core_perm(n))

    def ahead(value, k):
        return permute(value, plane_perm(n, k))

    send = messages(inputs, place, planes)
    got = {k: ahead(send[k], k) for k in near}
    crossed_0, slab_crossed_0 = across(send[0]), across(slab)

    first = [got[k] for k in near]
    count = len(near)
    near_send, far_send, pair_0 = pack(
        place, [*first, send[half], send[0], crossed_0, slab_crossed_0],
        [list(range(count)), [count], [count + 1, count + 2]],
    )
    got[half] = ahead(far_send, half)
    crossed_near = across(near_send)
    pair_0_other = other_core(pair_0)

    far_cross, pair_near, slab_send = pack(
        place, [got[half], near_send, crossed_near, slab, pair_0_other], [[0], [1, 2], [3]]
    )
    crossed_far = across(far_cross)
    pair_near_other = other_core(pair_near)
    slab_got = [ahead(slab_send, k) for k in near]

    pair_far, slab_near, slab_far_send = pack(
        place, [far_cross, crossed_far, *slab_got, slab_send, pair_near_other],
        [[0, 1], list(range(2, 2 + count)), [2 + count]],
    )
    pair_far_other = other_core(pair_far)
    slab_far = ahead(slab_far_send, half)
    slab_crossed_near = across(slab_near)
    grads = by_owner(out_grads, place, [far_cross], n)
    own_grads = lax.all_to_all(grads, "row", split_axis=0, concat_axis=0, tiled=True)

    pieces = [pair_0, pair_0_other, pair_near, pair_near_other, pair_far, pair_far_other]
    mine, other = gram_part(pieces, groups, input_factor, place, planes)

    mine, other = add_split(mine, other_core(other), place, 2, [])
    slab_crossed_far = across(slab_far)
    mine, low = add(mine, across(other), place)
    step = 4
    while step < n:
        mine, low = add(mine, permute(low, [(i, i ^ step) for i in range(n)]), place)
        step *= 2
    *slabs, low = pack(
        place, [slab, slab_crossed_0, slab_near, slab_crossed_near, slab_far, slab_crossed_far, low],
        [[0, 1], [2, 3], [4, 5], [6]],
    )
    slabs = sum(([s, other_core(s)] for s in slabs), [])
    low = join(low, across(low), place, 2)
    return update(
        slabs, token_blocks(groups), [low, other_core(low)], own_grads, output_factor, place, planes
    )


def solution(mesh):
    spec = P(("groups", "row"), None)
    return jax.shard_map(per_device, mesh=mesh, in_specs=(spec,) * 4, out_specs=spec, check_vma=False)
```

time: 273 us -> 149 us (0.55)
  waiting for transfers between devices: 223 us -> 95.2 us
  Pallas kernels: 0 us -> 26 us
  matrix products: 25.4 us -> 0 us
  starting transfers between devices: 7.47 us -> 25.9 us
  between operations: 13.1 us -> 0.12 us
    all_gather x2 -> x0, waiting for transfers between devices: 127 us -> none  [the longest x1 87.8 us: per_device(): whole = lax.all_gather(inputs, 'row', axis=0, tiled=True)]
    psum x1 -> x0, waiting for transfers between devices: 95.3 us -> none  [per_device(): gram = (lax.psum(partial_value, 'row') * factor).astype(jnp.bfloat16)]
    ppermute x0 -> x24, waiting for transfers between devices: none -> 95.2 us  [permute(): return lax.ppermute(value, 'row', perm)]
    pallas_call x0 -> x13, Pallas kernels: none -> 26 us  [the longest x1 14.9 us: update(): pl.pallas_call(body, grid=(columns // chunk,), in_specs=[pl.BlockSpec(mem...]
    dot_general x2 -> x0, matrix products: 25.4 us -> none  [the longest x1 13.6 us: per_device(): update = jnp.dot(left, slab_all, preferred_element_type=jnp.float32)]
    ppermute x0 -> x24, starting transfers between devices: none -> 21.7 us  [permute(): return lax.ppermute(value, 'row', perm)]
    all_to_all x1, starting transfers between devices: 7.39 us -> 4.15 us  [per_device(): lax.all_to_all(grads, 'row', split_axis=0, concat_axis=0, tiled=True)]
  transfers between devices with their start and end apart: 4 -> 25, of which waited for: 3 -> 11; matrix products, arithmetic and copies ran while one was open for 6% -> 1% of each run, Pallas kernels for 0% -> 2%
where the time goes in v2:
time: 149 us
  waiting for transfers between devices  95.2 us (64%)
  Pallas kernels  26 us (17%)
  starting transfers between devices  25.9 us (17%)
  local copies, waits for them, and re-layouts  2.01 us (1%)
    ppermute x24, waiting for transfers between devices, permute(): return lax.ppermute(value, 'row', perm)  95.2 us
    ppermute x24, starting transfers between devices, permute(): return lax.ppermute(value, 'row', perm)  21.7 us
    pallas_call x1, Pallas kernels, update(): pl.pallas_call(body, grid=(columns // chunk,), in_specs=[pl.BlockSpec(mem...  14.9 us
    pallas_call x12, Pallas kernels, call(): pl.pallas_call(body, in_specs=[pl.BlockSpec(memory_space=pltpu.SMEM)] + [...  11.1 us
    all_to_all x1, starting transfers between devices, per_device(): lax.all_to_all(grads, 'row', split_axis=0, concat_axis=0, tiled=True)  4.15 us
  transfers between devices with their start and end apart: 25, of which 11 were waited for; matrix products, arithmetic and copies ran while one was open for 1% of the time, Pallas kernels for 2%

profile of v2, /device:TPU:0, one launch (start us, length us, event | category | flops | bytes accessed | tf_op | source)
XLA Modules:
  0.0 149.1 jit_solution(4784062493392075263)
XLA Ops:
  0.0 0.0 copy-start.1
  0.0 1.0 copy-done.1
  1.0 0.1 shard_map.46
  1.1 3.1 %collective-permute-start.1 = (bf16[32,6144]{1,0:T(8,128)(2,1)S(1)}, bf16[32,6144]{1,0:T(8,128)(2,1)S(1)}, u32[]{:S(2)}, u32[]{:S(2)}) collective-permute-start(bf16[32,6144]{1,0:T(8,128)(2,1)S(1)} %get-tuple-element.31), channel_id=1, source_target_pairs={{0,4},{1,5},{2,6},{3,7},{4,8},{5,9},{6,10},{7,11},{8,12},{9,13},{1... | collective-permute-start | bytes 1179656 | tf_op jit(solution)/shard_map/ppermute | solution.py:16
  4.2 2.1 %collective-permute-start.2 = (bf16[32,6144]{1,0:T(8,128)(2,1)S(1)}, bf16[32,6144]{1,0:T(8,128)(2,1)S(1)}, u32[]{:S(2)}, u32[]{:S(2)}) collective-permute-start(bf16[32,6144]{1,0:T(8,128)(2,1)S(1)} %get-tuple-element.32), channel_id=1, source_target_pairs={{0,12},{1,13},{2,14},{3,15},{4,0},{5,1},{6,2},{7,3},{8,4},{9,5},{1... | collective-permute-start | bytes 1179656 | tf_op jit(solution)/shard_map/ppermute | solution.py:16
  6.3 1.7 %collective-permute-start.3 = (bf16[32,6144]{1,0:T(8,128)(2,1)S(1)}, bf16[32,6144]{1,0:T(8,128)(2,1)S(1)}, u32[]{:S(2)}, u32[]{:S(2)}) collective-permute-start(bf16[32,6144]{1,0:T(8,128)(2,1)S(1)} %get-tuple-element.34.refs_3_), channel_id=1, source_target_pairs={{0,2},{1,3},{2,0},{3,1},{4,6},{5,7},{6,4},{7,5},{8,10},{9,11},{10,... | collective-permute-start | bytes 1179656 | tf_op jit(solution)/shard_map/ppermute | solution.py:16
  8.0 1.0 slice.3.refs_3_.refs_0_
  9.0 0.4 collective-permute-start
  9.4 13.1 %collective-permute-done.refs_5_.refs_1_ = bf16[32,4096]{1,0:T(8,128)(2,1)S(1)} collective-permute-done((bf16[32,4096]{1,0:T(8,128)(2,1)S(1)}, bf16[32,4096]{1,0:T(8,128)(2,1)S(1)}, u32[]{:S(2)}, u32[]{:S(2)}) %collective-permute-start) | collective-permute-done | bytes 262176 | tf_op jit(solution)/shard_map/ppermute | solution.py:16
  22.5 0.0 collective-permute-done.1.refs_0_
  22.5 0.7 collective-permute-done.2.refs_1_
  23.2 0.0 collective-permute-done.3.refs_4_
  23.2 0.1 shard_map.47
  23.4 1.6 %collective-permute-start.5 = (bf16[64,6144]{1,0:T(8,128)(2,1)S(1)}, bf16[64,6144]{1,0:T(8,128)(2,1)S(1)}, u32[]{:S(2)}, u32[]{:S(2)}) collective-permute-start(bf16[64,6144]{1,0:T(8,128)(2,1)S(1)} %get-tuple-element.36.refs_1_), channel_id=1, source_target_pairs={{0,2},{1,3},{2,0},{3,1},{4,6},{5,7},{6,4},{7,5},{8,10},{9,11},{10,... | collective-permute-start | bytes 2359304 | tf_op jit(solution)/shard_map/ppermute | solution.py:16
  24.9 0.0 collective-permute-start.6
  24.9 1.3 collective-permute-start.4
  26.2 19.6 %collective-permute-done.4.refs_0_ = bf16[32,6144]{1,0:T(8,128)(2,1)S(1)} collective-permute-done((bf16[32,6144]{1,0:T(8,128)(2,1)S(1)}, bf16[32,6144]{1,0:T(8,128)(2,1)S(1)}, u32[]{:S(2)}, u32[]{:S(2)}) %collective-permute-start.4) | collective-permute-done | bytes 393248 | tf_op jit(solution)/shard_map/ppermute | solution.py:16
  45.8 0.0 collective-permute-done.5.refs_2_
  45.8 0.0 collective-permute-done.6.refs_4_.refs_1_
  45.8 0.1 shard_map.48
  46.0 0.1 collective-permute-start.10
  46.0 0.6 collective-permute-start.7
  46.6 2.2 %collective-permute-start.9 = (bf16[32,4096]{1,0:T(8,128)(2,1)S(1)}, bf16[32,4096]{1,0:T(8,128)(2,1)S(1)}, u32[]{:S(2)}, u32[]{:S(2)}) collective-permute-start(bf16[32,4096]{1,0:T(8,128)(2,1)S(1)} %get-tuple-element.39.refs_4_), channel_id=1, source_target_pairs={{0,12},{1,13},{2,14},{3,15},{4,0},{5,1},{6,2},{7,3},{8,4},{9,5},{1... | collective-permute-start | bytes 786440 | tf_op jit(solution)/shard_map/ppermute | solution.py:16
  48.8 0.0 collective-permute-start.8
  48.8 6.7 %collective-permute-done.9.refs_3_ = bf16[32,4096]{1,0:T(8,128)(2,1)S(1)} collective-permute-done((bf16[32,4096]{1,0:T(8,128)(2,1)S(1)}, bf16[32,4096]{1,0:T(8,128)(2,1)S(1)}, u32[]{:S(2)}, u32[]{:S(2)}) %collective-permute-start.9) | collective-permute-done | bytes 262176 | tf_op jit(solution)/shard_map/ppermute | solution.py:16
  55.5 5.5 %collective-permute-done.8.refs_2_ = bf16[32,4096]{1,0:T(8,128)(2,1)S(1)} collective-permute-done((bf16[32,4096]{1,0:T(8,128)(2,1)S(1)}, bf16[32,4096]{1,0:T(8,128)(2,1)S(1)}, u32[]{:S(2)}, u32[]{:S(2)}) %collective-permute-start.8) | collective-permute-done | bytes 262176 | tf_op jit(solution)/shard_map/ppermute | solution.py:16
  61.1 0.0 collective-permute-done.7.refs_1_
  61.1 0.0 collective-permute-done.10.refs_5_.refs_3_
  61.1 0.1 shard_map.49
  61.2 0.1 collective-permute-start.14
  61.3 2.3 %collective-permute-done.14.refs_5_ = bf16[64,6144]{1,0:T(8,128)(2,1)S(1)} collective-permute-done((bf16[64,6144]{1,0:T(8,128)(2,1)S(1)}, bf16[64,6144]{1,0:T(8,128)(2,1)S(1)}, u32[]{:S(2)}, u32[]{:S(2)}) %collective-permute-start.14) | collective-permute-done | bytes 786464 | tf_op jit(solution)/shard_map/ppermute | solution.py:16
  63.5 7.5 %shard_map.50 = (f32[256,512]{1,0:T(8,128)S(1)}, f32[256,512]{1,0:T(8,128)}) custom-call(s32[1]{0:T(128)} %bitcast.place_ref, bf16[64,6144]{1,0:T(8,128)(2,1)S(1)} %get-tuple-element.37.refs_0_, bf16[64,6144]{1,0:T(8,128)(2,1)S(1)} %collective-permute-done.6.refs_4_.refs_1_, bf16[128,6144]{1,0:T(8,128)(2,1)S(1)} %get-tuple-element.40.refs_2_, ...), custom_call_target="tpu_custom_call" | custom-call | flops 3489660928 | bytes 6291456 | tf_op jit(solution)/shard_map/pallas_call | solution.py:34
  71.1 0.2 collective-permute-start.15
  71.3 0.0 copy-done
  71.3 1.0 shard_map.57
  72.3 4.1 %all-to-all-start = ((bf16[16,32,1024]{2,1,0:T(8,128)(2,1)}), bf16[16,32,1024]{2,1,0:T(8,128)(2,1)S(1)}, u32[]{:S(2)}, u32[]{:S(2)}) async-start(bf16[16,32,1024]{2,1,0:T(8,128)(2,1)} %bitcast.1), calls=%async_computation | async-start | bytes 2097152 | tf_op jit(solution)/shard_map/all_to_all | solution.py:296
  76.5 2.8 %collective-permute-start.12 = (bf16[32,4096]{1,0:T(8,128)(2,1)S(1)}, bf16[32,4096]{1,0:T(8,128)(2,1)S(1)}, u32[]{:S(2)}, u32[]{:S(2)}) collective-permute-start(bf16[32,4096]{1,0:T(8,128)(2,1)S(1)} %get-tuple-element.42), channel_id=1, source_target_pairs={{0,8},{1,9},{2,10},{3,11},{4,12},{5,13},{6,14},{7,15},{8,0},{9,1},... | collective-permute-start | bytes 786440 | tf_op jit(solution)/shard_map/ppermute | solution.py:16
  79.3 1.5 collective-permute-start.11
  80.8 0.0 collective-permute-done.15.other_ref
  80.8 0.1 shard_map.51
  80.9 0.6 collective-permute-start.16
  81.5 23.0 %collective-permute-done.16.other_ref = bf16[128,512]{1,0:T(8,128)(2,1)S(1)} collective-permute-done((bf16[128,512]{1,0:T(8,128)(2,1)S(1)}, bf16[128,512]{1,0:T(8,128)(2,1)S(1)}, u32[]{:S(2)}, u32[]{:S(2)}) %collective-permute-start.16) | collective-permute-done | bytes 131104 | tf_op jit(solution)/shard_map/ppermute | solution.py:16
  104.5 0.5 collective-permute-start.17
  105.1 9.3 %collective-permute-done.12.refs_4_ = bf16[32,4096]{1,0:T(8,128)(2,1)S(1)} collective-permute-done((bf16[32,4096]{1,0:T(8,128)(2,1)S(1)}, bf16[32,4096]{1,0:T(8,128)(2,1)S(1)}, u32[]{:S(2)}, u32[]{:S(2)}) %collective-permute-start.12) | collective-permute-done | bytes 262176 | tf_op jit(solution)/shard_map/ppermute | solution.py:16
  114.4 1.4 collective-permute-start.13
  115.8 0.0 collective-permute-done.17.other_ref
  115.8 1.0 collective-permute-start.18
  116.8 7.6 %collective-permute-done.18.other_ref = bf16[128,512]{1,0:T(8,128)(2,1)S(1)} collective-permute-done((bf16[128,512]{1,0:T(8,128)(2,1)S(1)}, bf16[128,512]{1,0:T(8,128)(2,1)S(1)}, u32[]{:S(2)}, u32[]{:S(2)}) %collective-permute-start.18) | collective-permute-done | bytes 131104 | tf_op jit(solution)/shard_map/ppermute | solution.py:16
  124.3 0.7 shard_map.54
  125.1 0.0 collective-permute-done.13.refs_5_
  125.1 0.0 collective-permute-done.11.refs_3_
  125.1 1.1 shard_map.55
  126.2 0.0 collective-permute-start.20
  126.2 0.5 collective-permute-start.19
  126.7 0.0 collective-permute-start.21
  126.7 0.1 collective-permute-start.22
  126.8 5.8 %collective-permute-done.22.other_ref = bf16[128,512]{1,0:T(8,128)(2,1)S(1)} collective-permute-done((bf16[128,512]{1,0:T(8,128)(2,1)S(1)}, bf16[128,512]{1,0:T(8,128)(2,1)S(1)}, u32[]{:S(2)}, u32[]{:S(2)}) %collective-permute-start.22) | collective-permute-done | bytes 131104 | tf_op jit(solution)/shard_map/ppermute | solution.py:16
  132.6 0.1 collective-permute-start.23
  132.7 0.0 all-to-all-done
  132.7 1.5 %collective-permute-done.23.refs_7_ = bf16[256,512]{1,0:T(8,128)(2,1)S(1)} collective-permute-done((bf16[256,512]{1,0:T(8,128)(2,1)S(1)}, bf16[256,512]{1,0:T(8,128)(2,1)S(1)}, u32[]{:S(2)}, u32[]{:S(2)}) %collective-permute-start.23) | collective-permute-done | bytes 262176 | tf_op jit(solution)/shard_map/ppermute | solution.py:16
  134.2 0.0 collective-permute-done.19.refs_1_
  134.2 0.0 collective-permute-done.21.refs_5_
  134.2 0.0 collective-permute-done.20.refs_3_
  134.2 14.9 %shard_map.58 = f32[1024,4096]{1,0:T(8,128)} custom-call(s32[1]{0:T(128)} %bitcast.place_ref, bf16[64,4096]{1,0:T(8,128)(2,1)} %get-tuple-element.53.refs_0_, bf16[64,4096]{1,0:T(8,128)(2,1)S(1)} %collective-permute-done.19.refs_1_, bf16[128,4096]{1,0:T(8,128)(2,1)S(1)} %get-tuple-element.54.refs_2_, bf16[128,4096]{1,0:T(8,128)(2,1)} %collective-permute-done.20.refs_3_, ...), custom_call_target="tpu_custom_call" | custom-call | flops 4831838208 | bytes 33554432 | tf_op jit(solution)/shard_map/pallas_call | solution.py:216
  (4 shorter events, 0.1 us)
Async XLA Ops:
  0.0 1.0 copy-start.1
  1.1 21.4 %collective-permute-start.1 = (bf16[32,6144]{1,0:T(8,128)(2,1)S(1)}, bf16[32,6144]{1,0:T(8,128)(2,1)S(1)}, u32[]{:S(2)}, u32[]{:S(2)}) collective-permute-start(bf16[32,6144]{1,0:T(8,128)(2,1)S(1)} %get-tuple-element.31), channel_id=1, source_target_pairs={{0,4},{1,5},{2,6},{3,7},{4,8},{5,9},{6,10},{7,11},{8,12},{9,13},{1... | collective-permute-start | bytes 1179656 | tf_op jit(solution)/shard_map/ppermute | solution.py:16
  4.2 19.0 %collective-permute-start.2 = (bf16[32,6144]{1,0:T(8,128)(2,1)S(1)}, bf16[32,6144]{1,0:T(8,128)(2,1)S(1)}, u32[]{:S(2)}, u32[]{:S(2)}) collective-permute-start(bf16[32,6144]{1,0:T(8,128)(2,1)S(1)} %get-tuple-element.32), channel_id=1, source_target_pairs={{0,12},{1,13},{2,14},{3,15},{4,0},{5,1},{6,2},{7,3},{8,4},{9,5},{1... | collective-permute-start | bytes 1179656 | tf_op jit(solution)/shard_map/ppermute | solution.py:16
  6.3 16.9 %collective-permute-start.3 = (bf16[32,6144]{1,0:T(8,128)(2,1)S(1)}, bf16[32,6144]{1,0:T(8,128)(2,1)S(1)}, u32[]{:S(2)}, u32[]{:S(2)}) collective-permute-start(bf16[32,6144]{1,0:T(8,128)(2,1)S(1)} %get-tuple-element.34.refs_3_), channel_id=1, source_target_pairs={{0,2},{1,3},{2,0},{3,1},{4,6},{5,7},{6,4},{7,5},{8,10},{9,11},{10,... | collective-permute-start | bytes 1179656 | tf_op jit(solution)/shard_map/ppermute | solution.py:16
  9.0 13.5 %collective-permute-start = (bf16[32,4096]{1,0:T(8,128)(2,1)S(1)}, bf16[32,4096]{1,0:T(8,128)(2,1)S(1)}, u32[]{:S(2)}, u32[]{:S(2)}) collective-permute-start(bf16[32,4096]{1,0:T(8,128)(2,1)S(1)} %slice.3.refs_3_.refs_0_), channel_id=1, source_target_pairs={{0,2},{1,3},{2,0},{3,1},{4,6},{5,7},{6,4},{7,5},{8,10},{9,11},{10,... | collective-permute-start | bytes 786440 | tf_op jit(solution)/shard_map/ppermute | solution.py:16
  23.4 22.4 %collective-permute-start.5 = (bf16[64,6144]{1,0:T(8,128)(2,1)S(1)}, bf16[64,6144]{1,0:T(8,128)(2,1)S(1)}, u32[]{:S(2)}, u32[]{:S(2)}) collective-permute-start(bf16[64,6144]{1,0:T(8,128)(2,1)S(1)} %get-tuple-element.36.refs_1_), channel_id=1, source_target_pairs={{0,2},{1,3},{2,0},{3,1},{4,6},{5,7},{6,4},{7,5},{8,10},{9,11},{10,... | collective-permute-start | bytes 2359304 | tf_op jit(solution)/shard_map/ppermute | solution.py:16
  24.9 20.9 %collective-permute-start.6 = (bf16[64,6144]{1,0:T(8,128)(2,1)S(1)}, bf16[64,6144]{1,0:T(8,128)(2,1)S(1)}, u32[]{:S(2)}, u32[]{:S(2)}) collective-permute-start(bf16[64,6144]{1,0:T(8,128)(2,1)S(1)} %get-tuple-element.37.refs_0_), channel_id=1, source_target_pairs={{0,1},{1,0},{2,3},{3,2},{4,5},{5,4},{6,7},{7,6},{8,9},{9,8},{10,11... | collective-permute-start | bytes 2359304 | tf_op jit(solution)/shard_map/ppermute | solution.py:16
  24.9 20.9 %collective-permute-start.4 = (bf16[32,6144]{1,0:T(8,128)(2,1)S(1)}, bf16[32,6144]{1,0:T(8,128)(2,1)S(1)}, u32[]{:S(2)}, u32[]{:S(2)}) collective-permute-start(bf16[32,6144]{1,0:T(8,128)(2,1)S(1)} %get-tuple-element.35), channel_id=1, source_target_pairs={{0,8},{1,9},{2,10},{3,11},{4,12},{5,13},{6,14},{7,15},{8,0},{9,1},... | collective-permute-start | bytes 1179656 | tf_op jit(solution)/shard_map/ppermute | solution.py:16
  46.0 15.1 %collective-permute-start.10 = (bf16[128,6144]{1,0:T(8,128)(2,1)S(1)}, bf16[128,6144]{1,0:T(8,128)(2,1)S(1)}, u32[]{:S(2)}, u32[]{:S(2)}) collective-permute-start(bf16[128,6144]{1,0:T(8,128)(2,1)S(1)} %get-tuple-element.40.refs_2_), channel_id=1, source_target_pairs={{0,1},{1,0},{2,3},{3,2},{4,5},{5,4},{6,7},{7,6},{8,9},{9,8},{10,11... | collective-permute-start | bytes 4718600 | tf_op jit(solution)/shard_map/ppermute | solution.py:16
  46.0 15.0 %collective-permute-start.7 = (bf16[32,6144]{1,0:T(8,128)(2,1)S(1)}, bf16[32,6144]{1,0:T(8,128)(2,1)S(1)}, u32[]{:S(2)}, u32[]{:S(2)}) collective-permute-start(bf16[32,6144]{1,0:T(8,128)(2,1)S(1)} %get-tuple-element.38.refs_0_), channel_id=1, source_target_pairs={{0,2},{1,3},{2,0},{3,1},{4,6},{5,7},{6,4},{7,5},{8,10},{9,11},{10,... | collective-permute-start | bytes 1179656 | tf_op jit(solution)/shard_map/ppermute | solution.py:16
  46.6 24.7 %copy-start = (bf16[32,16384]{1,0:T(8,128)(2,1)S(1)}, bf16[32,16384]{1,0:T(8,128)(2,1)}, u32[]{:S(2)}) copy-start(bf16[32,16384]{1,0:T(8,128)(2,1)} %grads_ref.1) | copy-start | bytes 3145732
  46.6 8.9 %collective-permute-start.9 = (bf16[32,4096]{1,0:T(8,128)(2,1)S(1)}, bf16[32,4096]{1,0:T(8,128)(2,1)S(1)}, u32[]{:S(2)}, u32[]{:S(2)}) collective-permute-start(bf16[32,4096]{1,0:T(8,128)(2,1)S(1)} %get-tuple-element.39.refs_4_), channel_id=1, source_target_pairs={{0,12},{1,13},{2,14},{3,15},{4,0},{5,1},{6,2},{7,3},{8,4},{9,5},{1... | collective-permute-start | bytes 786440 | tf_op jit(solution)/shard_map/ppermute | solution.py:16
  48.8 12.3 %collective-permute-start.8 = (bf16[32,4096]{1,0:T(8,128)(2,1)S(1)}, bf16[32,4096]{1,0:T(8,128)(2,1)S(1)}, u32[]{:S(2)}, u32[]{:S(2)}) collective-permute-start(bf16[32,4096]{1,0:T(8,128)(2,1)S(1)} %get-tuple-element.39.refs_4_), channel_id=1, source_target_pairs={{0,4},{1,5},{2,6},{3,7},{4,8},{5,9},{6,10},{7,11},{8,12},{9,13},{1... | collective-permute-start | bytes 786440 | tf_op jit(solution)/shard_map/ppermute | solution.py:16
  61.2 2.4 %collective-permute-start.14 = (bf16[64,6144]{1,0:T(8,128)(2,1)S(1)}, bf16[64,6144]{1,0:T(8,128)(2,1)S(1)}, u32[]{:S(2)}, u32[]{:S(2)}) collective-permute-start(bf16[64,6144]{1,0:T(8,128)(2,1)S(1)} %get-tuple-element.43.refs_4_), channel_id=1, source_target_pairs={{0,1},{1,0},{2,3},{3,2},{4,5},{5,4},{6,7},{7,6},{8,9},{9,8},{10,11... | collective-permute-start | bytes 2359304 | tf_op jit(solution)/shard_map/ppermute | solution.py:16
  71.1 9.7 %collective-permute-start.15 = (f32[256,512]{1,0:T(8,128)}, f32[256,512]{1,0:T(8,128)S(1)}, u32[]{:S(2)}, u32[]{:S(2)}) collective-permute-start(f32[256,512]{1,0:T(8,128)} %get-tuple-element.45), channel_id=1, source_target_pairs={{0,1},{1,0},{2,3},{3,2},{4,5},{5,4},{6,7},{7,6},{8,9},{9,8},{10,11... | collective-permute-start | bytes 1572872 | tf_op jit(solution)/shard_map/ppermute | solution.py:16
  72.3 60.4 %all-to-all-start = ((bf16[16,32,1024]{2,1,0:T(8,128)(2,1)}), bf16[16,32,1024]{2,1,0:T(8,128)(2,1)S(1)}, u32[]{:S(2)}, u32[]{:S(2)}) async-start(bf16[16,32,1024]{2,1,0:T(8,128)(2,1)} %bitcast.1), calls=%async_computation | async-start | bytes 2097152 | tf_op jit(solution)/shard_map/all_to_all | solution.py:296
  76.5 37.9 %collective-permute-start.12 = (bf16[32,4096]{1,0:T(8,128)(2,1)S(1)}, bf16[32,4096]{1,0:T(8,128)(2,1)S(1)}, u32[]{:S(2)}, u32[]{:S(2)}) collective-permute-start(bf16[32,4096]{1,0:T(8,128)(2,1)S(1)} %get-tuple-element.42), channel_id=1, source_target_pairs={{0,8},{1,9},{2,10},{3,11},{4,12},{5,13},{6,14},{7,15},{8,0},{9,1},... | collective-permute-start | bytes 786440 | tf_op jit(solution)/shard_map/ppermute | solution.py:16
  79.3 45.7 %collective-permute-start.11 = (bf16[64,4096]{1,0:T(8,128)(2,1)S(1)}, bf16[64,4096]{1,0:T(8,128)(2,1)S(1)}, u32[]{:S(2)}, u32[]{:S(2)}) collective-permute-start(bf16[64,4096]{1,0:T(8,128)(2,1)S(1)} %get-tuple-element.41.refs_2_), channel_id=1, source_target_pairs={{0,2},{1,3},{2,0},{3,1},{4,6},{5,7},{6,4},{7,5},{8,10},{9,11},{10,... | collective-permute-start | bytes 1572872 | tf_op jit(solution)/shard_map/ppermute | solution.py:16
  80.9 23.6 %collective-permute-start.16 = (bf16[128,512]{1,0:T(8,128)(2,1)S(1)}, bf16[128,512]{1,0:T(8,128)(2,1)S(1)}, u32[]{:S(2)}, u32[]{:S(2)}) collective-permute-start(bf16[128,512]{1,0:T(8,128)(2,1)S(1)} %get-tuple-element.47), channel_id=1, source_target_pairs={{0,2},{1,3},{2,0},{3,1},{4,6},{5,7},{6,4},{7,5},{8,10},{9,11},{10,... | collective-permute-start | bytes 393224 | tf_op jit(solution)/shard_map/ppermute | solution.py:16
  104.5 11.2 %collective-permute-start.17 = (bf16[128,512]{1,0:T(8,128)(2,1)S(1)}, bf16[128,512]{1,0:T(8,128)(2,1)S(1)}, u32[]{:S(2)}, u32[]{:S(2)}) collective-permute-start(bf16[128,512]{1,0:T(8,128)(2,1)S(1)} %get-tuple-element.49), channel_id=1, source_target_pairs={{0,4},{1,5},{2,6},{3,7},{4,0},{5,1},{6,2},{7,3},{8,12},{9,13},{10,... | collective-permute-start | bytes 393224 | tf_op jit(solution)/shard_map/ppermute | solution.py:16
  114.4 10.7 %collective-permute-start.13 = (bf16[32,4096]{1,0:T(8,128)(2,1)S(1)}, bf16[32,4096]{1,0:T(8,128)(2,1)S(1)}, u32[]{:S(2)}, u32[]{:S(2)}) collective-permute-start(bf16[32,4096]{1,0:T(8,128)(2,1)S(1)} %collective-permute-done.12.refs_4_), channel_id=1, source_target_pairs={{0,2},{1,3},{2,0},{3,1},{4,6},{5,7},{6,4},{7,5},{8,10},{9,11},{10,... | collective-permute-start | bytes 786440 | tf_op jit(solution)/shard_map/ppermute | solution.py:16
  115.8 8.5 %collective-permute-start.18 = (bf16[128,512]{1,0:T(8,128)(2,1)S(1)}, bf16[128,512]{1,0:T(8,128)(2,1)S(1)}, u32[]{:S(2)}, u32[]{:S(2)}) collective-permute-start(bf16[128,512]{1,0:T(8,128)(2,1)S(1)} %get-tuple-element.51), channel_id=1, source_target_pairs={{0,8},{1,9},{2,10},{3,11},{4,12},{5,13},{6,14},{7,15},{8,0},{9,1},... | collective-permute-start | bytes 393224 | tf_op jit(solution)/shard_map/ppermute | solution.py:16
  126.2 8.1 %collective-permute-start.20 = (bf16[128,4096]{1,0:T(8,128)(2,1)S(1)}, bf16[128,4096]{1,0:T(8,128)(2,1)}, u32[]{:S(2)}, u32[]{:S(2)}) collective-permute-start(bf16[128,4096]{1,0:T(8,128)(2,1)S(1)} %get-tuple-element.54.refs_2_), channel_id=1, source_target_pairs={{0,1},{1,0},{2,3},{3,2},{4,5},{5,4},{6,7},{7,6},{8,9},{9,8},{10,11... | collective-permute-start | bytes 3145736 | tf_op jit(solution)/shard_map/ppermute | solution.py:16
  126.2 8.1 %collective-permute-start.19 = (bf16[64,4096]{1,0:T(8,128)(2,1)}, bf16[64,4096]{1,0:T(8,128)(2,1)S(1)}, u32[]{:S(2)}, u32[]{:S(2)}) collective-permute-start(bf16[64,4096]{1,0:T(8,128)(2,1)} %get-tuple-element.53.refs_0_), channel_id=1, source_target_pairs={{0,1},{1,0},{2,3},{3,2},{4,5},{5,4},{6,7},{7,6},{8,9},{9,8},{10,11... | collective-permute-start | bytes 1572872 | tf_op jit(solution)/shard_map/ppermute | solution.py:16
  126.7 7.6 %collective-permute-start.21 = (bf16[64,4096]{1,0:T(8,128)(2,1)}, bf16[64,4096]{1,0:T(8,128)(2,1)}, u32[]{:S(2)}, u32[]{:S(2)}) collective-permute-start(bf16[64,4096]{1,0:T(8,128)(2,1)} %get-tuple-element.55.refs_4_), channel_id=1, source_target_pairs={{0,1},{1,0},{2,3},{3,2},{4,5},{5,4},{6,7},{7,6},{8,9},{9,8},{10,11... | collective-permute-start | bytes 1572872 | tf_op jit(solution)/shard_map/ppermute | solution.py:16
  126.7 5.9 %collective-permute-start.22 = (bf16[128,512]{1,0:T(8,128)(2,1)S(1)}, bf16[128,512]{1,0:T(8,128)(2,1)S(1)}, u32[]{:S(2)}, u32[]{:S(2)}) collective-permute-start(bf16[128,512]{1,0:T(8,128)(2,1)S(1)} %get-tuple-element.56.mine_ref), channel_id=1, source_target_pairs={{0,2},{1,3},{2,0},{3,1},{4,6},{5,7},{6,4},{7,5},{8,10},{9,11},{10,... | collective-permute-start | bytes 393224 | tf_op jit(solution)/shard_map/ppermute | solution.py:16
  132.6 1.6 %collective-permute-start.23 = (bf16[256,512]{1,0:T(8,128)(2,1)S(1)}, bf16[256,512]{1,0:T(8,128)(2,1)S(1)}, u32[]{:S(2)}, u32[]{:S(2)}) collective-permute-start(bf16[256,512]{1,0:T(8,128)(2,1)S(1)} %shard_map.56.refs_6_), channel_id=1, source_target_pairs={{0,1},{1,0},{2,3},{3,2},{4,5},{5,4},{6,7},{7,6},{8,9},{9,8},{10,11... | collective-permute-start | bytes 786440 | tf_op jit(solution)/shard_map/ppermute | solution.py:16

commit v3 on v0

v3 whole, which is shorter than its diff:
```python
import enum

import jax
import jax.numpy as jnp
from jax import lax
from jax.experimental import pallas as pl
from jax.experimental.pallas import tpu as pltpu
from jax.sharding import PartitionSpec as P

BF16 = jnp.bfloat16
F32 = jnp.float32
MIB = 1024 * 1024
GRAM_ROWS_VMEM = 44 * MIB
UPDATE_VMEM = 22 * MIB
FETCH = True


class N(enum.Enum):
    near = enum.auto()
    rows = enum.auto()
    factor = enum.auto()
    mine = enum.auto()
    other = enum.auto()
    far = enum.auto()
    out = enum.auto()
    earlier = enum.auto()
    own = enum.auto()
    give = enum.auto()
    x = enum.auto()
    cross = enum.auto()
    grads = enum.auto()
    slab = enum.auto()
    chip = enum.auto()
    pair = enum.auto()
    crossed = enum.auto()
    sent = enum.auto()
    grads_crossed = enum.auto()
    slab_cross = enum.auto()
    send = enum.auto()
    between = enum.auto()
    products = enum.auto()
    late = enum.auto()
    keep = enum.auto()
    low = enum.auto()
    sum = enum.auto()
    grads_cross = enum.auto()
    far_slab = enum.auto()
    early = enum.auto()
    gram = enum.auto()
    slabs = enum.auto()


def permute(value, perm):
    return lax.ppermute(value, "row", perm)


def core_perm(n):
    return [(i, i ^ 1) for i in range(n)]


def y_perm(n):
    return [(i, i ^ 2) for i in range(n)]


def plane_perm(n, step):
    return [(i, (i + 4 * step) % n) for i in range(n)]


def call(body, place, inputs, outputs, scratch=(), limit=4 * MIB, flops=0, bytes_accessed=0, far=()):
    vmem = pl.BlockSpec(memory_space=pltpu.VMEM)
    anywhere = pl.BlockSpec(memory_space=pltpu.HBM)
    names = [*inputs, *outputs]

    def kernel(place_ref, *refs):
        body(place_ref[0], dict(zip(names, refs)), *refs[len(names):])

    results = pl.pallas_call(
        kernel,
        in_specs=[pl.BlockSpec(memory_space=pltpu.SMEM)] + [anywhere if k in far else vmem for k in inputs],
        out_specs=[vmem] * len(outputs),
        out_shape=[jax.ShapeDtypeStruct(shape, dtype) for shape, dtype in outputs.values()],
        scratch_shapes=list(scratch),
        compiler_params=pltpu.CompilerParams(vmem_limit_bytes=limit),
        cost_estimate=pl.CostEstimate(flops=flops, bytes_accessed=bytes_accessed, transcendentals=0),
    )(place, *inputs.values())
    return dict(zip(outputs, results))


def stack(out, refs):
    row = 0
    for ref in refs:
        out[row:row + ref.shape[0], :] = ref[...]
        row += ref.shape[0]


def token_blocks(groups):
    return [(k, y, core) for group in groups for core in (0, 1) for y in (0, 1) for k in group]


def shard_of(place, block, planes):
    back, other_y, other_core = block
    plane = lax.rem(place // 4 + planes - back, planes)
    y, core = lax.rem(place // 2, 2), lax.rem(place, 2)
    return plane * 4 + (1 - y if other_y else y) * 2 + (1 - core if other_core else core)


def half_block(place, planes, other):
    y = lax.rem(place // 2, 2)
    y = 1 - y if other else y
    return jnp.where(place // 4 < planes // 2, y, 1 - y)


def gram_rows(pieces, input_factor, place, planes):
    own, features = input_factor.shape
    width = features // planes
    half = planes // 2
    columns = pieces[0].shape[1]
    tokens = sum(p.shape[0] for p in pieces)
    count = len(pieces)

    def body(here, refs, sems):
        near, acc = refs[N.near], refs[N.rows]
        copies = []
        for j in range(half + 1):
            left = lax.rem(here // 4 + j, planes) * width
            size = width
            if j == half:
                size = width // 2
                left = left + half_block(here, planes, False) * size
            copies.append(
                pltpu.make_async_copy(
                    refs[N.factor].at[:, pl.ds(pl.multiple_of(left, size), size)],
                    near.at[:, j * width:j * width + size], sems.at[j],
                )
            )
            copies[-1].start()
        for j, copy in enumerate(copies):
            copy.wait()
            at = slice(j * width, min((j + 1) * width, columns))
            rows = jnp.concatenate([refs[i][:, at] for i in range(count)], 0)
            part = lax.dot_general(rows, near[:, at], (((1,), (1,)), ((), ())), preferred_element_type=F32)
            acc[...] = part * 0.5 if j == 0 else acc[...] + part

    out = call(
        body, place, {**dict(enumerate(pieces)), N.factor: input_factor},
        {N.rows: ((tokens, own), F32), N.near: ((own, columns), input_factor.dtype)},
        scratch=[pltpu.SemaphoreType.DMA((half + 1,))], limit=GRAM_ROWS_VMEM, far=(N.factor,),
        flops=2 * tokens * own * columns, bytes_accessed=2 * own * columns,
    )
    return out[N.rows], out[N.near]


def gram_part(rows, near, before, after, groups, place, planes, features, earlier):
    own, columns = near.shape
    width = features // planes
    blocks = token_blocks(groups)
    pieces = [*before, *after]
    tokens = sum(p.shape[0] for p in pieces)
    shard = tokens // len(blocks)
    count = len(pieces)
    scale = float(features) ** -0.5

    def body(here, refs, whole, total):
        ins = [refs[i] for i in range(count)]
        last = jnp.concatenate([refs[i][...] for i in range(len(before), count)], 0)
        near = refs[N.near]
        acc = 0.5 * lax.dot_general(
            last[:, :width], near[:, :width], (((1,), (1,)), ((), ())), preferred_element_type=F32
        )
        acc += lax.dot_general(last[:, width:], near[:, width:], (((1,), (1,)), ((), ())), preferred_element_type=F32)
        left = pl.multiple_of(lax.rem(here, 4) * own, own)
        at, first = 0, refs[N.rows].shape[0]
        for piece in ins:
            for low in range(0, piece.shape[0], shard):
                row = pl.multiple_of(shard_of(here, blocks[at // shard], planes) * shard, shard)
                mine = refs[N.rows][at:at + shard, :] if at < first else acc[at - first:at - first + shard, :]
                high = mine.astype(BF16)
                whole[0, pl.ds(row, shard), :] = high
                whole[1, pl.ds(row, shard), :] = (mine - high.astype(F32)).astype(BF16)
                whole[2, pl.ds(row, shard), :] = piece[low:low + shard, pl.ds(left, own)]
                at += shard
        half = lax.dot_general(whole[2], whole[0], (((1,), (1,)), ((), ())), preferred_element_type=F32)
        half += lax.dot_general(whole[2], whole[1], (((1,), (1,)), ((), ())), preferred_element_type=F32)
        total[...] = (half + half.T) * scale
        keep, give = cut(total, lax.rem(here, 2), tokens // 2)
        refs[N.mine][...] = keep
        refs[N.other][...] = give

    out = ((tokens // 2, tokens), F32)
    found = call(
        body, place,
        {**dict(enumerate(pieces)), N.rows: rows, N.near: near, **{(N.far, i): e for i, e in enumerate(earlier)}},
        {N.mine: out, N.other: out},
        scratch=[pltpu.VMEM((3, tokens, own), BF16), pltpu.VMEM((tokens, tokens), F32)],
        limit=16 * MIB, far=[(N.far, i) for i in range(len(earlier))],
        flops=2 * tokens * own * tokens, bytes_accessed=2 * own * tokens,
    )
    return found[N.mine], found[N.other]


def fetch(output_factor, place, earlier):
    def body(here, refs, sem):
        copy = pltpu.make_async_copy(refs[N.factor], refs[N.out], sem)
        copy.start()
        copy.wait()

    return call(
        body, place, {N.factor: output_factor, N.earlier: earlier}, {N.out: (output_factor.shape, F32)},
        scratch=[pltpu.SemaphoreType.DMA], limit=MIB, far=(N.factor, N.earlier),
    )[N.out]


def cut(value, which, rows):
    return (
        value[pl.ds(pl.multiple_of(which * rows, rows), rows), :],
        value[pl.ds(pl.multiple_of((1 - which) * rows, rows), rows), :],
    )


def update(pieces, groups, halves, output_factor, place, planes, slab_width):
    rows, columns = output_factor.shape
    blocks = token_blocks(groups)
    tokens = sum(p.shape[0] for p in pieces)
    shard = tokens // len(blocks)
    chunk = min(1024, columns)
    scale = 1.0 / tokens
    half = tokens // 2
    count = len(pieces)

    def body(place_ref, *refs):
        ins = refs[:count]
        mine_ref, other_ref, factor_ref, out_ref, gram, grads, left_abs, left = refs[count:]
        here = place_ref[0]

        @pl.when(pl.program_id(0) == 0)
        def _():
            core = lax.rem(here, 2)
            gram[pl.ds(pl.multiple_of(core * half, half), half), :] = mine_ref[...]
            gram[pl.ds(pl.multiple_of((1 - core) * half, half), half), :] = other_ref[...]
            at = 0
            for piece in ins:
                for low in range(0, piece.shape[0], shard):
                    row = pl.multiple_of(shard_of(here, blocks[at], planes) * shard, shard)
                    grads[pl.ds(row, shard), :] = piece[low:low + shard, slab_width:]
                    at += 1
            left_abs[...] = jnp.dot(gram[...], grads[...], preferred_element_type=F32).astype(BF16)
            order = []
            for block in blocks:
                row = pl.multiple_of(shard_of(here, block, planes) * shard, shard)
                order.append(left_abs[pl.ds(row, shard), :])
            left[...] = jnp.concatenate(order, 0).T

        at = pl.ds(pl.multiple_of(pl.program_id(0) * chunk, chunk), chunk)
        part = jnp.concatenate([p[:, at] for p in ins], 0)
        base = factor_ref[:, at] if FETCH else factor_ref[...]
        out_ref[...] = base + jnp.dot(left[...], part, preferred_element_type=F32) * scale

    vmem = pl.BlockSpec(memory_space=pltpu.VMEM)
    return pl.pallas_call(
        body,
        grid=(columns // chunk,),
        in_specs=[pl.BlockSpec(memory_space=pltpu.SMEM)] + [vmem] * (count + 2)
        + [vmem if FETCH else pl.BlockSpec((rows, chunk), lambda j: (0, j))],
        out_specs=pl.BlockSpec((rows, chunk), lambda j: (0, j)),
        scratch_shapes=[
            pltpu.VMEM((tokens, tokens), BF16), pltpu.VMEM((tokens, rows), BF16), pltpu.VMEM((tokens, rows), BF16),
            pltpu.VMEM((rows, tokens), BF16),
        ],
        out_shape=jax.ShapeDtypeStruct((rows, columns), F32),
        compiler_params=pltpu.CompilerParams(vmem_limit_bytes=UPDATE_VMEM),
        cost_estimate=pl.CostEstimate(
            flops=2 * rows * tokens * (columns + tokens), bytes_accessed=8 * rows * columns, transcendentals=0
        ),
    )(place, *pieces, *halves, output_factor)


def per_device(inputs, input_factor, out_grads, output_factor):
    n = lax.axis_size("row")
    planes = n // 4
    half = planes // 2
    place = lax.axis_index("row").reshape(1)
    near = sorted((k for k in range(1, planes) if k != half), key=lambda k: min(k, planes - k))
    early, late = near[: len(near) // 2], near[len(near) // 2:]
    rows, features = inputs.shape
    width, used = features // planes, half + 1
    x_width = half * width + width // 2
    slab_width = output_factor.shape[1]
    own_width = out_grads.shape[1] // n
    cross_width = slab_width + 2 * own_width
    pair_width = slab_width + own_width
    x_shape = ((rows, x_width), BF16)

    def across(value):
        return permute(value, y_perm(n))

    def other_core(value):
        return permute(value, core_perm(n))

    def ahead(value, k):
        return permute(value, plane_perm(n, k))

    def y_of(here):
        return lax.rem(here // 2, 2)

    def columns(ref, first, count, size):
        return ref[:, pl.ds(pl.multiple_of(first * size, size), count * size)]

    def take(out, row, ref, here, other):
        size = width // 2
        out[row:row + rows, : half * width] = ref[:, : half * width]
        left = pl.multiple_of(half * width + half_block(here, planes, other) * size, size)
        out[row:row + rows, half * width:] = ref[:, pl.ds(left, size)]

    def grads_ahead(grads, here, k):
        return columns(grads, lax.rem(here // 4 + k, planes), 1, 4 * own_width)

    def for_neighbour(ref, here):
        return columns(ref, 1 - y_of(here), 1, 2 * own_width)

    def pair(own, give, row, slab, grads, here):
        core = lax.rem(here, 2)
        for out, c in ((own, core), (give, 1 - core)):
            out[row:row + rows, :slab_width] = slab
            out[row:row + rows, slab_width:] = grads(c)

    def pairs(own, give, here, slabs, slabs_crossed, grads, grads_crossed):
        y = y_of(here)
        for i, ref in enumerate(slabs):
            pair(own, give, i * rows, ref[...], lambda c, i=i: columns(grads[i], y * 2 + c, 1, own_width), here)
        for i in range(len(slabs)):
            at = slice(i * rows, (i + 1) * rows)
            mine = lambda c, at=at: grads_crossed[at, pl.ds(pl.multiple_of(c * own_width, own_width), own_width)]
            pair(own, give, (len(slabs) + i) * rows, slabs_crossed[at, :], mine, here)

    def pair_shapes(count):
        return {k: ((2 * count * rows, pair_width), BF16) for k in (N.own, N.give)}

    slab_shape, grads_shape = ((rows, slab_width), BF16), ((rows, 4 * own_width), BF16)

    blocks = {k: used + (k == half - 1) for k in near}

    def first(here, r):
        plane = here // 4
        for k in near:
            for j in range(blocks[k]):
                r[k][:, j * width:(j + 1) * width] = columns(r[N.x], lax.rem(plane + k + j, planes), 1, width)
        for name, other in ((N.own, False), (N.cross, True)):
            for j in range(half):
                r[name][:, j * width:(j + 1) * width] = columns(r[N.x], lax.rem(plane + j, planes), 1, width)
            at = lax.rem(plane + half, planes) * 2 + half_block(here, planes, other)
            r[name][:, half * width:] = columns(r[N.x], at, 1, width // 2)

    def first_grads(here, r):
        plane = here // 4
        r[N.cross][:, :slab_width] = r[N.grads][:, :slab_width]
        r[N.cross][:, slab_width:] = columns(r[N.grads], plane * 2 + 1 - y_of(here), 1, 2 * own_width)
        r[N.slab][...] = r[N.grads][:, :slab_width]
        r[N.chip][...] = columns(r[N.grads], plane * 2 + y_of(here), 1, 2 * own_width)
        for k in range(1, planes):
            r[k][...] = grads_ahead(r[N.grads], here, k)

    out = call(
        first, place, {N.x: inputs},
        {**{k: ((rows, blocks[k] * width), BF16) for k in near}, N.own: x_shape, N.cross: x_shape},
    )
    own = out[N.own]
    got = {k: ahead(out[k], k) for k in near}
    crossed_0 = across(out[N.cross])
    sent = call(
        first_grads, place, {N.grads: out_grads},
        {
            N.cross: ((rows, cross_width), BF16), N.slab: slab_shape, N.chip: ((rows, 2 * own_width), BF16),
            **{k: grads_shape for k in range(1, planes)},
        },
    )
    grads_crossed_0 = across(sent[N.cross])

    def second(here, r):
        r[N.far][...] = r[half - 1][:, width:]
        for i, k in enumerate(near):
            take(r[N.near], i * rows, r[k], here, True)
        stack(r[N.pair], [r[N.own], r[N.crossed]])
        r[N.slab][...] = r[N.sent][...]

    out = call(
        second, place,
        {
            **{k: got[k] for k in near}, N.own: own, N.crossed: crossed_0, N.sent: sent[N.slab],
            N.grads_crossed: grads_crossed_0,
        },
        {
            N.far: ((rows, used * width), BF16), N.near: ((len(near) * rows, x_width), BF16),
            N.pair: ((2 * rows, x_width), BF16), N.slab: slab_shape,
        },
        far=(N.grads_crossed,),
    )
    pair_0 = out[N.pair]
    far = ahead(out[N.far], 1)
    crossed_near = across(out[N.near])
    pair_0_other = other_core(pair_0)
    slab_got = {k: ahead(out[N.slab], k) for k in early}

    def third(here, r):
        take(r[N.cross], 0, r[N.far], here, True)
        for i, k in enumerate(near):
            take(r[N.pair], i * rows, r[k], here, False)
        r[N.pair][len(near) * rows:, :] = r[N.crossed][...]
        stack(r[N.slab_cross], [r[N.slab, k] for k in early])
        r[N.slab][...] = r[N.sent][...]
        for k in near:
            r[N.send, k][...] = r[N.sent, k][...]

    out = call(
        third, place,
        {
            **{k: got[k] for k in near}, N.far: far, N.crossed: crossed_near, N.other: pair_0_other,
            N.sent: sent[N.slab], **{(N.sent, k): sent[k] for k in near}, **{(N.slab, k): slab_got[k] for k in early},
        },
        {
            N.cross: x_shape, N.pair: ((2 * len(near) * rows, x_width), BF16),
            N.slab_cross: ((len(early) * rows, slab_width), BF16), N.slab: slab_shape,
            **{(N.send, k): grads_shape for k in near},
        },
    )
    pair_near = out[N.pair]
    crossed_far = across(out[N.cross])
    pair_near_other = other_core(pair_near)
    grads_got = {k: ahead(out[N.send, k], k) for k in near}
    slab_got.update({k: ahead(out[N.slab], k) for k in late})
    slab_early_crossed = across(out[N.slab_cross])
    before = [pair_0, pair_0_other, pair_near, pair_near_other]
    products, blocks_here = gram_rows(before, input_factor, place, planes)

    def fourth(here, r):
        take(r[N.pair], 0, r[N.far], here, False)
        r[N.pair][rows:, :] = r[N.crossed][...]
        r[N.slab][...] = r[N.between][...]
        r[N.send][...] = r[N.sent][...]

    out = call(
        fourth, place,
        {
            N.far: far, N.crossed: crossed_far, N.other: pair_near_other, N.between: slab_got[half - 1],
            N.sent: sent[half], N.products: products, **{(N.grads, k): grads_got[k] for k in near},
            **{(N.late, k): slab_got[k] for k in late},
        },
        {N.pair: ((2 * rows, x_width), BF16), N.slab: slab_shape, N.send: grads_shape},
        far=(N.products, *[(N.grads, k) for k in near], *[(N.late, k) for k in late]),
    )
    after = [out[N.pair], other_core(out[N.pair])]
    far_slab = ahead(out[N.slab], 1)
    far_grads = ahead(out[N.send], half)

    def own_pair(here, r):
        mine = lambda c: columns(r[N.chip], c, 1, own_width)
        pair(r[N.own], r[N.give], 0, r[N.slab][...], mine, here)
        mine = lambda c: r[N.crossed][:, pl.ds(pl.multiple_of(slab_width + c * own_width, 128), own_width)]
        pair(r[N.own], r[N.give], rows, r[N.crossed][:, :slab_width], mine, here)

    out = call(
        own_pair, place, {N.slab: sent[N.slab], N.chip: sent[N.chip], N.crossed: grads_crossed_0}, pair_shapes(1)
    )
    final = [out[N.own], other_core(out[N.give])]
    mine, other = gram_part(products, blocks_here, before, after, [[0], near, [half]], place, planes, features, [])
    tokens = mine.shape[1]
    other = other_core(other)

    quarter = tokens // 4

    def fifth(here, r, total):
        total[...] = r[N.mine][...] + r[N.other][...]
        keep, give = cut(total, y_of(here), quarter)
        r[N.keep][...] = keep
        r[N.low][...] = give.astype(BF16)

    out = call(
        fifth, place, {N.mine: mine, N.other: other},
        {N.keep: ((quarter, tokens), F32), N.low: ((quarter, tokens), BF16)},
        scratch=[pltpu.VMEM((2 * quarter, tokens), F32)],
    )
    total, low = out[N.keep], across(out[N.low])

    def add(here, r):
        total = r[N.mine][...] + r[N.other][...].astype(F32)
        r[N.sum][...] = total
        r[N.low][...] = total.astype(BF16)

    def add_near(here, r):
        add(here, r)
        stack(r[N.slab_cross], [r[N.slab, k] for k in late])
        for i, k in enumerate(near):
            r[N.grads_cross][i * rows:(i + 1) * rows, :] = for_neighbour(r[N.grads, k], here)

    shapes = {N.sum: (total.shape, F32), N.low: (total.shape, BF16)}
    out = call(
        add_near, place,
        {
            N.mine: total, N.other: low, **{(N.slab, k): slab_got[k] for k in late},
            **{(N.grads, k): grads_got[k] for k in near},
        },
        {
            **shapes, N.slab_cross: ((len(late) * rows, slab_width), BF16),
            N.grads_cross: ((len(near) * rows, 2 * own_width), BF16),
        },
    )
    slab_late_crossed, grads_crossed = across(out[N.slab_cross]), across(out[N.grads_cross])
    factor = fetch(output_factor, place, out[N.sum])

    def far_slab_across(here, r):
        r[N.cross][...] = r[N.slab][...]

    def far_grads_across(here, r):
        r[N.cross][...] = for_neighbour(r[N.grads], here)

    step = 4
    while step < n:
        low = permute(out[N.low], [(i, i ^ step) for i in range(n)])
        ins = {N.mine: out[N.sum], N.other: low}
        if step == 4:
            out = call(
                add, place, {**ins, N.factor: factor, N.late: slab_late_crossed, N.near: grads_crossed, N.far_slab: far_slab}, shapes,
                far=(N.factor, N.late, N.near, N.far_slab),
            )
            far_sent = call(
                far_slab_across, place, {N.slab: far_slab, N.earlier: out[N.sum]}, {N.cross: slab_shape}, far=(N.earlier,)
            )
        else:
            out = call(add, place, ins, shapes)
        step *= 2
    far_slab_crossed = across(far_sent[N.cross])
    summed = out[N.sum]
    far_sent = call(
        far_grads_across, place, {N.grads: far_grads, N.earlier: summed},
        {N.cross: ((rows, 2 * own_width), BF16)}, far=(N.earlier,),
    )
    far_grads_crossed = across(far_sent[N.cross])

    def near_pairs(here, r):
        groups = ((early, r[N.early], 0), (late, r[N.late], len(early)))
        for i, (some, crossed, at) in enumerate(groups):
            pairs(
                r[N.own, i], r[N.give, i], here, [r[N.slab, k] for k in some], crossed, [r[N.grads, k] for k in some],
                r[N.grads_crossed].at[at * rows:(at + len(some)) * rows, :],
            )

    pair_out = call(
        near_pairs, place,
        {
            N.early: slab_early_crossed, N.late: slab_late_crossed, N.grads_crossed: grads_crossed,
            **{(N.slab, k): slab_got[k] for k in near}, **{(N.grads, k): grads_got[k] for k in near}, N.earlier: summed,
        },
        {(k, i): shape for i, some in enumerate((early, late)) for k, shape in pair_shapes(len(some)).items()},
        far=(N.earlier,),
    )
    for i in range(2):
        final += [pair_out[N.own, i], other_core(pair_out[N.give, i])]

    low = out[N.low]

    def join(here, r):
        y = y_of(here)
        r[N.gram][pl.ds(pl.multiple_of(y * quarter, quarter), quarter), :] = r[N.mine][...]
        r[N.gram][pl.ds(pl.multiple_of((1 - y) * quarter, quarter), quarter), :] = r[N.other][...]

    out = call(join, place, {N.mine: low, N.other: across(low)}, {N.gram: ((2 * quarter, tokens), BF16)})
    halves = [out[N.gram], other_core(out[N.gram])]

    def last(here, r):
        pairs(r[N.own], r[N.give], here, [r[N.slab]], r[N.slabs], [r[N.grads]], r[N.crossed])

    out = call(
        last, place,
        {
            N.slab: far_slab, N.slabs: far_slab_crossed, N.grads: far_grads, N.crossed: far_grads_crossed,
            N.earlier: out[N.gram],
        },
        pair_shapes(1), far=(N.earlier,),
    )
    final += [out[N.own], other_core(out[N.give])]
    return update(final, [[0], early, late, [half]], halves, factor, place, planes, slab_width)


def solution(mesh):
    spec = P(("groups", "row"), None)
    return jax.shard_map(per_device, mesh=mesh, in_specs=(spec,) * 4, out_specs=spec, check_vma=False)
```

time: 273 us -> 123 us (0.45)
  waiting for transfers between devices: 223 us -> 64.6 us
  matrix products: 25.4 us -> 0 us
  starting transfers between devices: 7.47 us -> 31.3 us
  Pallas kernels: 0 us -> 18.8 us
  between operations: 13.1 us -> 0.18 us
  local copies, waits for them, and re-layouts: 3.96 us -> 8.03 us
    all_gather x2 -> x0, waiting for transfers between devices: 127 us -> none  [the longest x1 87.8 us: per_device(): whole = lax.all_gather(inputs, 'row', axis=0, tiled=True)]
    psum x1 -> x0, waiting for transfers between devices: 95.3 us -> none  [per_device(): gram = (lax.psum(partial_value, 'row') * factor).astype(jnp.bfloat16)]
    ppermute x0 -> x31, waiting for transfers between devices: none -> 64.6 us  [permute(): return lax.ppermute(value, 'row', perm)]
    ppermute x0 -> x31, starting transfers between devices: none -> 31.3 us  [permute(): return lax.ppermute(value, 'row', perm)]
    dot_general x2 -> x0, matrix products: 25.4 us -> none  [the longest x1 13.6 us: per_device(): update = jnp.dot(left, slab_all, preferred_element_type=jnp.float32)]
    pallas_call x0 -> x19, Pallas kernels: none -> 18.8 us  [the longest x18 9.62 us: call(): pl.pallas_call(kernel, in_specs=[pl.BlockSpec(memory_space=pltpu.SMEM)] +...]
    unnamed x0 -> x6, local copies, waits for them, and re-layouts: none -> 8.03 us
    all_to_all x1 -> x0, starting transfers between devices: 7.39 us -> none  [per_device(): lax.all_to_all(out_grads, 'row', split_axis=1, concat_axis=0, tiled=True)]
  transfers between devices with their start and end apart: 4 -> 31, of which waited for: 3 -> 14; matrix products, arithmetic and copies ran while one was open for 6% -> 0% of each run, Pallas kernels for 0% -> 5%
where the time goes in v3:
time: 123 us
  waiting for transfers between devices  64.6 us (53%)
  starting transfers between devices  31.3 us (25%)
  Pallas kernels  18.8 us (15%)
  local copies, waits for them, and re-layouts  8.03 us (7%)
    ppermute x31, waiting for transfers between devices, permute(): return lax.ppermute(value, 'row', perm)  64.6 us
    ppermute x31, starting transfers between devices, permute(): return lax.ppermute(value, 'row', perm)  31.3 us
    pallas_call x18, Pallas kernels, call(): pl.pallas_call(kernel, in_specs=[pl.BlockSpec(memory_space=pltpu.SMEM)] +...  9.62 us
    pallas_call x1, Pallas kernels, update(): pl.pallas_call(body, grid=(columns // chunk,), in_specs=[pl.BlockSpec(mem...  9.21 us
    unnamed x6, local copies, waits for them, and re-layouts  8.03 us
  transfers between devices with their start and end apart: 31, of which 14 were waited for; matrix products, arithmetic and copies ran while one was open for 0% of the time, Pallas kernels for 5%

profile of v3, /device:TPU:0, one launch (start us, length us, event | category | flops | bytes accessed | tf_op | source)
XLA Modules:
  0.0 123.0 jit_solution(13655691891038066715)
XLA Ops:
  0.0 1.0 copy-done.2
  1.0 0.1 shard_map.48
  1.1 3.1 %collective-permute-start.2 = (bf16[32,8192]{1,0:T(8,128)(2,1)S(1)}, bf16[32,8192]{1,0:T(8,128)(2,1)S(1)}, u32[]{:S(2)}, u32[]{:S(2)}) collective-permute-start(bf16[32,8192]{1,0:T(8,128)(2,1)S(1)} %get-tuple-element.55), channel_id=1, source_target_pairs={{0,4},{1,5},{2,6},{3,7},{4,8},{5,9},{6,10},{7,11},{8,12},{9,13},{1... | collective-permute-start | bytes 1572872 | tf_op jit(solution)/shard_map/ppermute | solution.py:54
  4.2 1.2 copy-done.1
  5.5 0.1 shard_map.46
  5.6 1.6 %collective-permute-start = (bf16[32,6144]{1,0:T(8,128)(2,1)S(1)}, bf16[32,6144]{1,0:T(8,128)(2,1)S(1)}, u32[]{:S(2)}, u32[]{:S(2)}) collective-permute-start(bf16[32,6144]{1,0:T(8,128)(2,1)S(1)} %get-tuple-element.52), channel_id=1, source_target_pairs={{0,2},{1,3},{2,0},{3,1},{4,6},{5,7},{6,4},{7,5},{8,10},{9,11},{10,... | collective-permute-start | bytes 1179656 | tf_op jit(solution)/shard_map/ppermute | solution.py:54
  7.1 2.2 %collective-permute-start.3 = (bf16[32,6144]{1,0:T(8,128)(2,1)S(1)}, bf16[32,6144]{1,0:T(8,128)(2,1)S(1)}, u32[]{:S(2)}, u32[]{:S(2)}) collective-permute-start(bf16[32,6144]{1,0:T(8,128)(2,1)S(1)} %get-tuple-element.56), channel_id=1, source_target_pairs={{0,12},{1,13},{2,14},{3,15},{4,0},{5,1},{6,2},{7,3},{8,4},{9,5},{1... | collective-permute-start | bytes 1179656 | tf_op jit(solution)/shard_map/ppermute | solution.py:54
  9.4 0.3 collective-permute-start.4
  9.7 13.5 %collective-permute-done.4.refs_3_ = bf16[32,5120]{1,0:T(8,128)(2,1)S(1)} collective-permute-done((bf16[32,5120]{1,0:T(8,128)(2,1)S(1)}, bf16[32,5120]{1,0:T(8,128)(2,1)S(1)}, u32[]{:S(2)}, u32[]{:S(2)}) %collective-permute-start.4) | collective-permute-done | bytes 327712 | tf_op jit(solution)/shard_map/ppermute | solution.py:54
  23.2 0.0 collective-permute-done.refs_2_.refs_5_
  23.2 3.4 %collective-permute-done.3.refs_1_ = bf16[32,6144]{1,0:T(8,128)(2,1)S(1)} collective-permute-done((bf16[32,6144]{1,0:T(8,128)(2,1)S(1)}, bf16[32,6144]{1,0:T(8,128)(2,1)S(1)}, u32[]{:S(2)}, u32[]{:S(2)}) %collective-permute-start.3) | collective-permute-done | bytes 393248 | tf_op jit(solution)/shard_map/ppermute | solution.py:54
  26.6 0.0 collective-permute-done.2.refs_0_
  26.6 0.1 shard_map.49
  26.7 1.6 %collective-permute-start.6 = (bf16[64,5120]{1,0:T(8,128)(2,1)S(1)}, bf16[64,5120]{1,0:T(8,128)(2,1)S(1)}, u32[]{:S(2)}, u32[]{:S(2)}) collective-permute-start(bf16[64,5120]{1,0:T(8,128)(2,1)S(1)} %get-tuple-element.60), channel_id=1, source_target_pairs={{0,2},{1,3},{2,0},{3,1},{4,6},{5,7},{6,4},{7,5},{8,10},{9,11},{10,... | collective-permute-start | bytes 1966088 | tf_op jit(solution)/shard_map/ppermute | solution.py:54
  28.3 0.6 collective-permute-start.5
  28.9 0.7 collective-permute-start.8
  29.6 17.7 %collective-permute-done.8.refs_8_.refs_3_ = bf16[32,4096]{1,0:T(8,128)(2,1)S(1)} collective-permute-done((bf16[32,4096]{1,0:T(8,128)(2,1)S(1)}, bf16[32,4096]{1,0:T(8,128)(2,1)S(1)}, u32[]{:S(2)}, u32[]{:S(2)}) %collective-permute-start.8) | collective-permute-done | bytes 262176 | tf_op jit(solution)/shard_map/ppermute | solution.py:54
  47.3 0.2 shard_map.50
  47.5 0.1 collective-permute-start.10
  47.5 0.6 collective-permute-start.11
  48.1 0.0 collective-permute-start.12
  48.1 3.8 %collective-permute-start.13 = (bf16[32,4096]{1,0:T(8,128)(2,1)S(1)}, bf16[32,4096]{1,0:T(8,128)(2,1)S(1)}, u32[]{:S(2)}, u32[]{:S(2)}) collective-permute-start(bf16[32,4096]{1,0:T(8,128)(2,1)S(1)} %get-tuple-element.71), channel_id=1, source_target_pairs={{0,12},{1,13},{2,14},{3,15},{4,0},{5,1},{6,2},{7,3},{8,4},{9,5},{1... | collective-permute-start | bytes 786440 | tf_op jit(solution)/shard_map/ppermute | solution.py:54
  51.9 0.0 collective-permute-start.14
  52.0 0.0 collective-permute-done.10.refs_3_.refs_2_
  52.0 4.1 %shard_map.51 = (f32[384,512]{1,0:T(8,128)S(1)}, bf16[512,5120]{1,0:T(8,128)(2,1)S(1)}) custom-call(s32[1]{0:T(128)} %bitcast.place_ref, bf16[64,5120]{1,0:T(8,128)(2,1)S(1)} %get-tuple-element.61.refs_0_, bf16[64,5120]{1,0:T(8,128)(2,1)S(1)} %collective-permute-done.7.refs_4_.refs_1_, bf16[128,5120]{1,0:T(8,128)(2,1)S(1)} %get-tuple-element.66.refs_2_, ...), custom_call_target="tpu_custom_call" | custom-call | flops 2013265920 | bytes 5242880 | tf_op jit(solution)/shard_map/pallas_call | solution.py:77
  56.1 3.0 %collective-permute-done.12.refs_6_.refs_3_.refs_5_ = bf16[32,4096]{1,0:T(8,128)(2,1)S(1)} collective-permute-done((bf16[32,4096]{1,0:T(8,128)(2,1)S(1)}, bf16[32,4096]{1,0:T(8,128)(2,1)S(1)}, u32[]{:S(2)}, u32[]{:S(2)}) %collective-permute-start.12) | collective-permute-done | bytes 262176 | tf_op jit(solution)/shard_map/ppermute | solution.py:54
  59.1 3.8 %collective-permute-done.13.refs_7_.refs_4_.refs_6_ = bf16[32,4096]{1,0:T(8,128)(2,1)S(1)} collective-permute-done((bf16[32,4096]{1,0:T(8,128)(2,1)S(1)}, bf16[32,4096]{1,0:T(8,128)(2,1)S(1)}, u32[]{:S(2)}, u32[]{:S(2)}) %collective-permute-start.13) | collective-permute-done | bytes 262176 | tf_op jit(solution)/shard_map/ppermute | solution.py:54
  62.9 4.8 %collective-permute-done.14.refs_8_.refs_2_.refs_4_ = bf16[32,4096]{1,0:T(8,128)(2,1)S(1)} collective-permute-done((bf16[32,4096]{1,0:T(8,128)(2,1)S(1)}, bf16[32,4096]{1,0:T(8,128)(2,1)S(1)}, u32[]{:S(2)}, u32[]{:S(2)}) %collective-permute-start.14) | collective-permute-done | bytes 262176 | tf_op jit(solution)/shard_map/ppermute | solution.py:54
  67.7 0.1 shard_map.52
  67.8 0.1 collective-permute-start.15
  67.9 2.1 %collective-permute-done.15.refs_5_ = bf16[64,5120]{1,0:T(8,128)(2,1)S(1)} collective-permute-done((bf16[64,5120]{1,0:T(8,128)(2,1)S(1)}, bf16[64,5120]{1,0:T(8,128)(2,1)S(1)}, u32[]{:S(2)}, u32[]{:S(2)}) %collective-permute-start.15) | collective-permute-done | bytes 655392 | tf_op jit(solution)/shard_map/ppermute | solution.py:54
  70.0 3.1 %shard_map.53 = (f32[256,512]{1,0:T(8,128)S(1)}, f32[256,512]{1,0:T(8,128)S(1)}) custom-call(s32[1]{0:T(128)} %bitcast.place_ref, bf16[64,5120]{1,0:T(8,128)(2,1)S(1)} %get-tuple-element.61.refs_0_, bf16[64,5120]{1,0:T(8,128)(2,1)S(1)} %collective-permute-done.7.refs_4_.refs_1_, bf16[128,5120]{1,0:T(8,128)(2,1)S(1)} %get-tuple-element.66.refs_2_, ...), custom_call_target="tpu_custom_call" | custom-call | flops 268435456 | bytes 524288 | tf_op jit(solution)/shard_map/pallas_call | solution.py:77
  73.1 0.2 collective-permute-start.16
  73.3 1.8 %collective-permute-done.16.refs_1_ = f32[256,512]{1,0:T(8,128)S(1)} collective-permute-done((f32[256,512]{1,0:T(8,128)S(1)}, f32[256,512]{1,0:T(8,128)S(1)}, u32[]{:S(2)}, u32[]{:S(2)}) %collective-permute-start.16) | collective-permute-done | bytes 524320 | tf_op jit(solution)/shard_map/ppermute | solution.py:54
  75.1 0.1 shard_map.54
  75.2 1.6 %collective-permute-start.17 = (bf16[128,512]{1,0:T(8,128)(2,1)S(1)}, bf16[128,512]{1,0:T(8,128)(2,1)S(1)}, u32[]{:S(2)}, u32[]{:S(2)}) collective-permute-start(bf16[128,512]{1,0:T(8,128)(2,1)S(1)} %get-tuple-element.78), channel_id=1, source_target_pairs={{0,2},{1,3},{2,0},{3,1},{4,6},{5,7},{6,4},{7,5},{8,10},{9,11},{10,... | collective-permute-start | bytes 393224 | tf_op jit(solution)/shard_map/ppermute | solution.py:54
  76.8 0.0 collective-permute-start.21
  76.8 4.0 %collective-permute-done.17.refs_1_ = bf16[128,512]{1,0:T(8,128)(2,1)S(1)} collective-permute-done((bf16[128,512]{1,0:T(8,128)(2,1)S(1)}, bf16[128,512]{1,0:T(8,128)(2,1)S(1)}, u32[]{:S(2)}, u32[]{:S(2)}) %collective-permute-start.17) | collective-permute-done | bytes 131104 | tf_op jit(solution)/shard_map/ppermute | solution.py:54
  80.8 0.1 shard_map.55
  80.9 1.6 %collective-permute-start.18 = (bf16[32,4096]{1,0:T(8,128)(2,1)S(1)}, bf16[32,4096]{1,0:T(8,128)(2,1)S(1)}, u32[]{:S(2)}, u32[]{:S(2)}) collective-permute-start(bf16[32,4096]{1,0:T(8,128)(2,1)S(1)} %get-tuple-element.79), channel_id=1, source_target_pairs={{0,2},{1,3},{2,0},{3,1},{4,6},{5,7},{6,4},{7,5},{8,10},{9,11},{10,... | collective-permute-start | bytes 786440 | tf_op jit(solution)/shard_map/ppermute | solution.py:54
  82.4 0.5 collective-permute-start.19
  83.0 0.0 collective-permute-start.20
  83.0 2.6 %collective-permute-start.26 = (bf16[32,4096]{1,0:T(8,128)(2,1)S(1)}, bf16[32,4096]{1,0:T(8,128)(2,1)S(1)}, u32[]{:S(2)}, u32[]{:S(2)}) collective-permute-start(bf16[32,4096]{1,0:T(8,128)(2,1)S(1)} %get-tuple-element.91), channel_id=1, source_target_pairs={{0,8},{1,9},{2,10},{3,11},{4,12},{5,13},{6,14},{7,15},{8,0},{9,1},... | collective-permute-start | bytes 786440 | tf_op jit(solution)/shard_map/ppermute | solution.py:54
  85.6 5.8 %copy-done = f32[1024,4096]{1,0:T(8,128)S(1)} copy-done((f32[1024,4096]{1,0:T(8,128)S(1)}, f32[1024,4096]{1,0:T(8,128)}, u32[]{:S(2)}) %copy-start) | copy-done | bytes 16777240
  91.4 1.2 shard_map.56.refs_2_.refs_10_
  92.5 1.6 %collective-permute-start.9 = (bf16[32,4096]{1,0:T(8,128)(2,1)S(1)}, bf16[32,4096]{1,0:T(8,128)(2,1)S(1)}, u32[]{:S(2)}, u32[]{:S(2)}) collective-permute-start(bf16[32,4096]{1,0:T(8,128)(2,1)S(1)} %get-tuple-element.65), channel_id=1, source_target_pairs={{0,2},{1,3},{2,0},{3,1},{4,6},{5,7},{6,4},{7,5},{8,10},{9,11},{10,... | collective-permute-start | bytes 786440 | tf_op jit(solution)/shard_map/ppermute | solution.py:54
  94.1 0.0 collective-permute-done.20.refs_1_
  94.1 0.5 collective-permute-done.19.refs_4_.refs_2_
  94.7 3.6 %collective-permute-start.22 = (bf16[128,512]{1,0:T(8,128)(2,1)S(1)}, bf16[128,512]{1,0:T(8,128)(2,1)S(1)}, u32[]{:S(2)}, u32[]{:S(2)}) collective-permute-start(bf16[128,512]{1,0:T(8,128)(2,1)S(1)} %get-tuple-element.85), channel_id=1, source_target_pairs={{0,8},{1,9},{2,10},{3,11},{4,12},{5,13},{6,14},{7,15},{8,0},{9,1},... | collective-permute-start | bytes 393224 | tf_op jit(solution)/shard_map/ppermute | solution.py:54
  98.3 1.6 %collective-permute-start.25 = (bf16[32,4096]{1,0:T(8,128)(2,1)S(1)}, bf16[32,4096]{1,0:T(8,128)(2,1)S(1)}, u32[]{:S(2)}, u32[]{:S(2)}) collective-permute-start(bf16[32,4096]{1,0:T(8,128)(2,1)S(1)} %shard_map.60), channel_id=1, source_target_pairs={{0,2},{1,3},{2,0},{3,1},{4,6},{5,7},{6,4},{7,5},{8,10},{9,11},{10,... | collective-permute-start | bytes 786440 | tf_op jit(solution)/shard_map/ppermute | solution.py:54
  99.9 3.6 %collective-permute-done.22.refs_1_ = bf16[128,512]{1,0:T(8,128)(2,1)S(1)} collective-permute-done((bf16[128,512]{1,0:T(8,128)(2,1)S(1)}, bf16[128,512]{1,0:T(8,128)(2,1)S(1)}, u32[]{:S(2)}, u32[]{:S(2)}) %collective-permute-start.22) | collective-permute-done | bytes 131104 | tf_op jit(solution)/shard_map/ppermute | solution.py:54
  103.6 0.6 collective-permute-start.28
  104.2 1.6 %collective-permute-start.27 = (bf16[32,2048]{1,0:T(8,128)(2,1)S(1)}, bf16[32,2048]{1,0:T(8,128)(2,1)S(1)}, u32[]{:S(2)}, u32[]{:S(2)}) collective-permute-start(bf16[32,2048]{1,0:T(8,128)(2,1)S(1)} %shard_map.61), channel_id=1, source_target_pairs={{0,2},{1,3},{2,0},{3,1},{4,6},{5,7},{6,4},{7,5},{8,10},{9,11},{10,... | collective-permute-start | bytes 393224 | tf_op jit(solution)/shard_map/ppermute | solution.py:54
  105.7 0.1 shard_map.47
  105.8 0.1 collective-permute-start.1
  105.9 0.2 shard_map.59
  106.1 0.5 collective-permute-start.23
  106.7 3.1 %collective-permute-done.28.refs_1_ = bf16[128,512]{1,0:T(8,128)(2,1)S(1)} collective-permute-done((bf16[128,512]{1,0:T(8,128)(2,1)S(1)}, bf16[128,512]{1,0:T(8,128)(2,1)S(1)}, u32[]{:S(2)}, u32[]{:S(2)}) %collective-permute-start.28) | collective-permute-done | bytes 131104 | tf_op jit(solution)/shard_map/ppermute | solution.py:54
  109.8 1.4 %collective-permute-done.27.refs_3_ = bf16[32,2048]{1,0:T(8,128)(2,1)S(1)} collective-permute-done((bf16[32,2048]{1,0:T(8,128)(2,1)S(1)}, bf16[32,2048]{1,0:T(8,128)(2,1)S(1)}, u32[]{:S(2)}, u32[]{:S(2)}) %collective-permute-start.27) | collective-permute-done | bytes 131104 | tf_op jit(solution)/shard_map/ppermute | solution.py:54
  111.2 0.1 shard_map.63
  111.2 0.1 collective-permute-start.29
  111.3 0.5 collective-permute-start.30
  111.8 2.0 %collective-permute-done.30.refs_9_ = bf16[256,512]{1,0:T(8,128)(2,1)S(1)} collective-permute-done((bf16[256,512]{1,0:T(8,128)(2,1)S(1)}, bf16[256,512]{1,0:T(8,128)(2,1)S(1)}, u32[]{:S(2)}, u32[]{:S(2)}) %collective-permute-start.30) | collective-permute-done | bytes 262176 | tf_op jit(solution)/shard_map/ppermute | solution.py:54
  113.8 9.2 %shard_map.64 = f32[1024,4096]{1,0:T(8,128)} custom-call(s32[1]{0:T(128)} %bitcast.place_ref, bf16[64,5120]{1,0:T(8,128)(2,1)S(1)} %get-tuple-element.53.refs_0_, bf16[64,5120]{1,0:T(8,128)(2,1)S(1)} %collective-permute-done.1.refs_1_, bf16[64,5120]{1,0:T(8,128)(2,1)S(1)} %get-tuple-element.87.refs_2_, bf16[64,5120]{1,0:T(8,128)(2,1)S(1)} %collective-permute-done.23.refs_3_, ...), custom_call_target="tpu_custom_call" | custom-call | flops 4831838208 | bytes 33554432 | tf_op jit(solution)/shard_map/pallas_call | solution.py:259
  (23 shorter events, 0.2 us)
Async XLA Ops:
  0.0 1.0 copy-start.2
  1.1 25.5 %collective-permute-start.2 = (bf16[32,8192]{1,0:T(8,128)(2,1)S(1)}, bf16[32,8192]{1,0:T(8,128)(2,1)S(1)}, u32[]{:S(2)}, u32[]{:S(2)}) collective-permute-start(bf16[32,8192]{1,0:T(8,128)(2,1)S(1)} %get-tuple-element.55), channel_id=1, source_target_pairs={{0,4},{1,5},{2,6},{3,7},{4,8},{5,9},{6,10},{7,11},{8,12},{9,13},{1... | collective-permute-start | bytes 1572872 | tf_op jit(solution)/shard_map/ppermute | solution.py:54
  4.2 1.2 copy-start.1
  5.6 17.7 %collective-permute-start = (bf16[32,6144]{1,0:T(8,128)(2,1)S(1)}, bf16[32,6144]{1,0:T(8,128)(2,1)S(1)}, u32[]{:S(2)}, u32[]{:S(2)}) collective-permute-start(bf16[32,6144]{1,0:T(8,128)(2,1)S(1)} %get-tuple-element.52), channel_id=1, source_target_pairs={{0,2},{1,3},{2,0},{3,1},{4,6},{5,7},{6,4},{7,5},{8,10},{9,11},{10,... | collective-permute-start | bytes 1179656 | tf_op jit(solution)/shard_map/ppermute | solution.py:54
  7.1 19.5 %collective-permute-start.3 = (bf16[32,6144]{1,0:T(8,128)(2,1)S(1)}, bf16[32,6144]{1,0:T(8,128)(2,1)S(1)}, u32[]{:S(2)}, u32[]{:S(2)}) collective-permute-start(bf16[32,6144]{1,0:T(8,128)(2,1)S(1)} %get-tuple-element.56), channel_id=1, source_target_pairs={{0,12},{1,13},{2,14},{3,15},{4,0},{5,1},{6,2},{7,3},{8,4},{9,5},{1... | collective-permute-start | bytes 1179656 | tf_op jit(solution)/shard_map/ppermute | solution.py:54
  9.4 13.8 %collective-permute-start.4 = (bf16[32,5120]{1,0:T(8,128)(2,1)S(1)}, bf16[32,5120]{1,0:T(8,128)(2,1)S(1)}, u32[]{:S(2)}, u32[]{:S(2)}) collective-permute-start(bf16[32,5120]{1,0:T(8,128)(2,1)S(1)} %get-tuple-element.58), channel_id=1, source_target_pairs={{0,2},{1,3},{2,0},{3,1},{4,6},{5,7},{6,4},{7,5},{8,10},{9,11},{10,... | collective-permute-start | bytes 983048 | tf_op jit(solution)/shard_map/ppermute | solution.py:54
  26.7 20.5 %collective-permute-start.6 = (bf16[64,5120]{1,0:T(8,128)(2,1)S(1)}, bf16[64,5120]{1,0:T(8,128)(2,1)S(1)}, u32[]{:S(2)}, u32[]{:S(2)}) collective-permute-start(bf16[64,5120]{1,0:T(8,128)(2,1)S(1)} %get-tuple-element.60), channel_id=1, source_target_pairs={{0,2},{1,3},{2,0},{3,1},{4,6},{5,7},{6,4},{7,5},{8,10},{9,11},{10,... | collective-permute-start | bytes 1966088 | tf_op jit(solution)/shard_map/ppermute | solution.py:54
  28.3 19.0 %collective-permute-start.7 = (bf16[64,5120]{1,0:T(8,128)(2,1)S(1)}, bf16[64,5120]{1,0:T(8,128)(2,1)S(1)}, u32[]{:S(2)}, u32[]{:S(2)}) collective-permute-start(bf16[64,5120]{1,0:T(8,128)(2,1)S(1)} %get-tuple-element.61.refs_0_), channel_id=1, source_target_pairs={{0,1},{1,0},{2,3},{3,2},{4,5},{5,4},{6,7},{7,6},{8,9},{9,8},{10,11... | collective-permute-start | bytes 1966088 | tf_op jit(solution)/shard_map/ppermute | solution.py:54
  28.3 18.9 %collective-permute-start.5 = (bf16[32,6144]{1,0:T(8,128)(2,1)S(1)}, bf16[32,6144]{1,0:T(8,128)(2,1)S(1)}, u32[]{:S(2)}, u32[]{:S(2)}) collective-permute-start(bf16[32,6144]{1,0:T(8,128)(2,1)S(1)} %get-tuple-element.59), channel_id=1, source_target_pairs={{0,4},{1,5},{2,6},{3,7},{4,8},{5,9},{6,10},{7,11},{8,12},{9,13},{1... | collective-permute-start | bytes 1179656 | tf_op jit(solution)/shard_map/ppermute | solution.py:54
  28.9 18.4 %collective-permute-start.8 = (bf16[32,4096]{1,0:T(8,128)(2,1)S(1)}, bf16[32,4096]{1,0:T(8,128)(2,1)S(1)}, u32[]{:S(2)}, u32[]{:S(2)}) collective-permute-start(bf16[32,4096]{1,0:T(8,128)(2,1)S(1)} %get-tuple-element.64), channel_id=1, source_target_pairs={{0,4},{1,5},{2,6},{3,7},{4,8},{5,9},{6,10},{7,11},{8,12},{9,13},{1... | collective-permute-start | bytes 786440 | tf_op jit(solution)/shard_map/ppermute | solution.py:54
  47.5 4.5 %collective-permute-start.10 = (bf16[128,5120]{1,0:T(8,128)(2,1)S(1)}, bf16[128,5120]{1,0:T(8,128)(2,1)S(1)}, u32[]{:S(2)}, u32[]{:S(2)}) collective-permute-start(bf16[128,5120]{1,0:T(8,128)(2,1)S(1)} %get-tuple-element.66.refs_2_), channel_id=1, source_target_pairs={{0,1},{1,0},{2,3},{3,2},{4,5},{5,4},{6,7},{7,6},{8,9},{9,8},{10,11... | collective-permute-start | bytes 3932168 | tf_op jit(solution)/shard_map/ppermute | solution.py:54
  47.5 20.2 %collective-permute-start.11 = (bf16[32,5120]{1,0:T(8,128)(2,1)S(1)}, bf16[32,5120]{1,0:T(8,128)(2,1)S(1)}, u32[]{:S(2)}, u32[]{:S(2)}) collective-permute-start(bf16[32,5120]{1,0:T(8,128)(2,1)S(1)} %get-tuple-element.67), channel_id=1, source_target_pairs={{0,2},{1,3},{2,0},{3,1},{4,6},{5,7},{6,4},{7,5},{8,10},{9,11},{10,... | collective-permute-start | bytes 983048 | tf_op jit(solution)/shard_map/ppermute | solution.py:54
  48.1 11.0 %collective-permute-start.12 = (bf16[32,4096]{1,0:T(8,128)(2,1)S(1)}, bf16[32,4096]{1,0:T(8,128)(2,1)S(1)}, u32[]{:S(2)}, u32[]{:S(2)}) collective-permute-start(bf16[32,4096]{1,0:T(8,128)(2,1)S(1)} %get-tuple-element.70), channel_id=1, source_target_pairs={{0,4},{1,5},{2,6},{3,7},{4,8},{5,9},{6,10},{7,11},{8,12},{9,13},{1... | collective-permute-start | bytes 786440 | tf_op jit(solution)/shard_map/ppermute | solution.py:54
  48.1 14.8 %collective-permute-start.13 = (bf16[32,4096]{1,0:T(8,128)(2,1)S(1)}, bf16[32,4096]{1,0:T(8,128)(2,1)S(1)}, u32[]{:S(2)}, u32[]{:S(2)}) collective-permute-start(bf16[32,4096]{1,0:T(8,128)(2,1)S(1)} %get-tuple-element.71), channel_id=1, source_target_pairs={{0,12},{1,13},{2,14},{3,15},{4,0},{5,1},{6,2},{7,3},{8,4},{9,5},{1... | collective-permute-start | bytes 786440 | tf_op jit(solution)/shard_map/ppermute | solution.py:54
  51.9 15.8 %collective-permute-start.14 = (bf16[32,4096]{1,0:T(8,128)(2,1)S(1)}, bf16[32,4096]{1,0:T(8,128)(2,1)S(1)}, u32[]{:S(2)}, u32[]{:S(2)}) collective-permute-start(bf16[32,4096]{1,0:T(8,128)(2,1)S(1)} %get-tuple-element.72), channel_id=1, source_target_pairs={{0,12},{1,13},{2,14},{3,15},{4,0},{5,1},{6,2},{7,3},{8,4},{9,5},{1... | collective-permute-start | bytes 786440 | tf_op jit(solution)/shard_map/ppermute | solution.py:54
  67.8 2.2 %collective-permute-start.15 = (bf16[64,5120]{1,0:T(8,128)(2,1)S(1)}, bf16[64,5120]{1,0:T(8,128)(2,1)S(1)}, u32[]{:S(2)}, u32[]{:S(2)}) collective-permute-start(bf16[64,5120]{1,0:T(8,128)(2,1)S(1)} %get-tuple-element.73.refs_4_), channel_id=1, source_target_pairs={{0,1},{1,0},{2,3},{3,2},{4,5},{5,4},{6,7},{7,6},{8,9},{9,8},{10,11... | collective-permute-start | bytes 1966088 | tf_op jit(solution)/shard_map/ppermute | solution.py:54
  73.1 2.0 %collective-permute-start.16 = (f32[256,512]{1,0:T(8,128)S(1)}, f32[256,512]{1,0:T(8,128)S(1)}, u32[]{:S(2)}, u32[]{:S(2)}) collective-permute-start(f32[256,512]{1,0:T(8,128)S(1)} %get-tuple-element.76), channel_id=1, source_target_pairs={{0,1},{1,0},{2,3},{3,2},{4,5},{5,4},{6,7},{7,6},{8,9},{9,8},{10,11... | collective-permute-start | bytes 1572872 | tf_op jit(solution)/shard_map/ppermute | solution.py:54
  75.2 5.6 %collective-permute-start.17 = (bf16[128,512]{1,0:T(8,128)(2,1)S(1)}, bf16[128,512]{1,0:T(8,128)(2,1)S(1)}, u32[]{:S(2)}, u32[]{:S(2)}) collective-permute-start(bf16[128,512]{1,0:T(8,128)(2,1)S(1)} %get-tuple-element.78), channel_id=1, source_target_pairs={{0,2},{1,3},{2,0},{3,1},{4,6},{5,7},{6,4},{7,5},{8,10},{9,11},{10,... | collective-permute-start | bytes 393224 | tf_op jit(solution)/shard_map/ppermute | solution.py:54
  76.8 15.8 %collective-permute-start.21 = (bf16[32,4096]{1,0:T(8,128)(2,1)S(1)}, bf16[32,4096]{1,0:T(8,128)(2,1)S(1)}, u32[]{:S(2)}, u32[]{:S(2)}) collective-permute-start(bf16[32,4096]{1,0:T(8,128)(2,1)S(1)} %get-tuple-element.83), channel_id=1, source_target_pairs={{0,4},{1,5},{2,6},{3,7},{4,8},{5,9},{6,10},{7,11},{8,12},{9,13},{1... | collective-permute-start | bytes 786440 | tf_op jit(solution)/shard_map/ppermute | solution.py:54
  80.9 13.3 %collective-permute-start.18 = (bf16[32,4096]{1,0:T(8,128)(2,1)S(1)}, bf16[32,4096]{1,0:T(8,128)(2,1)S(1)}, u32[]{:S(2)}, u32[]{:S(2)}) collective-permute-start(bf16[32,4096]{1,0:T(8,128)(2,1)S(1)} %get-tuple-element.79), channel_id=1, source_target_pairs={{0,2},{1,3},{2,0},{3,1},{4,6},{5,7},{6,4},{7,5},{8,10},{9,11},{10,... | collective-permute-start | bytes 786440 | tf_op jit(solution)/shard_map/ppermute | solution.py:54
  82.4 12.2 %collective-permute-start.19 = (bf16[64,2048]{1,0:T(8,128)(2,1)S(1)}, bf16[64,2048]{1,0:T(8,128)(2,1)S(1)}, u32[]{:S(2)}, u32[]{:S(2)}) collective-permute-start(bf16[64,2048]{1,0:T(8,128)(2,1)S(1)} %get-tuple-element.80), channel_id=1, source_target_pairs={{0,2},{1,3},{2,0},{3,1},{4,6},{5,7},{6,4},{7,5},{8,10},{9,11},{10,... | collective-permute-start | bytes 786440 | tf_op jit(solution)/shard_map/ppermute | solution.py:54
  83.0 11.2 %collective-permute-start.20 = (bf16[128,512]{1,0:T(8,128)(2,1)S(1)}, bf16[128,512]{1,0:T(8,128)(2,1)S(1)}, u32[]{:S(2)}, u32[]{:S(2)}) collective-permute-start(bf16[128,512]{1,0:T(8,128)(2,1)S(1)} %get-tuple-element.82), channel_id=1, source_target_pairs={{0,4},{1,5},{2,6},{3,7},{4,0},{5,1},{6,2},{7,3},{8,12},{9,13},{10,... | collective-permute-start | bytes 393224 | tf_op jit(solution)/shard_map/ppermute | solution.py:54
  83.0 21.2 %collective-permute-start.26 = (bf16[32,4096]{1,0:T(8,128)(2,1)S(1)}, bf16[32,4096]{1,0:T(8,128)(2,1)S(1)}, u32[]{:S(2)}, u32[]{:S(2)}) collective-permute-start(bf16[32,4096]{1,0:T(8,128)(2,1)S(1)} %get-tuple-element.91), channel_id=1, source_target_pairs={{0,8},{1,9},{2,10},{3,11},{4,12},{5,13},{6,14},{7,15},{8,0},{9,1},... | collective-permute-start | bytes 786440 | tf_op jit(solution)/shard_map/ppermute | solution.py:54
  85.6 5.8 %copy-start = (f32[1024,4096]{1,0:T(8,128)S(1)}, f32[1024,4096]{1,0:T(8,128)}, u32[]{:S(2)}) copy-start(f32[1024,4096]{1,0:T(8,128)} %refs_0_.5) | copy-start | bytes 50331652
  92.5 13.4 %collective-permute-start.9 = (bf16[32,4096]{1,0:T(8,128)(2,1)S(1)}, bf16[32,4096]{1,0:T(8,128)(2,1)S(1)}, u32[]{:S(2)}, u32[]{:S(2)}) collective-permute-start(bf16[32,4096]{1,0:T(8,128)(2,1)S(1)} %get-tuple-element.65), channel_id=1, source_target_pairs={{0,2},{1,3},{2,0},{3,1},{4,6},{5,7},{6,4},{7,5},{8,10},{9,11},{10,... | collective-permute-start | bytes 786440 | tf_op jit(solution)/shard_map/ppermute | solution.py:54
  94.7 8.9 %collective-permute-start.22 = (bf16[128,512]{1,0:T(8,128)(2,1)S(1)}, bf16[128,512]{1,0:T(8,128)(2,1)S(1)}, u32[]{:S(2)}, u32[]{:S(2)}) collective-permute-start(bf16[128,512]{1,0:T(8,128)(2,1)S(1)} %get-tuple-element.85), channel_id=1, source_target_pairs={{0,8},{1,9},{2,10},{3,11},{4,12},{5,13},{6,14},{7,15},{8,0},{9,1},... | collective-permute-start | bytes 393224 | tf_op jit(solution)/shard_map/ppermute | solution.py:54
  98.3 12.8 %collective-permute-start.25 = (bf16[32,4096]{1,0:T(8,128)(2,1)S(1)}, bf16[32,4096]{1,0:T(8,128)(2,1)S(1)}, u32[]{:S(2)}, u32[]{:S(2)}) collective-permute-start(bf16[32,4096]{1,0:T(8,128)(2,1)S(1)} %shard_map.60), channel_id=1, source_target_pairs={{0,2},{1,3},{2,0},{3,1},{4,6},{5,7},{6,4},{7,5},{8,10},{9,11},{10,... | collective-permute-start | bytes 786440 | tf_op jit(solution)/shard_map/ppermute | solution.py:54
  103.6 6.2 %collective-permute-start.28 = (bf16[128,512]{1,0:T(8,128)(2,1)S(1)}, bf16[128,512]{1,0:T(8,128)(2,1)S(1)}, u32[]{:S(2)}, u32[]{:S(2)}) collective-permute-start(bf16[128,512]{1,0:T(8,128)(2,1)S(1)} %get-tuple-element.92.refs_0_), channel_id=1, source_target_pairs={{0,2},{1,3},{2,0},{3,1},{4,6},{5,7},{6,4},{7,5},{8,10},{9,11},{10,... | collective-permute-start | bytes 393224 | tf_op jit(solution)/shard_map/ppermute | solution.py:54
  104.2 7.0 %collective-permute-start.27 = (bf16[32,2048]{1,0:T(8,128)(2,1)S(1)}, bf16[32,2048]{1,0:T(8,128)(2,1)S(1)}, u32[]{:S(2)}, u32[]{:S(2)}) collective-permute-start(bf16[32,2048]{1,0:T(8,128)(2,1)S(1)} %shard_map.61), channel_id=1, source_target_pairs={{0,2},{1,3},{2,0},{3,1},{4,6},{5,7},{6,4},{7,5},{8,10},{9,11},{10,... | collective-permute-start | bytes 393224 | tf_op jit(solution)/shard_map/ppermute | solution.py:54
  105.8 6.0 %collective-permute-start.1 = (bf16[64,5120]{1,0:T(8,128)(2,1)S(1)}, bf16[64,5120]{1,0:T(8,128)(2,1)S(1)}, u32[]{:S(2)}, u32[]{:S(2)}) collective-permute-start(bf16[64,5120]{1,0:T(8,128)(2,1)S(1)} %get-tuple-element.54), channel_id=1, source_target_pairs={{0,1},{1,0},{2,3},{3,2},{4,5},{5,4},{6,7},{7,6},{8,9},{9,8},{10,11... | collective-permute-start | bytes 1966088 | tf_op jit(solution)/shard_map/ppermute | solution.py:54
  106.1 7.7 %collective-permute-start.23 = (bf16[64,5120]{1,0:T(8,128)(2,1)S(1)}, bf16[64,5120]{1,0:T(8,128)(2,1)S(1)}, u32[]{:S(2)}, u32[]{:S(2)}) collective-permute-start(bf16[64,5120]{1,0:T(8,128)(2,1)S(1)} %get-tuple-element.88), channel_id=1, source_target_pairs={{0,1},{1,0},{2,3},{3,2},{4,5},{5,4},{6,7},{7,6},{8,9},{9,8},{10,11... | collective-permute-start | bytes 1966088 | tf_op jit(solution)/shard_map/ppermute | solution.py:54
  109.7 4.0 %collective-permute-start.24 = (bf16[64,5120]{1,0:T(8,128)(2,1)S(1)}, bf16[64,5120]{1,0:T(8,128)(2,1)S(1)}, u32[]{:S(2)}, u32[]{:S(2)}) collective-permute-start(bf16[64,5120]{1,0:T(8,128)(2,1)S(1)} %get-tuple-element.90), channel_id=1, source_target_pairs={{0,1},{1,0},{2,3},{3,2},{4,5},{5,4},{6,7},{7,6},{8,9},{9,8},{10,11... | collective-permute-start | bytes 1966088 | tf_op jit(solution)/shard_map/ppermute | solution.py:54
  111.2 2.5 %collective-permute-start.29 = (bf16[64,5120]{1,0:T(8,128)(2,1)S(1)}, bf16[64,5120]{1,0:T(8,128)(2,1)S(1)}, u32[]{:S(2)}, u32[]{:S(2)}) collective-permute-start(bf16[64,5120]{1,0:T(8,128)(2,1)S(1)} %get-tuple-element.94), channel_id=1, source_target_pairs={{0,1},{1,0},{2,3},{3,2},{4,5},{5,4},{6,7},{7,6},{8,9},{9,8},{10,11... | collective-permute-start | bytes 1966088 | tf_op jit(solution)/shard_map/ppermute | solution.py:54
  111.3 2.5 %collective-permute-start.30 = (bf16[256,512]{1,0:T(8,128)(2,1)S(1)}, bf16[256,512]{1,0:T(8,128)(2,1)S(1)}, u32[]{:S(2)}, u32[]{:S(2)}) collective-permute-start(bf16[256,512]{1,0:T(8,128)(2,1)S(1)} %shard_map.62.refs_4_.refs_8_), channel_id=1, source_target_pairs={{0,1},{1,0},{2,3},{3,2},{4,5},{5,4},{6,7},{7,6},{8,9},{9,8},{10,11... | collective-permute-start | bytes 786440 | tf_op jit(solution)/shard_map/ppermute | solution.py:54

commit v4 on v3

--- a/solution.py
+++ b/solution.py
@@ -21,6 +21,7 @@
     factor = enum.auto()
     mine = enum.auto()
     other = enum.auto()
+    low = enum.auto()
     far = enum.auto()
     out = enum.auto()
     earlier = enum.auto()
@@ -37,15 +38,10 @@
     grads_crossed = enum.auto()
     slab_cross = enum.auto()
     send = enum.auto()
-    between = enum.auto()
     products = enum.auto()
-    late = enum.auto()
+    rest = enum.auto()
     keep = enum.auto()
-    low = enum.auto()
     sum = enum.auto()
-    grads_cross = enum.auto()
-    far_slab = enum.auto()
-    early = enum.auto()
     gram = enum.auto()
     slabs = enum.auto()
 
@@ -184,18 +180,20 @@
         total[...] = (half + half.T) * scale
         keep, give = cut(total, lax.rem(here, 2), tokens // 2)
         refs[N.mine][...] = keep
-        refs[N.other][...] = give
-
-    out = ((tokens // 2, tokens), F32)
+        high = give.astype(BF16)
+        refs[N.other][...] = high
+        refs[N.low][...] = (give - high.astype(F32)).astype(BF16)
+
+    out = (tokens // 2, tokens)
     found = call(
         body, place,
         {**dict(enumerate(pieces)), N.rows: rows, N.near: near, **{(N.far, i): e for i, e in enumerate(earlier)}},
-        {N.mine: out, N.other: out},
+        {N.mine: (out, F32), N.other: (out, BF16), N.low: (out, BF16)},
         scratch=[pltpu.VMEM((3, tokens, own), BF16), pltpu.VMEM((tokens, tokens), F32)],
         limit=16 * MIB, far=[(N.far, i) for i in range(len(earlier))],
         flops=2 * tokens * own * tokens, bytes_accessed=2 * own * tokens,
     )
-    return found[N.mine], found[N.other]
+    return found[N.mine], found[N.other], found[N.low]
 
 
 def fetch(output_factor, place, earlier):
@@ -279,7 +277,7 @@
     planes = n // 4
     half = planes // 2
     place = lax.axis_index("row").reshape(1)
-    near = sorted((k for k in range(1, planes) if k != half), key=lambda k: min(k, planes - k))
+    near = sorted((k for k in range(1, planes) if k != half), key=lambda k: (k != half - 1, min(k, planes - k)))
     early, late = near[: len(near) // 2], near[len(near) // 2:]
     rows, features = inputs.shape
     width, used = features // planes, half + 1
@@ -314,8 +312,8 @@
     def grads_ahead(grads, here, k):
         return columns(grads, lax.rem(here // 4 + k, planes), 1, 4 * own_width)
 
-    def for_neighbour(ref, here):
-        return columns(ref, 1 - y_of(here), 1, 2 * own_width)
+    def for_neighbour(ref, here, low=0):
+        return ref[:, pl.ds(pl.multiple_of(low + (1 - y_of(here)) * 2 * own_width, own_width), 2 * own_width)]
 
     def pair(own, give, row, slab, grads, here):
         core = lax.rem(here, 2)
@@ -323,10 +321,13 @@
             out[row:row + rows, :slab_width] = slab
             out[row:row + rows, slab_width:] = grads(c)
 
-    def pairs(own, give, here, slabs, slabs_crossed, grads, grads_crossed):
+    def pairs(own, give, here, slabs, slabs_crossed, grads, lows, grads_crossed):
         y = y_of(here)
         for i, ref in enumerate(slabs):
-            pair(own, give, i * rows, ref[...], lambda c, i=i: columns(grads[i], y * 2 + c, 1, own_width), here)
+            mine = lambda c, i=i: grads[i][
+                :, pl.ds(pl.multiple_of(lows[i] + (y * 2 + c) * own_width, own_width), own_width)
+            ]
+            pair(own, give, i * rows, ref[:, :slab_width], mine, here)
         for i in range(len(slabs)):
             at = slice(i * rows, (i + 1) * rows)
             mine = lambda c, at=at: grads_crossed[at, pl.ds(pl.multiple_of(c * own_width, own_width), own_width)]
@@ -336,6 +337,8 @@
         return {k: ((2 * count * rows, pair_width), BF16) for k in (N.own, N.give)}
 
     slab_shape, grads_shape = ((rows, slab_width), BF16), ((rows, 4 * own_width), BF16)
+    wide_shape = ((rows, slab_width + 4 * own_width), BF16)
+    together = half - 1 == 1
 
     blocks = {k: used + (k == half - 1) for k in near}
 
@@ -406,27 +409,32 @@
             take(r[N.pair], i * rows, r[k], here, False)
         r[N.pair][len(near) * rows:, :] = r[N.crossed][...]
         stack(r[N.slab_cross], [r[N.slab, k] for k in early])
-        r[N.slab][...] = r[N.sent][...]
-        for k in near:
-            r[N.send, k][...] = r[N.sent, k][...]
+        for k in early:
+            if together and k == half - 1:
+                r[N.send, k][:, :slab_width] = r[N.slab, k][...]
+                r[N.send, k][:, slab_width:] = r[N.sent, k][...]
+            else:
+                r[N.send, k][...] = r[N.sent, k][...]
+        if not together:
+            r[N.slab][...] = r[N.slab, half - 1][...]
 
     out = call(
         third, place,
         {
             **{k: got[k] for k in near}, N.far: far, N.crossed: crossed_near, N.other: pair_0_other,
-            N.sent: sent[N.slab], **{(N.sent, k): sent[k] for k in near}, **{(N.slab, k): slab_got[k] for k in early},
+            **{(N.sent, k): sent[k] for k in early}, **{(N.slab, k): slab_got[k] for k in early},
         },
         {
             N.cross: x_shape, N.pair: ((2 * len(near) * rows, x_width), BF16),
-            N.slab_cross: ((len(early) * rows, slab_width), BF16), N.slab: slab_shape,
-            **{(N.send, k): grads_shape for k in near},
+            N.slab_cross: ((len(early) * rows, slab_width), BF16), **({} if together else {N.slab: slab_shape}),
+            **{(N.send, k): wide_shape if together and k == half - 1 else grads_shape for k in early},
         },
     )
     pair_near = out[N.pair]
     crossed_far = across(out[N.cross])
     pair_near_other = other_core(pair_near)
-    grads_got = {k: ahead(out[N.send, k], k) for k in near}
-    slab_got.update({k: ahead(out[N.slab], k) for k in late})
+    grads_got = {k: (ahead(out[N.send, k], k), slab_width if together and k == half - 1 else 0) for k in early}
+    far_slab = grads_got[half - 1][0] if together else ahead(out[N.slab], 1)
     slab_early_crossed = across(out[N.slab_cross])
     before = [pair_0, pair_0_other, pair_near, pair_near_other]
     products, blocks_here = gram_rows(before, input_factor, place, planes)
@@ -434,21 +442,25 @@
     def fourth(here, r):
         take(r[N.pair], 0, r[N.far], here, False)
         r[N.pair][rows:, :] = r[N.crossed][...]
-        r[N.slab][...] = r[N.between][...]
-        r[N.send][...] = r[N.sent][...]
+        r[N.send][...] = r[N.sent, half][...]
+        for k in late:
+            r[N.send, k][:, :slab_width] = r[N.sent][...]
+            r[N.send, k][:, slab_width:] = r[N.sent, k][...]
 
     out = call(
         fourth, place,
         {
-            N.far: far, N.crossed: crossed_far, N.other: pair_near_other, N.between: slab_got[half - 1],
-            N.sent: sent[half], N.products: products, **{(N.grads, k): grads_got[k] for k in near},
-            **{(N.late, k): slab_got[k] for k in late},
-        },
-        {N.pair: ((2 * rows, x_width), BF16), N.slab: slab_shape, N.send: grads_shape},
-        far=(N.products, *[(N.grads, k) for k in near], *[(N.late, k) for k in late]),
+            N.far: far, N.crossed: crossed_far, N.other: pair_near_other, N.products: products,
+            N.sent: sent[N.slab], **{(N.sent, k): sent[k] for k in [*late, half]},
+            **{(N.grads, k): grads_got[k][0] for k in early}, N.slab_cross: slab_early_crossed,
+        },
+        {N.pair: ((2 * rows, x_width), BF16), N.send: grads_shape, **{(N.send, k): wide_shape for k in late}},
+        far=(N.products, N.slab_cross, *[(N.grads, k) for k in early]),
     )
     after = [out[N.pair], other_core(out[N.pair])]
-    far_slab = ahead(out[N.slab], 1)
+    for k in late:
+        slab_got[k] = ahead(out[N.send, k], k)
+        grads_got[k] = (slab_got[k], slab_width)
     far_grads = ahead(out[N.send], half)
 
     def own_pair(here, r):
@@ -461,24 +473,38 @@
         own_pair, place, {N.slab: sent[N.slab], N.chip: sent[N.chip], N.crossed: grads_crossed_0}, pair_shapes(1)
     )
     final = [out[N.own], other_core(out[N.give])]
-    mine, other = gram_part(products, blocks_here, before, after, [[0], near, [half]], place, planes, features, [])
+    mine, other, rest = gram_part(products, blocks_here, before, after, [[0], near, [half]], place, planes, features, [])
     tokens = mine.shape[1]
-    other = other_core(other)
+    other, rest = other_core(other), other_core(rest)
 
     quarter = tokens // 4
 
     def fifth(here, r, total):
-        total[...] = r[N.mine][...] + r[N.other][...]
+        total[...] = r[N.mine][...] + (r[N.other][...].astype(F32) + r[N.rest][...].astype(F32))
         keep, give = cut(total, y_of(here), quarter)
         r[N.keep][...] = keep
         r[N.low][...] = give.astype(BF16)
 
     out = call(
-        fifth, place, {N.mine: mine, N.other: other},
+        fifth, place, {N.mine: mine, N.other: other, N.rest: rest},
         {N.keep: ((quarter, tokens), F32), N.low: ((quarter, tokens), BF16)},
         scratch=[pltpu.VMEM((2 * quarter, tokens), F32)],
     )
     total, low = out[N.keep], across(out[N.low])
+
+    def late_across(here, r):
+        for i, k in enumerate(late):
+            at = slice(i * rows, (i + 1) * rows)
+            r[N.cross][at, :slab_width] = r[N.grads, k][:, :slab_width]
+            r[N.cross][at, slab_width:] = for_neighbour(r[N.grads, k], here, grads_got[k][1])
+
+    mixed_shape = ((len(late) * rows, cross_width), BF16)
+    late_out = call(
+        late_across, place,
+        {N.earlier: out[N.low], **{(N.grads, k): grads_got[k][0] for k in late}},
+        {N.cross: mixed_shape}, far=(N.earlier,),
+    )
+    mixed_crossed = across(late_out[N.cross])
 
     def add(here, r):
         total = r[N.mine][...] + r[N.other][...].astype(F32)
@@ -487,28 +513,22 @@
 
     def add_near(here, r):
         add(here, r)
-        stack(r[N.slab_cross], [r[N.slab, k] for k in late])
-        for i, k in enumerate(near):
-            r[N.grads_cross][i * rows:(i + 1) * rows, :] = for_neighbour(r[N.grads, k], here)
+        for i, k in enumerate(early):
+            at = slice(i * rows, (i + 1) * rows)
+            r[N.cross][at, slab_width:] = for_neighbour(r[N.grads, k], here, grads_got[k][1])
+        r[N.cross][:rows, :slab_width] = r[N.slab][:, :slab_width]
 
     shapes = {N.sum: (total.shape, F32), N.low: (total.shape, BF16)}
     out = call(
         add_near, place,
         {
-            N.mine: total, N.other: low, **{(N.slab, k): slab_got[k] for k in late},
-            **{(N.grads, k): grads_got[k] for k in near},
-        },
-        {
-            **shapes, N.slab_cross: ((len(late) * rows, slab_width), BF16),
-            N.grads_cross: ((len(near) * rows, 2 * own_width), BF16),
-        },
-    )
-    slab_late_crossed, grads_crossed = across(out[N.slab_cross]), across(out[N.grads_cross])
+            N.mine: total, N.other: low, N.slab: far_slab, N.earlier: late_out[N.cross],
+            **{(N.grads, k): grads_got[k][0] for k in early},
+        },
+        {**shapes, N.cross: mixed_shape}, far=(N.earlier,),
+    )
+    far_mixed_crossed = across(out[N.cross])
     factor = fetch(output_factor, place, out[N.sum])
-
-    def far_slab_across(here, r):
-        r[N.cross][...] = r[N.slab][...]
-
     def far_grads_across(here, r):
         r[N.cross][...] = for_neighbour(r[N.grads], here)
 
@@ -517,17 +537,11 @@
         low = permute(out[N.low], [(i, i ^ step) for i in range(n)])
         ins = {N.mine: out[N.sum], N.other: low}
         if step == 4:
-            out = call(
-                add, place, {**ins, N.factor: factor, N.late: slab_late_crossed, N.near: grads_crossed, N.far_slab: far_slab}, shapes,
-                far=(N.factor, N.late, N.near, N.far_slab),
-            )
-            far_sent = call(
-                far_slab_across, place, {N.slab: far_slab, N.earlier: out[N.sum]}, {N.cross: slab_shape}, far=(N.earlier,)
-            )
+            ins.update({N.factor: factor, N.crossed: far_mixed_crossed, N.grads: far_grads})
+            out = call(add, place, ins, shapes, far=(N.factor, N.crossed, N.grads))
         else:
-            out = call(add, place, ins, shapes)
+            out = call(add, place, {**ins, N.crossed: mixed_crossed}, shapes, far=(N.crossed,))
         step *= 2
-    far_slab_crossed = across(far_sent[N.cross])
     summed = out[N.sum]
     far_sent = call(
         far_grads_across, place, {N.grads: far_grads, N.earlier: summed},
@@ -536,18 +550,21 @@
     far_grads_crossed = across(far_sent[N.cross])
 
     def near_pairs(here, r):
-        groups = ((early, r[N.early], 0), (late, r[N.late], len(early)))
-        for i, (some, crossed, at) in enumerate(groups):
-            pairs(
-                r[N.own, i], r[N.give, i], here, [r[N.slab, k] for k in some], crossed, [r[N.grads, k] for k in some],
-                r[N.grads_crossed].at[at * rows:(at + len(some)) * rows, :],
-            )
+        mixed, far_mixed = r[N.crossed], r[N.far]
+        sources = (
+            (early, r[N.slab], far_mixed.at[:, slab_width:]),
+            (late, mixed.at[:, :slab_width], mixed.at[:, slab_width:]),
+        )
+        for i, (some, slabs, crossed) in enumerate(sources):
+            own_slabs = [r[N.slab, k] if k in early else r[N.grads, k] for k in some]
+            grads = [r[N.grads, k] for k in some]
+            pairs(r[N.own, i], r[N.give, i], here, own_slabs, slabs, grads, [grads_got[k][1] for k in some], crossed)
 
     pair_out = call(
         near_pairs, place,
         {
-            N.early: slab_early_crossed, N.late: slab_late_crossed, N.grads_crossed: grads_crossed,
-            **{(N.slab, k): slab_got[k] for k in near}, **{(N.grads, k): grads_got[k] for k in near}, N.earlier: summed,
+            N.slab: slab_early_crossed, N.crossed: mixed_crossed, N.far: far_mixed_crossed, N.earlier: summed,
+            **{(N.slab, k): slab_got[k] for k in early}, **{(N.grads, k): grads_got[k][0] for k in near},
         },
         {(k, i): shape for i, some in enumerate((early, late)) for k, shape in pair_shapes(len(some)).items()},
         far=(N.earlier,),
@@ -566,12 +583,13 @@
     halves = [out[N.gram], other_core(out[N.gram])]
 
     def last(here, r):
-        pairs(r[N.own], r[N.give], here, [r[N.slab]], r[N.slabs], [r[N.grads]], r[N.crossed])
+        slabs = r[N.slabs].at[:rows, :slab_width]
+        pairs(r[N.own], r[N.give], here, [r[N.slab]], slabs, [r[N.grads]], [0], r[N.crossed])
 
     out = call(
         last, place,
         {
-            N.slab: far_slab, N.slabs: far_slab_crossed, N.grads: far_grads, N.crossed: far_grads_crossed,
+            N.slab: far_slab, N.slabs: far_mixed_crossed, N.grads: far_grads, N.crossed: far_grads_crossed,
             N.earlier: out[N.gram],
         },
         pair_shapes(1), far=(N.earlier,),

time: 123 us -> 120 us (0.976)
  starting transfers between devices: 31.3 us -> 27.2 us
    ppermute x31 -> x29, starting transfers between devices: 31.3 us -> 27.2 us  [permute(): return lax.ppermute(value, 'row', perm)]
    ppermute x31 -> x29, waiting for transfers between devices: 64.6 us -> 65.5 us  [permute(): return lax.ppermute(value, 'row', perm)]
  transfers between devices with their start and end apart: 31 -> 29, of which waited for: 14 -> 15; matrix products, arithmetic and copies ran while one was open for 0% -> 0% of each run, Pallas kernels for 5% -> 8%
where the time goes in v4:
time: 120 us
  waiting for transfers between devices  65.5 us (55%)
  starting transfers between devices  27.2 us (23%)
  Pallas kernels  19 us (16%)
  local copies, waits for them, and re-layouts  8.03 us (7%)
    ppermute x29, waiting for transfers between devices, permute(): return lax.ppermute(value, 'row', perm)  65.5 us
    ppermute x29, starting transfers between devices, permute(): return lax.ppermute(value, 'row', perm)  27.2 us
    pallas_call x18, Pallas kernels, call(): pl.pallas_call(kernel, in_specs=[pl.BlockSpec(memory_space=pltpu.SMEM)] +...  9.78 us
    pallas_call x1, Pallas kernels, update(): pl.pallas_call(body, grid=(columns // chunk,), in_specs=[pl.BlockSpec(mem...  9.22 us
    unnamed x6, local copies, waits for them, and re-layouts  8.03 us
  transfers between devices with their start and end apart: 29, of which 15 were waited for; matrix products, arithmetic and copies ran while one was open for 0% of the time, Pallas kernels for 8%

profile of v4, /device:TPU:0, one launch (start us, length us, event | category | flops | bytes accessed | tf_op | source)
XLA Modules:
  0.0 119.8 jit_solution(118068928556590617)
XLA Ops:
  0.0 1.0 copy-done.2
  1.0 0.1 shard_map.48
  1.1 3.1 %collective-permute-start.2 = (bf16[32,8192]{1,0:T(8,128)(2,1)S(1)}, bf16[32,8192]{1,0:T(8,128)(2,1)S(1)}, u32[]{:S(2)}, u32[]{:S(2)}) collective-permute-start(bf16[32,8192]{1,0:T(8,128)(2,1)S(1)} %get-tuple-element.53), channel_id=1, source_target_pairs={{0,4},{1,5},{2,6},{3,7},{4,8},{5,9},{6,10},{7,11},{8,12},{9,13},{1... | collective-permute-start | bytes 1572872 | tf_op jit(solution)/shard_map/ppermute | solution.py:50
  4.2 1.2 %copy-done.1 = bf16[32,16384]{1,0:T(8,128)(2,1)S(1)} copy-done((bf16[32,16384]{1,0:T(8,128)(2,1)S(1)}, bf16[32,16384]{1,0:T(8,128)(2,1)}, u32[]{:S(2)}) %copy-start.1) | copy-done | bytes 1048600
  5.5 0.1 shard_map.46
  5.6 1.6 %collective-permute-start = (bf16[32,6144]{1,0:T(8,128)(2,1)S(1)}, bf16[32,6144]{1,0:T(8,128)(2,1)S(1)}, u32[]{:S(2)}, u32[]{:S(2)}) collective-permute-start(bf16[32,6144]{1,0:T(8,128)(2,1)S(1)} %get-tuple-element.50), channel_id=1, source_target_pairs={{0,2},{1,3},{2,0},{3,1},{4,6},{5,7},{6,4},{7,5},{8,10},{9,11},{10,... | collective-permute-start | bytes 1179656 | tf_op jit(solution)/shard_map/ppermute | solution.py:50
  7.1 2.2 %collective-permute-start.3 = (bf16[32,6144]{1,0:T(8,128)(2,1)S(1)}, bf16[32,6144]{1,0:T(8,128)(2,1)S(1)}, u32[]{:S(2)}, u32[]{:S(2)}) collective-permute-start(bf16[32,6144]{1,0:T(8,128)(2,1)S(1)} %get-tuple-element.54), channel_id=1, source_target_pairs={{0,12},{1,13},{2,14},{3,15},{4,0},{5,1},{6,2},{7,3},{8,4},{9,5},{1... | collective-permute-start | bytes 1179656 | tf_op jit(solution)/shard_map/ppermute | solution.py:50
  9.4 0.3 collective-permute-start.4
  9.7 13.5 %collective-permute-done.4.refs_3_ = bf16[32,5120]{1,0:T(8,128)(2,1)S(1)} collective-permute-done((bf16[32,5120]{1,0:T(8,128)(2,1)S(1)}, bf16[32,5120]{1,0:T(8,128)(2,1)S(1)}, u32[]{:S(2)}, u32[]{:S(2)}) %collective-permute-start.4) | collective-permute-done | bytes 327712 | tf_op jit(solution)/shard_map/ppermute | solution.py:50
  23.2 3.4 %collective-permute-done.3.refs_1_ = bf16[32,6144]{1,0:T(8,128)(2,1)S(1)} collective-permute-done((bf16[32,6144]{1,0:T(8,128)(2,1)S(1)}, bf16[32,6144]{1,0:T(8,128)(2,1)S(1)}, u32[]{:S(2)}, u32[]{:S(2)}) %collective-permute-start.3) | collective-permute-done | bytes 393248 | tf_op jit(solution)/shard_map/ppermute | solution.py:50
  26.6 0.1 shard_map.49
  26.7 1.6 %collective-permute-start.6 = (bf16[64,5120]{1,0:T(8,128)(2,1)S(1)}, bf16[64,5120]{1,0:T(8,128)(2,1)S(1)}, u32[]{:S(2)}, u32[]{:S(2)}) collective-permute-start(bf16[64,5120]{1,0:T(8,128)(2,1)S(1)} %get-tuple-element.58), channel_id=1, source_target_pairs={{0,2},{1,3},{2,0},{3,1},{4,6},{5,7},{6,4},{7,5},{8,10},{9,11},{10,... | collective-permute-start | bytes 1966088 | tf_op jit(solution)/shard_map/ppermute | solution.py:50
  28.3 0.0 collective-permute-start.7
  28.3 0.6 collective-permute-start.5
  28.9 0.7 collective-permute-start.8
  29.6 17.7 %collective-permute-done.8.refs_6_.refs_4_ = bf16[32,4096]{1,0:T(8,128)(2,1)S(1)} collective-permute-done((bf16[32,4096]{1,0:T(8,128)(2,1)S(1)}, bf16[32,4096]{1,0:T(8,128)(2,1)S(1)}, u32[]{:S(2)}, u32[]{:S(2)}) %collective-permute-start.8) | collective-permute-done | bytes 262176 | tf_op jit(solution)/shard_map/ppermute | solution.py:50
  47.3 0.0 collective-permute-done.5.refs_2_.refs_0_
  47.3 0.0 collective-permute-done.6.refs_3_
  47.3 0.0 collective-permute-done.7.refs_4_.refs_1_
  47.3 0.2 shard_map.50
  47.5 0.1 collective-permute-start.10
  47.5 0.1 collective-permute-start.12
  47.6 0.6 collective-permute-start.11
  48.2 1.5 %collective-permute-start.9 = (bf16[32,4096]{1,0:T(8,128)(2,1)S(1)}, bf16[32,4096]{1,0:T(8,128)(2,1)S(1)}, u32[]{:S(2)}, u32[]{:S(2)}) collective-permute-start(bf16[32,4096]{1,0:T(8,128)(2,1)S(1)} %get-tuple-element.62), channel_id=1, source_target_pairs={{0,2},{1,3},{2,0},{3,1},{4,6},{5,7},{6,4},{7,5},{8,10},{9,11},{10,... | collective-permute-start | bytes 786440 | tf_op jit(solution)/shard_map/ppermute | solution.py:50
  49.7 0.8 collective-permute-done.10.refs_3_.refs_2_
  50.6 4.1 %shard_map.51 = (f32[384,512]{1,0:T(8,128)S(1)}, bf16[512,5120]{1,0:T(8,128)(2,1)S(1)}) custom-call(s32[1]{0:T(128)} %bitcast.place_ref, bf16[64,5120]{1,0:T(8,128)(2,1)S(1)} %get-tuple-element.59.refs_0_, bf16[64,5120]{1,0:T(8,128)(2,1)S(1)} %collective-permute-done.7.refs_4_.refs_1_, bf16[128,5120]{1,0:T(8,128)(2,1)S(1)} %get-tuple-element.63.refs_2_, ...), custom_call_target="tpu_custom_call" | custom-call | flops 2013265920 | bytes 5242880 | tf_op jit(solution)/shard_map/pallas_call | solution.py:73
  54.7 8.6 %collective-permute-done.9.refs_8_.refs_0_ = bf16[32,4096]{1,0:T(8,128)(2,1)S(1)} collective-permute-done((bf16[32,4096]{1,0:T(8,128)(2,1)S(1)}, bf16[32,4096]{1,0:T(8,128)(2,1)S(1)}, u32[]{:S(2)}, u32[]{:S(2)}) %collective-permute-start.9) | collective-permute-done | bytes 262176 | tf_op jit(solution)/shard_map/ppermute | solution.py:50
  63.3 0.4 collective-permute-done.12.refs_7_.refs_2_.refs_4_.refs_5_.refs_0_
  63.7 0.1 shard_map.52
  63.8 0.1 collective-permute-start.13
  63.8 3.2 %collective-permute-start.16 = (bf16[32,8192]{1,0:T(8,128)(2,1)S(1)}, bf16[32,8192]{1,0:T(8,128)(2,1)S(1)}, u32[]{:S(2)}, u32[]{:S(2)}) collective-permute-start(bf16[32,8192]{1,0:T(8,128)(2,1)S(1)} %get-tuple-element.75), channel_id=1, source_target_pairs={{0,12},{1,13},{2,14},{3,15},{4,0},{5,1},{6,2},{7,3},{8,4},{9,5},{1... | collective-permute-start | bytes 1572872 | tf_op jit(solution)/shard_map/ppermute | solution.py:50
  67.0 3.2 %shard_map.53 = (f32[256,512]{1,0:T(8,128)S(1)}, bf16[256,512]{1,0:T(8,128)(2,1)S(1)}, bf16[256,512]{1,0:T(8,128)(2,1)S(1)}) custom-call(s32[1]{0:T(128)} %bitcast.place_ref, bf16[64,5120]{1,0:T(8,128)(2,1)S(1)} %get-tuple-element.59.refs_0_, bf16[64,5120]{1,0:T(8,128)(2,1)S(1)} %collective-permute-done.7.refs_4_.refs_1_, ...), custom_call_target="tpu_custom_call" | custom-call | flops 268435456 | bytes 524288 | tf_op jit(solution)/shard_map/pallas_call | solution.py:73
  70.2 0.2 collective-permute-start.14
  70.4 0.4 collective-permute-start.15
  70.8 1.0 collective-permute-done.14.refs_1_
  71.8 0.4 collective-permute-done.15.refs_2_
  72.2 0.2 shard_map.54
  72.4 0.6 collective-permute-start.18
  73.0 5.9 %collective-permute-done.16.refs_1_.refs_6_ = bf16[32,8192]{1,0:T(8,128)(2,1)S(1)} collective-permute-done((bf16[32,8192]{1,0:T(8,128)(2,1)S(1)}, bf16[32,8192]{1,0:T(8,128)(2,1)S(1)}, u32[]{:S(2)}, u32[]{:S(2)}) %collective-permute-start.16) | collective-permute-done | bytes 524320 | tf_op jit(solution)/shard_map/ppermute | solution.py:50
  78.9 0.1 shard_map.56
  78.9 0.6 collective-permute-start.19
  79.5 1.3 %collective-permute-start.21 = (bf16[32,4096]{1,0:T(8,128)(2,1)S(1)}, bf16[32,4096]{1,0:T(8,128)(2,1)S(1)}, u32[]{:S(2)}, u32[]{:S(2)}) collective-permute-start(bf16[32,4096]{1,0:T(8,128)(2,1)S(1)} %get-tuple-element.80), channel_id=1, source_target_pairs={{0,8},{1,9},{2,10},{3,11},{4,12},{5,13},{6,14},{7,15},{8,0},{9,1},... | collective-permute-start | bytes 786440 | tf_op jit(solution)/shard_map/ppermute | solution.py:50
  80.8 1.5 %collective-permute-start.17 = (bf16[32,6144]{1,0:T(8,128)(2,1)S(1)}, bf16[32,6144]{1,0:T(8,128)(2,1)S(1)}, u32[]{:S(2)}, u32[]{:S(2)}) collective-permute-start(bf16[32,6144]{1,0:T(8,128)(2,1)S(1)} %shard_map.55.refs_3_), channel_id=1, source_target_pairs={{0,2},{1,3},{2,0},{3,1},{4,6},{5,7},{6,4},{7,5},{8,10},{9,11},{10,... | collective-permute-start | bytes 1179656 | tf_op jit(solution)/shard_map/ppermute | solution.py:50
  82.3 3.5 %collective-permute-start.20 = (bf16[128,512]{1,0:T(8,128)(2,1)S(1)}, bf16[128,512]{1,0:T(8,128)(2,1)S(1)}, u32[]{:S(2)}, u32[]{:S(2)}) collective-permute-start(bf16[128,512]{1,0:T(8,128)(2,1)S(1)} %get-tuple-element.79), channel_id=1, source_target_pairs={{0,4},{1,5},{2,6},{3,7},{4,0},{5,1},{6,2},{7,3},{8,12},{9,13},{10,... | collective-permute-start | bytes 393224 | tf_op jit(solution)/shard_map/ppermute | solution.py:50
  85.9 5.8 %copy-done = f32[1024,4096]{1,0:T(8,128)S(1)} copy-done((f32[1024,4096]{1,0:T(8,128)S(1)}, f32[1024,4096]{1,0:T(8,128)}, u32[]{:S(2)}) %copy-start) | copy-done | bytes 16777240
  91.7 1.2 shard_map.57.refs_2_.refs_10_
  92.8 0.8 collective-permute-done.21.refs_4_.refs_0_.refs_2_
  93.7 0.1 collective-permute-start.22
  93.8 4.4 %collective-permute-done.17.refs_2_.refs_1_ = bf16[32,6144]{1,0:T(8,128)(2,1)S(1)} collective-permute-done((bf16[32,6144]{1,0:T(8,128)(2,1)S(1)}, bf16[32,6144]{1,0:T(8,128)(2,1)S(1)}, u32[]{:S(2)}, u32[]{:S(2)}) %collective-permute-start.17) | collective-permute-done | bytes 393248 | tf_op jit(solution)/shard_map/ppermute | solution.py:50
  98.1 3.2 %collective-permute-done.22.refs_1_ = bf16[128,512]{1,0:T(8,128)(2,1)S(1)} collective-permute-done((bf16[128,512]{1,0:T(8,128)(2,1)S(1)}, bf16[128,512]{1,0:T(8,128)(2,1)S(1)}, u32[]{:S(2)}, u32[]{:S(2)}) %collective-permute-start.22) | collective-permute-done | bytes 131104 | tf_op jit(solution)/shard_map/ppermute | solution.py:50
  101.3 1.6 %collective-permute-start.26 = (bf16[128,512]{1,0:T(8,128)(2,1)S(1)}, bf16[128,512]{1,0:T(8,128)(2,1)S(1)}, u32[]{:S(2)}, u32[]{:S(2)}) collective-permute-start(bf16[128,512]{1,0:T(8,128)(2,1)S(1)} %get-tuple-element.88.refs_0_), channel_id=1, source_target_pairs={{0,2},{1,3},{2,0},{3,1},{4,6},{5,7},{6,4},{7,5},{8,10},{9,11},{10,... | collective-permute-start | bytes 393224 | tf_op jit(solution)/shard_map/ppermute | solution.py:50
  102.9 0.6 collective-permute-start.25
  103.5 0.1 shard_map.47
  103.6 0.1 collective-permute-start.1
  103.7 0.2 shard_map.60
  103.9 0.6 collective-permute-start.23
  104.4 0.1 collective-permute-start.24
  104.5 1.9 %collective-permute-done.26.refs_1_ = bf16[128,512]{1,0:T(8,128)(2,1)S(1)} collective-permute-done((bf16[128,512]{1,0:T(8,128)(2,1)S(1)}, bf16[128,512]{1,0:T(8,128)(2,1)S(1)}, u32[]{:S(2)}, u32[]{:S(2)}) %collective-permute-start.26) | collective-permute-done | bytes 131104 | tf_op jit(solution)/shard_map/ppermute | solution.py:50
  106.4 1.6 %collective-permute-done.25.refs_3_ = bf16[32,2048]{1,0:T(8,128)(2,1)S(1)} collective-permute-done((bf16[32,2048]{1,0:T(8,128)(2,1)S(1)}, bf16[32,2048]{1,0:T(8,128)(2,1)S(1)}, u32[]{:S(2)}, u32[]{:S(2)}) %collective-permute-start.25) | collective-permute-done | bytes 131104 | tf_op jit(solution)/shard_map/ppermute | solution.py:50
  108.0 0.1 shard_map.63
  108.1 0.1 collective-permute-start.27
  108.1 0.5 collective-permute-start.28
  108.6 2.0 %collective-permute-done.28.refs_9_ = bf16[256,512]{1,0:T(8,128)(2,1)S(1)} collective-permute-done((bf16[256,512]{1,0:T(8,128)(2,1)S(1)}, bf16[256,512]{1,0:T(8,128)(2,1)S(1)}, u32[]{:S(2)}, u32[]{:S(2)}) %collective-permute-start.28) | collective-permute-done | bytes 262176 | tf_op jit(solution)/shard_map/ppermute | solution.py:50
  110.6 9.2 %shard_map.64 = f32[1024,4096]{1,0:T(8,128)} custom-call(s32[1]{0:T(128)} %bitcast.place_ref, bf16[64,5120]{1,0:T(8,128)(2,1)S(1)} %get-tuple-element.51.refs_0_, bf16[64,5120]{1,0:T(8,128)(2,1)S(1)} %collective-permute-done.1.refs_1_, bf16[64,5120]{1,0:T(8,128)(2,1)S(1)} %get-tuple-element.84.refs_2_, bf16[64,5120]{1,0:T(8,128)(2,1)S(1)} %collective-permute-done.23.refs_3_, ...), custom_call_target="tpu_custom_call" | custom-call | flops 4831838208 | bytes 33554432 | tf_op jit(solution)/shard_map/pallas_call | solution.py:257
  (19 shorter events, 0.2 us)
Async XLA Ops:
  0.0 1.0 copy-start.2
  1.1 25.5 %collective-permute-start.2 = (bf16[32,8192]{1,0:T(8,128)(2,1)S(1)}, bf16[32,8192]{1,0:T(8,128)(2,1)S(1)}, u32[]{:S(2)}, u32[]{:S(2)}) collective-permute-start(bf16[32,8192]{1,0:T(8,128)(2,1)S(1)} %get-tuple-element.53), channel_id=1, source_target_pairs={{0,4},{1,5},{2,6},{3,7},{4,8},{5,9},{6,10},{7,11},{8,12},{9,13},{1... | collective-permute-start | bytes 1572872 | tf_op jit(solution)/shard_map/ppermute | solution.py:50
  4.2 1.2 %copy-start.1 = (bf16[32,16384]{1,0:T(8,128)(2,1)S(1)}, bf16[32,16384]{1,0:T(8,128)(2,1)}, u32[]{:S(2)}) copy-start(bf16[32,16384]{1,0:T(8,128)(2,1)} %refs_0_.3) | copy-start | bytes 3145732
  5.6 17.7 %collective-permute-start = (bf16[32,6144]{1,0:T(8,128)(2,1)S(1)}, bf16[32,6144]{1,0:T(8,128)(2,1)S(1)}, u32[]{:S(2)}, u32[]{:S(2)}) collective-permute-start(bf16[32,6144]{1,0:T(8,128)(2,1)S(1)} %get-tuple-element.50), channel_id=1, source_target_pairs={{0,2},{1,3},{2,0},{3,1},{4,6},{5,7},{6,4},{7,5},{8,10},{9,11},{10,... | collective-permute-start | bytes 1179656 | tf_op jit(solution)/shard_map/ppermute | solution.py:50
  7.1 19.5 %collective-permute-start.3 = (bf16[32,6144]{1,0:T(8,128)(2,1)S(1)}, bf16[32,6144]{1,0:T(8,128)(2,1)S(1)}, u32[]{:S(2)}, u32[]{:S(2)}) collective-permute-start(bf16[32,6144]{1,0:T(8,128)(2,1)S(1)} %get-tuple-element.54), channel_id=1, source_target_pairs={{0,12},{1,13},{2,14},{3,15},{4,0},{5,1},{6,2},{7,3},{8,4},{9,5},{1... | collective-permute-start | bytes 1179656 | tf_op jit(solution)/shard_map/ppermute | solution.py:50
  9.4 13.8 %collective-permute-start.4 = (bf16[32,5120]{1,0:T(8,128)(2,1)S(1)}, bf16[32,5120]{1,0:T(8,128)(2,1)S(1)}, u32[]{:S(2)}, u32[]{:S(2)}) collective-permute-start(bf16[32,5120]{1,0:T(8,128)(2,1)S(1)} %get-tuple-element.56), channel_id=1, source_target_pairs={{0,2},{1,3},{2,0},{3,1},{4,6},{5,7},{6,4},{7,5},{8,10},{9,11},{10,... | collective-permute-start | bytes 983048 | tf_op jit(solution)/shard_map/ppermute | solution.py:50
  26.7 20.5 %collective-permute-start.6 = (bf16[64,5120]{1,0:T(8,128)(2,1)S(1)}, bf16[64,5120]{1,0:T(8,128)(2,1)S(1)}, u32[]{:S(2)}, u32[]{:S(2)}) collective-permute-start(bf16[64,5120]{1,0:T(8,128)(2,1)S(1)} %get-tuple-element.58), channel_id=1, source_target_pairs={{0,2},{1,3},{2,0},{3,1},{4,6},{5,7},{6,4},{7,5},{8,10},{9,11},{10,... | collective-permute-start | bytes 1966088 | tf_op jit(solution)/shard_map/ppermute | solution.py:50
  28.3 19.0 %collective-permute-start.7 = (bf16[64,5120]{1,0:T(8,128)(2,1)S(1)}, bf16[64,5120]{1,0:T(8,128)(2,1)S(1)}, u32[]{:S(2)}, u32[]{:S(2)}) collective-permute-start(bf16[64,5120]{1,0:T(8,128)(2,1)S(1)} %get-tuple-element.59.refs_0_), channel_id=1, source_target_pairs={{0,1},{1,0},{2,3},{3,2},{4,5},{5,4},{6,7},{7,6},{8,9},{9,8},{10,11... | collective-permute-start | bytes 1966088 | tf_op jit(solution)/shard_map/ppermute | solution.py:50
  28.3 18.9 %collective-permute-start.5 = (bf16[32,6144]{1,0:T(8,128)(2,1)S(1)}, bf16[32,6144]{1,0:T(8,128)(2,1)S(1)}, u32[]{:S(2)}, u32[]{:S(2)}) collective-permute-start(bf16[32,6144]{1,0:T(8,128)(2,1)S(1)} %get-tuple-element.57), channel_id=1, source_target_pairs={{0,4},{1,5},{2,6},{3,7},{4,8},{5,9},{6,10},{7,11},{8,12},{9,13},{1... | collective-permute-start | bytes 1179656 | tf_op jit(solution)/shard_map/ppermute | solution.py:50
  28.9 18.4 %collective-permute-start.8 = (bf16[32,4096]{1,0:T(8,128)(2,1)S(1)}, bf16[32,4096]{1,0:T(8,128)(2,1)S(1)}, u32[]{:S(2)}, u32[]{:S(2)}) collective-permute-start(bf16[32,4096]{1,0:T(8,128)(2,1)S(1)} %get-tuple-element.61), channel_id=1, source_target_pairs={{0,4},{1,5},{2,6},{3,7},{4,8},{5,9},{6,10},{7,11},{8,12},{9,13},{1... | collective-permute-start | bytes 786440 | tf_op jit(solution)/shard_map/ppermute | solution.py:50
  47.5 3.1 %collective-permute-start.10 = (bf16[128,5120]{1,0:T(8,128)(2,1)S(1)}, bf16[128,5120]{1,0:T(8,128)(2,1)S(1)}, u32[]{:S(2)}, u32[]{:S(2)}) collective-permute-start(bf16[128,5120]{1,0:T(8,128)(2,1)S(1)} %get-tuple-element.63.refs_2_), channel_id=1, source_target_pairs={{0,1},{1,0},{2,3},{3,2},{4,5},{5,4},{6,7},{7,6},{8,9},{9,8},{10,11... | collective-permute-start | bytes 3932168 | tf_op jit(solution)/shard_map/ppermute | solution.py:50
  47.5 16.1 %collective-permute-start.12 = (bf16[32,8192]{1,0:T(8,128)(2,1)S(1)}, bf16[32,8192]{1,0:T(8,128)(2,1)S(1)}, u32[]{:S(2)}, u32[]{:S(2)}) collective-permute-start(bf16[32,8192]{1,0:T(8,128)(2,1)S(1)} %get-tuple-element.68), channel_id=1, source_target_pairs={{0,4},{1,5},{2,6},{3,7},{4,8},{5,9},{6,10},{7,11},{8,12},{9,13},{1... | collective-permute-start | bytes 1572872 | tf_op jit(solution)/shard_map/ppermute | solution.py:50
  47.6 15.7 %collective-permute-start.11 = (bf16[32,5120]{1,0:T(8,128)(2,1)S(1)}, bf16[32,5120]{1,0:T(8,128)(2,1)S(1)}, u32[]{:S(2)}, u32[]{:S(2)}) collective-permute-start(bf16[32,5120]{1,0:T(8,128)(2,1)S(1)} %get-tuple-element.64), channel_id=1, source_target_pairs={{0,2},{1,3},{2,0},{3,1},{4,6},{5,7},{6,4},{7,5},{8,10},{9,11},{10,... | collective-permute-start | bytes 983048 | tf_op jit(solution)/shard_map/ppermute | solution.py:50
  48.2 15.1 %collective-permute-start.9 = (bf16[32,4096]{1,0:T(8,128)(2,1)S(1)}, bf16[32,4096]{1,0:T(8,128)(2,1)S(1)}, u32[]{:S(2)}, u32[]{:S(2)}) collective-permute-start(bf16[32,4096]{1,0:T(8,128)(2,1)S(1)} %get-tuple-element.62), channel_id=1, source_target_pairs={{0,2},{1,3},{2,0},{3,1},{4,6},{5,7},{6,4},{7,5},{8,10},{9,11},{10,... | collective-permute-start | bytes 786440 | tf_op jit(solution)/shard_map/ppermute | solution.py:50
  63.8 3.3 %collective-permute-start.13 = (bf16[64,5120]{1,0:T(8,128)(2,1)S(1)}, bf16[64,5120]{1,0:T(8,128)(2,1)S(1)}, u32[]{:S(2)}, u32[]{:S(2)}) collective-permute-start(bf16[64,5120]{1,0:T(8,128)(2,1)S(1)} %get-tuple-element.69.refs_4_), channel_id=1, source_target_pairs={{0,1},{1,0},{2,3},{3,2},{4,5},{5,4},{6,7},{7,6},{8,9},{9,8},{10,11... | collective-permute-start | bytes 1966088 | tf_op jit(solution)/shard_map/ppermute | solution.py:50
  63.8 15.0 %collective-permute-start.16 = (bf16[32,8192]{1,0:T(8,128)(2,1)S(1)}, bf16[32,8192]{1,0:T(8,128)(2,1)S(1)}, u32[]{:S(2)}, u32[]{:S(2)}) collective-permute-start(bf16[32,8192]{1,0:T(8,128)(2,1)S(1)} %get-tuple-element.75), channel_id=1, source_target_pairs={{0,12},{1,13},{2,14},{3,15},{4,0},{5,1},{6,2},{7,3},{8,4},{9,5},{1... | collective-permute-start | bytes 1572872 | tf_op jit(solution)/shard_map/ppermute | solution.py:50
  70.2 1.6 %collective-permute-start.14 = (bf16[256,512]{1,0:T(8,128)(2,1)S(1)}, bf16[256,512]{1,0:T(8,128)(2,1)S(1)}, u32[]{:S(2)}, u32[]{:S(2)}) collective-permute-start(bf16[256,512]{1,0:T(8,128)(2,1)S(1)} %get-tuple-element.72), channel_id=1, source_target_pairs={{0,1},{1,0},{2,3},{3,2},{4,5},{5,4},{6,7},{7,6},{8,9},{9,8},{10,11... | collective-permute-start | bytes 786440 | tf_op jit(solution)/shard_map/ppermute | solution.py:50
  70.4 1.8 %collective-permute-start.15 = (bf16[256,512]{1,0:T(8,128)(2,1)S(1)}, bf16[256,512]{1,0:T(8,128)(2,1)S(1)}, u32[]{:S(2)}, u32[]{:S(2)}) collective-permute-start(bf16[256,512]{1,0:T(8,128)(2,1)S(1)} %get-tuple-element.73), channel_id=1, source_target_pairs={{0,1},{1,0},{2,3},{3,2},{4,5},{5,4},{6,7},{7,6},{8,9},{9,8},{10,11... | collective-permute-start | bytes 786440 | tf_op jit(solution)/shard_map/ppermute | solution.py:50
  72.4 6.5 %collective-permute-start.18 = (bf16[128,512]{1,0:T(8,128)(2,1)S(1)}, bf16[128,512]{1,0:T(8,128)(2,1)S(1)}, u32[]{:S(2)}, u32[]{:S(2)}) collective-permute-start(bf16[128,512]{1,0:T(8,128)(2,1)S(1)} %get-tuple-element.74.refs_0_), channel_id=1, source_target_pairs={{0,2},{1,3},{2,0},{3,1},{4,6},{5,7},{6,4},{7,5},{8,10},{9,11},{10,... | collective-permute-start | bytes 393224 | tf_op jit(solution)/shard_map/ppermute | solution.py:50
  78.9 14.7 %collective-permute-start.19 = (bf16[32,6144]{1,0:T(8,128)(2,1)S(1)}, bf16[32,6144]{1,0:T(8,128)(2,1)S(1)}, u32[]{:S(2)}, u32[]{:S(2)}) collective-permute-start(bf16[32,6144]{1,0:T(8,128)(2,1)S(1)} %get-tuple-element.77), channel_id=1, source_target_pairs={{0,2},{1,3},{2,0},{3,1},{4,6},{5,7},{6,4},{7,5},{8,10},{9,11},{10,... | collective-permute-start | bytes 1179656 | tf_op jit(solution)/shard_map/ppermute | solution.py:50
  79.5 14.1 %collective-permute-start.21 = (bf16[32,4096]{1,0:T(8,128)(2,1)S(1)}, bf16[32,4096]{1,0:T(8,128)(2,1)S(1)}, u32[]{:S(2)}, u32[]{:S(2)}) collective-permute-start(bf16[32,4096]{1,0:T(8,128)(2,1)S(1)} %get-tuple-element.80), channel_id=1, source_target_pairs={{0,8},{1,9},{2,10},{3,11},{4,12},{5,13},{6,14},{7,15},{8,0},{9,1},... | collective-permute-start | bytes 786440 | tf_op jit(solution)/shard_map/ppermute | solution.py:50
  80.8 17.3 %collective-permute-start.17 = (bf16[32,6144]{1,0:T(8,128)(2,1)S(1)}, bf16[32,6144]{1,0:T(8,128)(2,1)S(1)}, u32[]{:S(2)}, u32[]{:S(2)}) collective-permute-start(bf16[32,6144]{1,0:T(8,128)(2,1)S(1)} %shard_map.55.refs_3_), channel_id=1, source_target_pairs={{0,2},{1,3},{2,0},{3,1},{4,6},{5,7},{6,4},{7,5},{8,10},{9,11},{10,... | collective-permute-start | bytes 1179656 | tf_op jit(solution)/shard_map/ppermute | solution.py:50
  82.3 11.3 %collective-permute-start.20 = (bf16[128,512]{1,0:T(8,128)(2,1)S(1)}, bf16[128,512]{1,0:T(8,128)(2,1)S(1)}, u32[]{:S(2)}, u32[]{:S(2)}) collective-permute-start(bf16[128,512]{1,0:T(8,128)(2,1)S(1)} %get-tuple-element.79), channel_id=1, source_target_pairs={{0,4},{1,5},{2,6},{3,7},{4,0},{5,1},{6,2},{7,3},{8,12},{9,13},{10,... | collective-permute-start | bytes 393224 | tf_op jit(solution)/shard_map/ppermute | solution.py:50
  85.9 5.8 %copy-start = (f32[1024,4096]{1,0:T(8,128)S(1)}, f32[1024,4096]{1,0:T(8,128)}, u32[]{:S(2)}) copy-start(f32[1024,4096]{1,0:T(8,128)} %refs_0_.5) | copy-start | bytes 50331652
  93.7 7.6 %collective-permute-start.22 = (bf16[128,512]{1,0:T(8,128)(2,1)S(1)}, bf16[128,512]{1,0:T(8,128)(2,1)S(1)}, u32[]{:S(2)}, u32[]{:S(2)}) collective-permute-start(bf16[128,512]{1,0:T(8,128)(2,1)S(1)} %get-tuple-element.82), channel_id=1, source_target_pairs={{0,8},{1,9},{2,10},{3,11},{4,12},{5,13},{6,14},{7,15},{8,0},{9,1},... | collective-permute-start | bytes 393224 | tf_op jit(solution)/shard_map/ppermute | solution.py:50
  101.3 5.0 %collective-permute-start.26 = (bf16[128,512]{1,0:T(8,128)(2,1)S(1)}, bf16[128,512]{1,0:T(8,128)(2,1)S(1)}, u32[]{:S(2)}, u32[]{:S(2)}) collective-permute-start(bf16[128,512]{1,0:T(8,128)(2,1)S(1)} %get-tuple-element.88.refs_0_), channel_id=1, source_target_pairs={{0,2},{1,3},{2,0},{3,1},{4,6},{5,7},{6,4},{7,5},{8,10},{9,11},{10,... | collective-permute-start | bytes 393224 | tf_op jit(solution)/shard_map/ppermute | solution.py:50
  102.9 5.0 %collective-permute-start.25 = (bf16[32,2048]{1,0:T(8,128)(2,1)S(1)}, bf16[32,2048]{1,0:T(8,128)(2,1)S(1)}, u32[]{:S(2)}, u32[]{:S(2)}) collective-permute-start(bf16[32,2048]{1,0:T(8,128)(2,1)S(1)} %shard_map.61), channel_id=1, source_target_pairs={{0,2},{1,3},{2,0},{3,1},{4,6},{5,7},{6,4},{7,5},{8,10},{9,11},{10,... | collective-permute-start | bytes 393224 | tf_op jit(solution)/shard_map/ppermute | solution.py:50
  103.6 5.0 %collective-permute-start.1 = (bf16[64,5120]{1,0:T(8,128)(2,1)S(1)}, bf16[64,5120]{1,0:T(8,128)(2,1)S(1)}, u32[]{:S(2)}, u32[]{:S(2)}) collective-permute-start(bf16[64,5120]{1,0:T(8,128)(2,1)S(1)} %get-tuple-element.52), channel_id=1, source_target_pairs={{0,1},{1,0},{2,3},{3,2},{4,5},{5,4},{6,7},{7,6},{8,9},{9,8},{10,11... | collective-permute-start | bytes 1966088 | tf_op jit(solution)/shard_map/ppermute | solution.py:50
  103.9 6.7 %collective-permute-start.23 = (bf16[64,5120]{1,0:T(8,128)(2,1)S(1)}, bf16[64,5120]{1,0:T(8,128)(2,1)S(1)}, u32[]{:S(2)}, u32[]{:S(2)}) collective-permute-start(bf16[64,5120]{1,0:T(8,128)(2,1)S(1)} %get-tuple-element.85), channel_id=1, source_target_pairs={{0,1},{1,0},{2,3},{3,2},{4,5},{5,4},{6,7},{7,6},{8,9},{9,8},{10,11... | collective-permute-start | bytes 1966088 | tf_op jit(solution)/shard_map/ppermute | solution.py:50
  104.4 6.2 %collective-permute-start.24 = (bf16[64,5120]{1,0:T(8,128)(2,1)S(1)}, bf16[64,5120]{1,0:T(8,128)(2,1)S(1)}, u32[]{:S(2)}, u32[]{:S(2)}) collective-permute-start(bf16[64,5120]{1,0:T(8,128)(2,1)S(1)} %get-tuple-element.87), channel_id=1, source_target_pairs={{0,1},{1,0},{2,3},{3,2},{4,5},{5,4},{6,7},{7,6},{8,9},{9,8},{10,11... | collective-permute-start | bytes 1966088 | tf_op jit(solution)/shard_map/ppermute | solution.py:50
  108.1 2.5 %collective-permute-start.27 = (bf16[64,5120]{1,0:T(8,128)(2,1)S(1)}, bf16[64,5120]{1,0:T(8,128)(2,1)S(1)}, u32[]{:S(2)}, u32[]{:S(2)}) collective-permute-start(bf16[64,5120]{1,0:T(8,128)(2,1)S(1)} %get-tuple-element.90), channel_id=1, source_target_pairs={{0,1},{1,0},{2,3},{3,2},{4,5},{5,4},{6,7},{7,6},{8,9},{9,8},{10,11... | collective-permute-start | bytes 1966088 | tf_op jit(solution)/shard_map/ppermute | solution.py:50
  108.1 2.5 %collective-permute-start.28 = (bf16[256,512]{1,0:T(8,128)(2,1)S(1)}, bf16[256,512]{1,0:T(8,128)(2,1)S(1)}, u32[]{:S(2)}, u32[]{:S(2)}) collective-permute-start(bf16[256,512]{1,0:T(8,128)(2,1)S(1)} %shard_map.62.refs_4_.refs_8_), channel_id=1, source_target_pairs={{0,1},{1,0},{2,3},{3,2},{4,5},{5,4},{6,7},{7,6},{8,9},{9,8},{10,11... | collective-permute-start | bytes 786440 | tf_op jit(solution)/shard_map/ppermute | solution.py:50

commit v5 on v4

--- a/solution.py
+++ b/solution.py
@@ -539,12 +539,13 @@
         if step == 4:
             ins.update({N.factor: factor, N.crossed: far_mixed_crossed, N.grads: far_grads})
             out = call(add, place, ins, shapes, far=(N.factor, N.crossed, N.grads))
+            first_sum = out[N.sum]
         else:
             out = call(add, place, {**ins, N.crossed: mixed_crossed}, shapes, far=(N.crossed,))
         step *= 2
     summed = out[N.sum]
     far_sent = call(
-        far_grads_across, place, {N.grads: far_grads, N.earlier: summed},
+        far_grads_across, place, {N.grads: far_grads, N.earlier: first_sum},
         {N.cross: ((rows, 2 * own_width), BF16)}, far=(N.earlier,),
     )
     far_grads_crossed = across(far_sent[N.cross])
@@ -590,7 +591,7 @@
         last, place,
         {
             N.slab: far_slab, N.slabs: far_mixed_crossed, N.grads: far_grads, N.crossed: far_grads_crossed,
-            N.earlier: out[N.gram],
+            N.earlier: summed,
         },
         pair_shapes(1), far=(N.earlier,),
     )

time: 120 us -> 119 us (level)
  waiting for transfers between devices: 65.5 us -> 64.1 us
    ppermute x29, waiting for transfers between devices: 65.5 us -> 64.1 us  [permute(): return lax.ppermute(value, 'row', perm)]
  transfers between devices with their start and end apart: 29 -> 29, of which waited for: 15 -> 14; matrix products, arithmetic and copies ran while one was open for 0% -> 0% of each run, Pallas kernels for 8% -> 8%
where the time goes in v5:
time: 119 us
  waiting for transfers between devices  64.1 us (54%)
  starting transfers between devices  27.7 us (23%)
  Pallas kernels  19 us (16%)
  local copies, waits for them, and re-layouts  8.03 us (7%)
    ppermute x29, waiting for transfers between devices, permute(): return lax.ppermute(value, 'row', perm)  64.1 us
    ppermute x29, starting transfers between devices, permute(): return lax.ppermute(value, 'row', perm)  27.7 us
    pallas_call x18, Pallas kernels, call(): pl.pallas_call(kernel, in_specs=[pl.BlockSpec(memory_space=pltpu.SMEM)] +...  9.79 us
    pallas_call x1, Pallas kernels, update(): pl.pallas_call(body, grid=(columns // chunk,), in_specs=[pl.BlockSpec(mem...  9.21 us
    unnamed x6, local copies, waits for them, and re-layouts  8.03 us
  transfers between devices with their start and end apart: 29, of which 14 were waited for; matrix products, arithmetic and copies ran while one was open for 0% of the time, Pallas kernels for 8%

profile of v5, /device:TPU:0, one launch (start us, length us, event | category | flops | bytes accessed | tf_op | source)
XLA Modules:
  0.0 119.1 jit_solution(7921182179510016248)
XLA Ops:
  0.0 1.0 copy-done.2
  1.0 0.1 shard_map.48
  1.1 3.1 %collective-permute-start.2 = (bf16[32,8192]{1,0:T(8,128)(2,1)S(1)}, bf16[32,8192]{1,0:T(8,128)(2,1)S(1)}, u32[]{:S(2)}, u32[]{:S(2)}) collective-permute-start(bf16[32,8192]{1,0:T(8,128)(2,1)S(1)} %get-tuple-element.53), channel_id=1, source_target_pairs={{0,4},{1,5},{2,6},{3,7},{4,8},{5,9},{6,10},{7,11},{8,12},{9,13},{1... | collective-permute-start | bytes 1572872 | tf_op jit(solution)/shard_map/ppermute | solution.py:50
  4.2 1.2 %copy-done.1 = bf16[32,16384]{1,0:T(8,128)(2,1)S(1)} copy-done((bf16[32,16384]{1,0:T(8,128)(2,1)S(1)}, bf16[32,16384]{1,0:T(8,128)(2,1)}, u32[]{:S(2)}) %copy-start.1) | copy-done | bytes 1048600
  5.5 0.1 shard_map.46
  5.6 1.6 %collective-permute-start = (bf16[32,6144]{1,0:T(8,128)(2,1)S(1)}, bf16[32,6144]{1,0:T(8,128)(2,1)S(1)}, u32[]{:S(2)}, u32[]{:S(2)}) collective-permute-start(bf16[32,6144]{1,0:T(8,128)(2,1)S(1)} %get-tuple-element.50), channel_id=1, source_target_pairs={{0,2},{1,3},{2,0},{3,1},{4,6},{5,7},{6,4},{7,5},{8,10},{9,11},{10,... | collective-permute-start | bytes 1179656 | tf_op jit(solution)/shard_map/ppermute | solution.py:50
  7.1 2.2 %collective-permute-start.3 = (bf16[32,6144]{1,0:T(8,128)(2,1)S(1)}, bf16[32,6144]{1,0:T(8,128)(2,1)S(1)}, u32[]{:S(2)}, u32[]{:S(2)}) collective-permute-start(bf16[32,6144]{1,0:T(8,128)(2,1)S(1)} %get-tuple-element.54), channel_id=1, source_target_pairs={{0,12},{1,13},{2,14},{3,15},{4,0},{5,1},{6,2},{7,3},{8,4},{9,5},{1... | collective-permute-start | bytes 1179656 | tf_op jit(solution)/shard_map/ppermute | solution.py:50
  9.4 0.3 collective-permute-start.4
  9.7 13.5 %collective-permute-done.4.refs_3_ = bf16[32,5120]{1,0:T(8,128)(2,1)S(1)} collective-permute-done((bf16[32,5120]{1,0:T(8,128)(2,1)S(1)}, bf16[32,5120]{1,0:T(8,128)(2,1)S(1)}, u32[]{:S(2)}, u32[]{:S(2)}) %collective-permute-start.4) | collective-permute-done | bytes 327712 | tf_op jit(solution)/shard_map/ppermute | solution.py:50
  23.2 3.4 %collective-permute-done.3.refs_1_ = bf16[32,6144]{1,0:T(8,128)(2,1)S(1)} collective-permute-done((bf16[32,6144]{1,0:T(8,128)(2,1)S(1)}, bf16[32,6144]{1,0:T(8,128)(2,1)S(1)}, u32[]{:S(2)}, u32[]{:S(2)}) %collective-permute-start.3) | collective-permute-done | bytes 393248 | tf_op jit(solution)/shard_map/ppermute | solution.py:50
  26.6 0.0 collective-permute-done.2.refs_0_
  26.6 0.1 shard_map.49
  26.7 1.6 %collective-permute-start.6 = (bf16[64,5120]{1,0:T(8,128)(2,1)S(1)}, bf16[64,5120]{1,0:T(8,128)(2,1)S(1)}, u32[]{:S(2)}, u32[]{:S(2)}) collective-permute-start(bf16[64,5120]{1,0:T(8,128)(2,1)S(1)} %get-tuple-element.58), channel_id=1, source_target_pairs={{0,2},{1,3},{2,0},{3,1},{4,6},{5,7},{6,4},{7,5},{8,10},{9,11},{10,... | collective-permute-start | bytes 1966088 | tf_op jit(solution)/shard_map/ppermute | solution.py:50
  28.3 0.0 collective-permute-start.7
  28.3 0.6 collective-permute-start.5
  28.9 0.7 collective-permute-start.8
  29.6 17.7 %collective-permute-done.8.refs_6_.refs_4_ = bf16[32,4096]{1,0:T(8,128)(2,1)S(1)} collective-permute-done((bf16[32,4096]{1,0:T(8,128)(2,1)S(1)}, bf16[32,4096]{1,0:T(8,128)(2,1)S(1)}, u32[]{:S(2)}, u32[]{:S(2)}) %collective-permute-start.8) | collective-permute-done | bytes 262176 | tf_op jit(solution)/shard_map/ppermute | solution.py:50
  47.3 0.0 collective-permute-done.6.refs_3_
  47.3 0.0 collective-permute-done.7.refs_4_.refs_1_
  47.3 0.2 shard_map.50
  47.5 0.1 collective-permute-start.10
  47.5 0.1 collective-permute-start.12
  47.6 0.6 collective-permute-start.11
  48.2 1.5 %collective-permute-start.9 = (bf16[32,4096]{1,0:T(8,128)(2,1)S(1)}, bf16[32,4096]{1,0:T(8,128)(2,1)S(1)}, u32[]{:S(2)}, u32[]{:S(2)}) collective-permute-start(bf16[32,4096]{1,0:T(8,128)(2,1)S(1)} %get-tuple-element.62), channel_id=1, source_target_pairs={{0,2},{1,3},{2,0},{3,1},{4,6},{5,7},{6,4},{7,5},{8,10},{9,11},{10,... | collective-permute-start | bytes 786440 | tf_op jit(solution)/shard_map/ppermute | solution.py:50
  49.7 0.8 collective-permute-done.10.refs_3_.refs_2_
  50.6 4.1 %shard_map.51 = (f32[384,512]{1,0:T(8,128)S(1)}, bf16[512,5120]{1,0:T(8,128)(2,1)S(1)}) custom-call(s32[1]{0:T(128)} %bitcast.place_ref, bf16[64,5120]{1,0:T(8,128)(2,1)S(1)} %get-tuple-element.59.refs_0_, bf16[64,5120]{1,0:T(8,128)(2,1)S(1)} %collective-permute-done.7.refs_4_.refs_1_, bf16[128,5120]{1,0:T(8,128)(2,1)S(1)} %get-tuple-element.63.refs_2_, ...), custom_call_target="tpu_custom_call" | custom-call | flops 2013265920 | bytes 5242880 | tf_op jit(solution)/shard_map/pallas_call | solution.py:73
  54.7 8.6 %collective-permute-done.9.refs_8_.refs_0_ = bf16[32,4096]{1,0:T(8,128)(2,1)S(1)} collective-permute-done((bf16[32,4096]{1,0:T(8,128)(2,1)S(1)}, bf16[32,4096]{1,0:T(8,128)(2,1)S(1)}, u32[]{:S(2)}, u32[]{:S(2)}) %collective-permute-start.9) | collective-permute-done | bytes 262176 | tf_op jit(solution)/shard_map/ppermute | solution.py:50
  63.3 0.0 collective-permute-done.11.refs_1_
  63.3 0.4 collective-permute-done.12.refs_7_.refs_2_.refs_4_.refs_5_.refs_0_
  63.7 0.1 shard_map.52
  63.8 0.1 collective-permute-start.13
  63.8 3.2 %collective-permute-start.16 = (bf16[32,8192]{1,0:T(8,128)(2,1)S(1)}, bf16[32,8192]{1,0:T(8,128)(2,1)S(1)}, u32[]{:S(2)}, u32[]{:S(2)}) collective-permute-start(bf16[32,8192]{1,0:T(8,128)(2,1)S(1)} %get-tuple-element.75), channel_id=1, source_target_pairs={{0,12},{1,13},{2,14},{3,15},{4,0},{5,1},{6,2},{7,3},{8,4},{9,5},{1... | collective-permute-start | bytes 1572872 | tf_op jit(solution)/shard_map/ppermute | solution.py:50
  67.0 3.2 %shard_map.53 = (f32[256,512]{1,0:T(8,128)S(1)}, bf16[256,512]{1,0:T(8,128)(2,1)S(1)}, bf16[256,512]{1,0:T(8,128)(2,1)S(1)}) custom-call(s32[1]{0:T(128)} %bitcast.place_ref, bf16[64,5120]{1,0:T(8,128)(2,1)S(1)} %get-tuple-element.59.refs_0_, bf16[64,5120]{1,0:T(8,128)(2,1)S(1)} %collective-permute-done.7.refs_4_.refs_1_, ...), custom_call_target="tpu_custom_call" | custom-call | flops 268435456 | bytes 524288 | tf_op jit(solution)/shard_map/pallas_call | solution.py:73
  70.2 0.2 collective-permute-start.14
  70.4 0.4 collective-permute-start.15
  70.8 1.0 collective-permute-done.14.refs_1_
  71.8 0.4 collective-permute-done.15.refs_2_
  72.2 0.2 shard_map.54
  72.4 0.6 collective-permute-start.18
  73.0 5.9 %collective-permute-done.16.refs_1_.refs_6_ = bf16[32,8192]{1,0:T(8,128)(2,1)S(1)} collective-permute-done((bf16[32,8192]{1,0:T(8,128)(2,1)S(1)}, bf16[32,8192]{1,0:T(8,128)(2,1)S(1)}, u32[]{:S(2)}, u32[]{:S(2)}) %collective-permute-start.16) | collective-permute-done | bytes 524320 | tf_op jit(solution)/shard_map/ppermute | solution.py:50
  78.9 0.1 shard_map.56
  78.9 0.6 collective-permute-start.19
  79.5 1.3 %collective-permute-start.21 = (bf16[32,4096]{1,0:T(8,128)(2,1)S(1)}, bf16[32,4096]{1,0:T(8,128)(2,1)S(1)}, u32[]{:S(2)}, u32[]{:S(2)}) collective-permute-start(bf16[32,4096]{1,0:T(8,128)(2,1)S(1)} %get-tuple-element.80), channel_id=1, source_target_pairs={{0,8},{1,9},{2,10},{3,11},{4,12},{5,13},{6,14},{7,15},{8,0},{9,1},... | collective-permute-start | bytes 786440 | tf_op jit(solution)/shard_map/ppermute | solution.py:50
  80.8 1.5 %collective-permute-start.17 = (bf16[32,6144]{1,0:T(8,128)(2,1)S(1)}, bf16[32,6144]{1,0:T(8,128)(2,1)S(1)}, u32[]{:S(2)}, u32[]{:S(2)}) collective-permute-start(bf16[32,6144]{1,0:T(8,128)(2,1)S(1)} %shard_map.55.refs_3_), channel_id=1, source_target_pairs={{0,2},{1,3},{2,0},{3,1},{4,6},{5,7},{6,4},{7,5},{8,10},{9,11},{10,... | collective-permute-start | bytes 1179656 | tf_op jit(solution)/shard_map/ppermute | solution.py:50
  82.3 3.5 %collective-permute-start.20 = (bf16[128,512]{1,0:T(8,128)(2,1)S(1)}, bf16[128,512]{1,0:T(8,128)(2,1)S(1)}, u32[]{:S(2)}, u32[]{:S(2)}) collective-permute-start(bf16[128,512]{1,0:T(8,128)(2,1)S(1)} %get-tuple-element.79), channel_id=1, source_target_pairs={{0,4},{1,5},{2,6},{3,7},{4,0},{5,1},{6,2},{7,3},{8,12},{9,13},{10,... | collective-permute-start | bytes 393224 | tf_op jit(solution)/shard_map/ppermute | solution.py:50
  85.9 5.8 %copy-done = f32[1024,4096]{1,0:T(8,128)S(1)} copy-done((f32[1024,4096]{1,0:T(8,128)S(1)}, f32[1024,4096]{1,0:T(8,128)}, u32[]{:S(2)}) %copy-start) | copy-done | bytes 16777240
  91.7 1.2 shard_map.57.refs_2_.refs_10_
  92.8 0.8 collective-permute-done.21.refs_4_.refs_0_.refs_2_
  93.7 0.1 collective-permute-start.22
  93.8 1.6 %collective-permute-start.25 = (bf16[32,2048]{1,0:T(8,128)(2,1)S(1)}, bf16[32,2048]{1,0:T(8,128)(2,1)S(1)}, u32[]{:S(2)}, u32[]{:S(2)}) collective-permute-start(bf16[32,2048]{1,0:T(8,128)(2,1)S(1)} %shard_map.61), channel_id=1, source_target_pairs={{0,2},{1,3},{2,0},{3,1},{4,6},{5,7},{6,4},{7,5},{8,10},{9,11},{10,... | collective-permute-start | bytes 393224 | tf_op jit(solution)/shard_map/ppermute | solution.py:50
  95.4 0.1 shard_map.47
  95.5 0.1 collective-permute-start.1
  95.5 3.9 %collective-permute-done.17.refs_2_.refs_1_ = bf16[32,6144]{1,0:T(8,128)(2,1)S(1)} collective-permute-done((bf16[32,6144]{1,0:T(8,128)(2,1)S(1)}, bf16[32,6144]{1,0:T(8,128)(2,1)S(1)}, u32[]{:S(2)}, u32[]{:S(2)}) %collective-permute-start.17) | collective-permute-done | bytes 393248 | tf_op jit(solution)/shard_map/ppermute | solution.py:50
  99.5 1.8 %collective-permute-done.22.refs_1_ = bf16[128,512]{1,0:T(8,128)(2,1)S(1)} collective-permute-done((bf16[128,512]{1,0:T(8,128)(2,1)S(1)}, bf16[128,512]{1,0:T(8,128)(2,1)S(1)}, u32[]{:S(2)}, u32[]{:S(2)}) %collective-permute-start.22) | collective-permute-done | bytes 131104 | tf_op jit(solution)/shard_map/ppermute | solution.py:50
  101.3 0.2 shard_map.60
  101.5 0.1 collective-permute-start.23
  101.6 0.5 collective-permute-start.24
  102.1 0.1 shard_map.62
  102.2 0.1 collective-permute-start.26
  102.3 1.5 %collective-permute-start.27 = (bf16[128,512]{1,0:T(8,128)(2,1)S(1)}, bf16[128,512]{1,0:T(8,128)(2,1)S(1)}, u32[]{:S(2)}, u32[]{:S(2)}) collective-permute-start(bf16[128,512]{1,0:T(8,128)(2,1)S(1)} %get-tuple-element.90.refs_0_), channel_id=1, source_target_pairs={{0,2},{1,3},{2,0},{3,1},{4,6},{5,7},{6,4},{7,5},{8,10},{9,11},{10,... | collective-permute-start | bytes 393224 | tf_op jit(solution)/shard_map/ppermute | solution.py:50
  103.9 4.3 %collective-permute-done.27.refs_1_ = bf16[128,512]{1,0:T(8,128)(2,1)S(1)} collective-permute-done((bf16[128,512]{1,0:T(8,128)(2,1)S(1)}, bf16[128,512]{1,0:T(8,128)(2,1)S(1)}, u32[]{:S(2)}, u32[]{:S(2)}) %collective-permute-start.27) | collective-permute-done | bytes 131104 | tf_op jit(solution)/shard_map/ppermute | solution.py:50
  108.2 0.1 collective-permute-start.28
  108.3 1.5 %collective-permute-done.28.refs_9_ = bf16[256,512]{1,0:T(8,128)(2,1)S(1)} collective-permute-done((bf16[256,512]{1,0:T(8,128)(2,1)S(1)}, bf16[256,512]{1,0:T(8,128)(2,1)S(1)}, u32[]{:S(2)}, u32[]{:S(2)}) %collective-permute-start.28) | collective-permute-done | bytes 262176 | tf_op jit(solution)/shard_map/ppermute | solution.py:50
  109.8 9.2 %shard_map.64 = f32[1024,4096]{1,0:T(8,128)} custom-call(s32[1]{0:T(128)} %bitcast.place_ref, bf16[64,5120]{1,0:T(8,128)(2,1)S(1)} %get-tuple-element.51.refs_0_, bf16[64,5120]{1,0:T(8,128)(2,1)S(1)} %collective-permute-done.1.refs_1_, bf16[64,5120]{1,0:T(8,128)(2,1)S(1)} %get-tuple-element.84.refs_2_, bf16[64,5120]{1,0:T(8,128)(2,1)S(1)} %collective-permute-done.23.refs_3_, ...), custom_call_target="tpu_custom_call" | custom-call | flops 4831838208 | bytes 33554432 | tf_op jit(solution)/shard_map/pallas_call | solution.py:257
  (19 shorter events, 0.2 us)
Async XLA Ops:
  0.0 1.0 copy-start.2
  1.1 25.5 %collective-permute-start.2 = (bf16[32,8192]{1,0:T(8,128)(2,1)S(1)}, bf16[32,8192]{1,0:T(8,128)(2,1)S(1)}, u32[]{:S(2)}, u32[]{:S(2)}) collective-permute-start(bf16[32,8192]{1,0:T(8,128)(2,1)S(1)} %get-tuple-element.53), channel_id=1, source_target_pairs={{0,4},{1,5},{2,6},{3,7},{4,8},{5,9},{6,10},{7,11},{8,12},{9,13},{1... | collective-permute-start | bytes 1572872 | tf_op jit(solution)/shard_map/ppermute | solution.py:50
  4.2 1.2 %copy-start.1 = (bf16[32,16384]{1,0:T(8,128)(2,1)S(1)}, bf16[32,16384]{1,0:T(8,128)(2,1)}, u32[]{:S(2)}) copy-start(bf16[32,16384]{1,0:T(8,128)(2,1)} %refs_0_.3) | copy-start | bytes 3145732
  5.6 17.7 %collective-permute-start = (bf16[32,6144]{1,0:T(8,128)(2,1)S(1)}, bf16[32,6144]{1,0:T(8,128)(2,1)S(1)}, u32[]{:S(2)}, u32[]{:S(2)}) collective-permute-start(bf16[32,6144]{1,0:T(8,128)(2,1)S(1)} %get-tuple-element.50), channel_id=1, source_target_pairs={{0,2},{1,3},{2,0},{3,1},{4,6},{5,7},{6,4},{7,5},{8,10},{9,11},{10,... | collective-permute-start | bytes 1179656 | tf_op jit(solution)/shard_map/ppermute | solution.py:50
  7.1 19.5 %collective-permute-start.3 = (bf16[32,6144]{1,0:T(8,128)(2,1)S(1)}, bf16[32,6144]{1,0:T(8,128)(2,1)S(1)}, u32[]{:S(2)}, u32[]{:S(2)}) collective-permute-start(bf16[32,6144]{1,0:T(8,128)(2,1)S(1)} %get-tuple-element.54), channel_id=1, source_target_pairs={{0,12},{1,13},{2,14},{3,15},{4,0},{5,1},{6,2},{7,3},{8,4},{9,5},{1... | collective-permute-start | bytes 1179656 | tf_op jit(solution)/shard_map/ppermute | solution.py:50
  9.4 13.8 %collective-permute-start.4 = (bf16[32,5120]{1,0:T(8,128)(2,1)S(1)}, bf16[32,5120]{1,0:T(8,128)(2,1)S(1)}, u32[]{:S(2)}, u32[]{:S(2)}) collective-permute-start(bf16[32,5120]{1,0:T(8,128)(2,1)S(1)} %get-tuple-element.56), channel_id=1, source_target_pairs={{0,2},{1,3},{2,0},{3,1},{4,6},{5,7},{6,4},{7,5},{8,10},{9,11},{10,... | collective-permute-start | bytes 983048 | tf_op jit(solution)/shard_map/ppermute | solution.py:50
  26.7 20.5 %collective-permute-start.6 = (bf16[64,5120]{1,0:T(8,128)(2,1)S(1)}, bf16[64,5120]{1,0:T(8,128)(2,1)S(1)}, u32[]{:S(2)}, u32[]{:S(2)}) collective-permute-start(bf16[64,5120]{1,0:T(8,128)(2,1)S(1)} %get-tuple-element.58), channel_id=1, source_target_pairs={{0,2},{1,3},{2,0},{3,1},{4,6},{5,7},{6,4},{7,5},{8,10},{9,11},{10,... | collective-permute-start | bytes 1966088 | tf_op jit(solution)/shard_map/ppermute | solution.py:50
  28.3 19.0 %collective-permute-start.7 = (bf16[64,5120]{1,0:T(8,128)(2,1)S(1)}, bf16[64,5120]{1,0:T(8,128)(2,1)S(1)}, u32[]{:S(2)}, u32[]{:S(2)}) collective-permute-start(bf16[64,5120]{1,0:T(8,128)(2,1)S(1)} %get-tuple-element.59.refs_0_), channel_id=1, source_target_pairs={{0,1},{1,0},{2,3},{3,2},{4,5},{5,4},{6,7},{7,6},{8,9},{9,8},{10,11... | collective-permute-start | bytes 1966088 | tf_op jit(solution)/shard_map/ppermute | solution.py:50
  28.3 18.9 %collective-permute-start.5 = (bf16[32,6144]{1,0:T(8,128)(2,1)S(1)}, bf16[32,6144]{1,0:T(8,128)(2,1)S(1)}, u32[]{:S(2)}, u32[]{:S(2)}) collective-permute-start(bf16[32,6144]{1,0:T(8,128)(2,1)S(1)} %get-tuple-element.57), channel_id=1, source_target_pairs={{0,4},{1,5},{2,6},{3,7},{4,8},{5,9},{6,10},{7,11},{8,12},{9,13},{1... | collective-permute-start | bytes 1179656 | tf_op jit(solution)/shard_map/ppermute | solution.py:50
  28.9 18.4 %collective-permute-start.8 = (bf16[32,4096]{1,0:T(8,128)(2,1)S(1)}, bf16[32,4096]{1,0:T(8,128)(2,1)S(1)}, u32[]{:S(2)}, u32[]{:S(2)}) collective-permute-start(bf16[32,4096]{1,0:T(8,128)(2,1)S(1)} %get-tuple-element.61), channel_id=1, source_target_pairs={{0,4},{1,5},{2,6},{3,7},{4,8},{5,9},{6,10},{7,11},{8,12},{9,13},{1... | collective-permute-start | bytes 786440 | tf_op jit(solution)/shard_map/ppermute | solution.py:50
  47.5 3.1 %collective-permute-start.10 = (bf16[128,5120]{1,0:T(8,128)(2,1)S(1)}, bf16[128,5120]{1,0:T(8,128)(2,1)S(1)}, u32[]{:S(2)}, u32[]{:S(2)}) collective-permute-start(bf16[128,5120]{1,0:T(8,128)(2,1)S(1)} %get-tuple-element.63.refs_2_), channel_id=1, source_target_pairs={{0,1},{1,0},{2,3},{3,2},{4,5},{5,4},{6,7},{7,6},{8,9},{9,8},{10,11... | collective-permute-start | bytes 3932168 | tf_op jit(solution)/shard_map/ppermute | solution.py:50
  47.5 16.1 %collective-permute-start.12 = (bf16[32,8192]{1,0:T(8,128)(2,1)S(1)}, bf16[32,8192]{1,0:T(8,128)(2,1)S(1)}, u32[]{:S(2)}, u32[]{:S(2)}) collective-permute-start(bf16[32,8192]{1,0:T(8,128)(2,1)S(1)} %get-tuple-element.68), channel_id=1, source_target_pairs={{0,4},{1,5},{2,6},{3,7},{4,8},{5,9},{6,10},{7,11},{8,12},{9,13},{1... | collective-permute-start | bytes 1572872 | tf_op jit(solution)/shard_map/ppermute | solution.py:50
  47.6 15.7 %collective-permute-start.11 = (bf16[32,5120]{1,0:T(8,128)(2,1)S(1)}, bf16[32,5120]{1,0:T(8,128)(2,1)S(1)}, u32[]{:S(2)}, u32[]{:S(2)}) collective-permute-start(bf16[32,5120]{1,0:T(8,128)(2,1)S(1)} %get-tuple-element.64), channel_id=1, source_target_pairs={{0,2},{1,3},{2,0},{3,1},{4,6},{5,7},{6,4},{7,5},{8,10},{9,11},{10,... | collective-permute-start | bytes 983048 | tf_op jit(solution)/shard_map/ppermute | solution.py:50
  48.2 15.1 %collective-permute-start.9 = (bf16[32,4096]{1,0:T(8,128)(2,1)S(1)}, bf16[32,4096]{1,0:T(8,128)(2,1)S(1)}, u32[]{:S(2)}, u32[]{:S(2)}) collective-permute-start(bf16[32,4096]{1,0:T(8,128)(2,1)S(1)} %get-tuple-element.62), channel_id=1, source_target_pairs={{0,2},{1,3},{2,0},{3,1},{4,6},{5,7},{6,4},{7,5},{8,10},{9,11},{10,... | collective-permute-start | bytes 786440 | tf_op jit(solution)/shard_map/ppermute | solution.py:50
  63.8 3.3 %collective-permute-start.13 = (bf16[64,5120]{1,0:T(8,128)(2,1)S(1)}, bf16[64,5120]{1,0:T(8,128)(2,1)S(1)}, u32[]{:S(2)}, u32[]{:S(2)}) collective-permute-start(bf16[64,5120]{1,0:T(8,128)(2,1)S(1)} %get-tuple-element.69.refs_4_), channel_id=1, source_target_pairs={{0,1},{1,0},{2,3},{3,2},{4,5},{5,4},{6,7},{7,6},{8,9},{9,8},{10,11... | collective-permute-start | bytes 1966088 | tf_op jit(solution)/shard_map/ppermute | solution.py:50
  63.8 15.0 %collective-permute-start.16 = (bf16[32,8192]{1,0:T(8,128)(2,1)S(1)}, bf16[32,8192]{1,0:T(8,128)(2,1)S(1)}, u32[]{:S(2)}, u32[]{:S(2)}) collective-permute-start(bf16[32,8192]{1,0:T(8,128)(2,1)S(1)} %get-tuple-element.75), channel_id=1, source_target_pairs={{0,12},{1,13},{2,14},{3,15},{4,0},{5,1},{6,2},{7,3},{8,4},{9,5},{1... | collective-permute-start | bytes 1572872 | tf_op jit(solution)/shard_map/ppermute | solution.py:50
  70.2 1.6 %collective-permute-start.14 = (bf16[256,512]{1,0:T(8,128)(2,1)S(1)}, bf16[256,512]{1,0:T(8,128)(2,1)S(1)}, u32[]{:S(2)}, u32[]{:S(2)}) collective-permute-start(bf16[256,512]{1,0:T(8,128)(2,1)S(1)} %get-tuple-element.72), channel_id=1, source_target_pairs={{0,1},{1,0},{2,3},{3,2},{4,5},{5,4},{6,7},{7,6},{8,9},{9,8},{10,11... | collective-permute-start | bytes 786440 | tf_op jit(solution)/shard_map/ppermute | solution.py:50
  70.4 1.8 %collective-permute-start.15 = (bf16[256,512]{1,0:T(8,128)(2,1)S(1)}, bf16[256,512]{1,0:T(8,128)(2,1)S(1)}, u32[]{:S(2)}, u32[]{:S(2)}) collective-permute-start(bf16[256,512]{1,0:T(8,128)(2,1)S(1)} %get-tuple-element.73), channel_id=1, source_target_pairs={{0,1},{1,0},{2,3},{3,2},{4,5},{5,4},{6,7},{7,6},{8,9},{9,8},{10,11... | collective-permute-start | bytes 786440 | tf_op jit(solution)/shard_map/ppermute | solution.py:50
  72.4 6.5 %collective-permute-start.18 = (bf16[128,512]{1,0:T(8,128)(2,1)S(1)}, bf16[128,512]{1,0:T(8,128)(2,1)S(1)}, u32[]{:S(2)}, u32[]{:S(2)}) collective-permute-start(bf16[128,512]{1,0:T(8,128)(2,1)S(1)} %get-tuple-element.74.refs_0_), channel_id=1, source_target_pairs={{0,2},{1,3},{2,0},{3,1},{4,6},{5,7},{6,4},{7,5},{8,10},{9,11},{10,... | collective-permute-start | bytes 393224 | tf_op jit(solution)/shard_map/ppermute | solution.py:50
  78.9 14.7 %collective-permute-start.19 = (bf16[32,6144]{1,0:T(8,128)(2,1)S(1)}, bf16[32,6144]{1,0:T(8,128)(2,1)S(1)}, u32[]{:S(2)}, u32[]{:S(2)}) collective-permute-start(bf16[32,6144]{1,0:T(8,128)(2,1)S(1)} %get-tuple-element.77), channel_id=1, source_target_pairs={{0,2},{1,3},{2,0},{3,1},{4,6},{5,7},{6,4},{7,5},{8,10},{9,11},{10,... | collective-permute-start | bytes 1179656 | tf_op jit(solution)/shard_map/ppermute | solution.py:50
  79.5 14.1 %collective-permute-start.21 = (bf16[32,4096]{1,0:T(8,128)(2,1)S(1)}, bf16[32,4096]{1,0:T(8,128)(2,1)S(1)}, u32[]{:S(2)}, u32[]{:S(2)}) collective-permute-start(bf16[32,4096]{1,0:T(8,128)(2,1)S(1)} %get-tuple-element.80), channel_id=1, source_target_pairs={{0,8},{1,9},{2,10},{3,11},{4,12},{5,13},{6,14},{7,15},{8,0},{9,1},... | collective-permute-start | bytes 786440 | tf_op jit(solution)/shard_map/ppermute | solution.py:50
  80.8 18.6 %collective-permute-start.17 = (bf16[32,6144]{1,0:T(8,128)(2,1)S(1)}, bf16[32,6144]{1,0:T(8,128)(2,1)S(1)}, u32[]{:S(2)}, u32[]{:S(2)}) collective-permute-start(bf16[32,6144]{1,0:T(8,128)(2,1)S(1)} %shard_map.55.refs_3_), channel_id=1, source_target_pairs={{0,2},{1,3},{2,0},{3,1},{4,6},{5,7},{6,4},{7,5},{8,10},{9,11},{10,... | collective-permute-start | bytes 1179656 | tf_op jit(solution)/shard_map/ppermute | solution.py:50
  82.3 11.3 %collective-permute-start.20 = (bf16[128,512]{1,0:T(8,128)(2,1)S(1)}, bf16[128,512]{1,0:T(8,128)(2,1)S(1)}, u32[]{:S(2)}, u32[]{:S(2)}) collective-permute-start(bf16[128,512]{1,0:T(8,128)(2,1)S(1)} %get-tuple-element.79), channel_id=1, source_target_pairs={{0,4},{1,5},{2,6},{3,7},{4,0},{5,1},{6,2},{7,3},{8,12},{9,13},{10,... | collective-permute-start | bytes 393224 | tf_op jit(solution)/shard_map/ppermute | solution.py:50
  85.9 5.8 %copy-start = (f32[1024,4096]{1,0:T(8,128)S(1)}, f32[1024,4096]{1,0:T(8,128)}, u32[]{:S(2)}) copy-start(f32[1024,4096]{1,0:T(8,128)} %refs_0_.5) | copy-start | bytes 50331652
  93.7 7.6 %collective-permute-start.22 = (bf16[128,512]{1,0:T(8,128)(2,1)S(1)}, bf16[128,512]{1,0:T(8,128)(2,1)S(1)}, u32[]{:S(2)}, u32[]{:S(2)}) collective-permute-start(bf16[128,512]{1,0:T(8,128)(2,1)S(1)} %get-tuple-element.82), channel_id=1, source_target_pairs={{0,8},{1,9},{2,10},{3,11},{4,12},{5,13},{6,14},{7,15},{8,0},{9,1},... | collective-permute-start | bytes 393224 | tf_op jit(solution)/shard_map/ppermute | solution.py:50
  93.8 8.3 %collective-permute-start.25 = (bf16[32,2048]{1,0:T(8,128)(2,1)S(1)}, bf16[32,2048]{1,0:T(8,128)(2,1)S(1)}, u32[]{:S(2)}, u32[]{:S(2)}) collective-permute-start(bf16[32,2048]{1,0:T(8,128)(2,1)S(1)} %shard_map.61), channel_id=1, source_target_pairs={{0,2},{1,3},{2,0},{3,1},{4,6},{5,7},{6,4},{7,5},{8,10},{9,11},{10,... | collective-permute-start | bytes 393224 | tf_op jit(solution)/shard_map/ppermute | solution.py:50
  95.5 12.8 %collective-permute-start.1 = (bf16[64,5120]{1,0:T(8,128)(2,1)S(1)}, bf16[64,5120]{1,0:T(8,128)(2,1)S(1)}, u32[]{:S(2)}, u32[]{:S(2)}) collective-permute-start(bf16[64,5120]{1,0:T(8,128)(2,1)S(1)} %get-tuple-element.52), channel_id=1, source_target_pairs={{0,1},{1,0},{2,3},{3,2},{4,5},{5,4},{6,7},{7,6},{8,9},{9,8},{10,11... | collective-permute-start | bytes 1966088 | tf_op jit(solution)/shard_map/ppermute | solution.py:50
  101.5 8.3 %collective-permute-start.23 = (bf16[64,5120]{1,0:T(8,128)(2,1)S(1)}, bf16[64,5120]{1,0:T(8,128)(2,1)S(1)}, u32[]{:S(2)}, u32[]{:S(2)}) collective-permute-start(bf16[64,5120]{1,0:T(8,128)(2,1)S(1)} %get-tuple-element.85), channel_id=1, source_target_pairs={{0,1},{1,0},{2,3},{3,2},{4,5},{5,4},{6,7},{7,6},{8,9},{9,8},{10,11... | collective-permute-start | bytes 1966088 | tf_op jit(solution)/shard_map/ppermute | solution.py:50
  101.6 8.2 %collective-permute-start.24 = (bf16[64,5120]{1,0:T(8,128)(2,1)S(1)}, bf16[64,5120]{1,0:T(8,128)(2,1)S(1)}, u32[]{:S(2)}, u32[]{:S(2)}) collective-permute-start(bf16[64,5120]{1,0:T(8,128)(2,1)S(1)} %get-tuple-element.87), channel_id=1, source_target_pairs={{0,1},{1,0},{2,3},{3,2},{4,5},{5,4},{6,7},{7,6},{8,9},{9,8},{10,11... | collective-permute-start | bytes 1966088 | tf_op jit(solution)/shard_map/ppermute | solution.py:50
  102.2 7.6 %collective-permute-start.26 = (bf16[64,5120]{1,0:T(8,128)(2,1)S(1)}, bf16[64,5120]{1,0:T(8,128)(2,1)S(1)}, u32[]{:S(2)}, u32[]{:S(2)}) collective-permute-start(bf16[64,5120]{1,0:T(8,128)(2,1)S(1)} %get-tuple-element.89), channel_id=1, source_target_pairs={{0,1},{1,0},{2,3},{3,2},{4,5},{5,4},{6,7},{7,6},{8,9},{9,8},{10,11... | collective-permute-start | bytes 1966088 | tf_op jit(solution)/shard_map/ppermute | solution.py:50
  102.3 5.8 %collective-permute-start.27 = (bf16[128,512]{1,0:T(8,128)(2,1)S(1)}, bf16[128,512]{1,0:T(8,128)(2,1)S(1)}, u32[]{:S(2)}, u32[]{:S(2)}) collective-permute-start(bf16[128,512]{1,0:T(8,128)(2,1)S(1)} %get-tuple-element.90.refs_0_), channel_id=1, source_target_pairs={{0,2},{1,3},{2,0},{3,1},{4,6},{5,7},{6,4},{7,5},{8,10},{9,11},{10,... | collective-permute-start | bytes 393224 | tf_op jit(solution)/shard_map/ppermute | solution.py:50
  108.2 1.6 %collective-permute-start.28 = (bf16[256,512]{1,0:T(8,128)(2,1)S(1)}, bf16[256,512]{1,0:T(8,128)(2,1)S(1)}, u32[]{:S(2)}, u32[]{:S(2)}) collective-permute-start(bf16[256,512]{1,0:T(8,128)(2,1)S(1)} %shard_map.63.refs_8_), channel_id=1, source_target_pairs={{0,1},{1,0},{2,3},{3,2},{4,5},{5,4},{6,7},{7,6},{8,9},{9,8},{10,11... | collective-permute-start | bytes 786440 | tf_op jit(solution)/shard_map/ppermute | solution.py:50
